TPU v7x, 32 devices: a whole 2x2x4 slice. The times are simulated.
32 devices in a mesh: seq: 4 (over x, core), tp: 8 (over z, y).
Axes of the slice: x: 2, y: 2, z: 4, core: 2. Of those that a mesh axis runs over, the one named last changes fastest.
Arguments:
- tokens: bfloat16 [1024, 4096], P('seq', 'tp'), may hold values from -12 to 12
- norm_gain: float32 [2, 4096], replicated, may hold values from 0.5 to 1.5
- w_in: bfloat16 [2, 4096, 2, 8192], P(None, None, None, 'tp'), may hold values from -0.09375 to 0.09375
- w_low: bfloat16 [2, 4096, 288], P(None, 'tp'), may hold values from -0.09375 to 0.09375
- w_dt: bfloat16 [2, 256, 8192], P(None, None, 'tp'), may hold values from -0.75 to 0.75
- a_rate: float32 [2, 16, 8192], P(None, None, 'tp'), may hold values from 0.00048828125 to 0.2
- dt_bias: float32 [2, 8192], P(None, 'tp'), may hold values from -5 to -1
- skip_gain: float32 [2, 8192], P(None, 'tp'), may hold values from 0.5 to 1.5
- threshold: float32 [2, 8192], P(None, 'tp'), may hold values from 0.1 to 0.8
- w_out: bfloat16 [2, 8192, 4096], P(None, 'tp'), may hold values from -0.09375 to 0.09375
Outputs:
- hidden: bfloat16 [1024, 4096], P('seq', 'tp')
All inputs are finite; a program needn't handle non-finite values.
Results may differ from a plain program's by a relative error of at most 0.019.
Values may be sent and summed in bfloat16 or wider, within the bound.
No kernel may reach another device: no remote copies, remote signals or barrier semaphores. Data moves between devices by JAX's collectives and lax.ppermute only.
A program may use at most 192 MiB of HBM per device.

v0:
```python
import functools
import math

import jax
import jax.numpy as jnp
from jax import lax
from jax.experimental import pallas as pl
from jax.experimental.pallas import tpu as pltpu
from jax.sharding import PartitionSpec as P

LANES = 128
WIDE = 256
STRIDE = 3
EPS = 1e-05
DEPTH = 4
F32 = jnp.float32
BF16 = jnp.bfloat16
VMEM = pl.BlockSpec(memory_space=pltpu.VMEM)
SMEM = pl.BlockSpec(memory_space=pltpu.SMEM)
HBM = pl.BlockSpec(memory_space=pltpu.HBM)
ANY = pl.BlockSpec(memory_space=pl.ANY)
COST = pl.CostEstimate(flops=1, bytes_accessed=1, transcendentals=0)
LONG = pl.CostEstimate(flops=10**10, bytes_accessed=1, transcendentals=0)


def row_factor(square_sum, width):
    return lax.rsqrt(square_sum / width + EPS)


def fold_stride(count):
    return STRIDE * count + 1


def params(mebibytes):
    return pltpu.CompilerParams(vmem_limit_bytes=mebibytes * 1024 * 1024)


def proj_kernel(count, first, layer, table_at, table_ref, *refs):
    shards = refs[:count]
    gain_ref, w_ref = refs[count : count + 2]
    raw_s, split_s, sems = refs[-3:]
    cur_ref, gate_ref, square_ref = refs[-6:-3]
    rows, width = shards[0].shape
    chans = cur_ref.shape[1]
    pieces, size, _ = raw_s.shape
    pieces //= count
    per = 2 * chans // LANES
    depth = size // per
    apart = fold_stride(depth)
    taken = max(per, 16)
    places = [table_ref[table_at + j] for j in range(count)]

    def copy(j, q):
        n = j * pieces + q
        begin = (places[j] * width + q * depth) * per
        source = w_ref.at[layer, pl.ds(pl.multiple_of(begin, size), size), :]
        return pltpu.make_async_copy(source, raw_s.at[n], sems.at[n])

    for j in range(count):
        for q in range(pieces):
            copy(j, q).start()
    squares = jnp.zeros((rows, 1), F32) if first else square_ref[...]
    for j in range(count):
        values = shards[j][:, :width].astype(F32)
        gain = gain_ref[layer : layer + 1, pl.ds(pl.multiple_of(places[j] * width, width), width)]
        left = (values * gain).astype(BF16)
        squares = squares + jnp.sum(values * values, axis=1, keepdims=True)
        for q in range(pieces):
            copy(j, q).wait()
            slot = (j * pieces + q) % split_s.shape[0]
            for begin in range(0, size, taken):
                part = raw_s[j * pieces + q, begin : begin + taken, :].astype(F32)
                for k in range(taken // per):
                    d = begin // per + k
                    place = pl.ds(d * STRIDE, per, stride=apart)
                    split_s[slot, place, :] = part[k * per : (k + 1) * per]
        for e, out in enumerate((cur_ref, gate_ref)):
            for begin in range(0, chans, WIDE):
                tiles = [
                    jnp.concatenate(
                        [
                            split_s[
                                (j * pieces + q) % split_s.shape[0],
                                pl.ds((2 * t + e) * apart, depth, stride=STRIDE),
                                :,
                            ].astype(BF16)
                            for q in range(pieces)
                        ],
                        axis=0,
                    )
                    for t in range(begin // LANES, (begin + WIDE) // LANES)
                ]
                product = jnp.dot(left, jnp.concatenate(tiles, axis=1), preferred_element_type=F32)
                cols = slice(begin, begin + WIDE)
                if first and j == 0:
                    out[:, cols] = product
                else:
                    out[:, cols] += product
    square_ref[...] = squares


def project(layer, shards, table, table_at, norm_gain, w_raw, chans, before, earlier):
    count = len(shards)
    rows, width = shards[0].shape
    depth = min(width, WIDE)
    pieces = count * (width // depth)
    per = 2 * chans // LANES
    shapes = [(rows, chans), (rows, chans), (rows, 1)]
    operands = [table, *shards, norm_gain, w_raw]
    in_specs = [SMEM] + [VMEM] * (count + 1) + [HBM]
    aliases = {}
    if before is not None:
        aliases = {len(operands) + j: j for j in range(len(shapes))}
        in_specs += [VMEM] * len(shapes)
        operands += list(before)
    in_specs += [ANY] * len(earlier)
    operands += earlier
    return pl.pallas_call(
        functools.partial(proj_kernel, count, before is None, layer, table_at),
        out_shape=[jax.ShapeDtypeStruct(shape, F32) for shape in shapes],
        in_specs=in_specs,
        out_specs=[VMEM] * len(shapes),
        scratch_shapes=[
            pltpu.VMEM((pieces, depth * per, LANES), BF16),
            pltpu.VMEM((pieces, per * fold_stride(depth), LANES), F32),
            pltpu.SemaphoreType.DMA((pieces,)),
        ],
        input_output_aliases=aliases,
        compiler_params=params(36),
        cost_estimate=LONG,
        name="project",
    )(*operands)


def unpack_kernel(count, layer, table_at, width, table_ref, w_ref, *refs):
    out_ref, token_ref, raw_s, split_s, sems = refs[-5:]
    pieces, size, _ = raw_s.shape
    chans = out_ref.shape[2]
    per = 2 * chans // LANES
    depth = size // per
    apart = fold_stride(depth)
    taken = max(per, 16)
    each = width // depth

    def copy(n):
        begin = (table_ref[table_at + n // each] * width + n % each * depth) * per
        source = w_ref.at[layer, pl.ds(pl.multiple_of(begin, size), size), :]
        return pltpu.make_async_copy(source, raw_s.at[n], sems.at[n])

    for n in range(pieces):
        copy(n).start()
    token_ref[...] = jnp.zeros_like(token_ref)
    for n in range(pieces):
        copy(n).wait()
        slot = n % split_s.shape[0]
        for begin in range(0, size, taken):
            part = raw_s[n, begin : begin + taken, :].astype(F32)
            for k in range(taken // per):
                place = pl.ds((begin // per + k) * STRIDE, per, stride=apart)
                split_s[slot, place, :] = part[k * per : (k + 1) * per]
        for e in range(2):
            for begin in range(0, chans, WIDE):
                tiles = [
                    split_s[slot, pl.ds((2 * t + e) * apart, depth, stride=STRIDE), :].astype(BF16)
                    for t in range(begin // LANES, (begin + WIDE) // LANES)
                ]
                rows = slice(n * depth, (n + 1) * depth)
                out_ref[e, rows, begin : begin + WIDE] = jnp.concatenate(tiles, axis=1)


def unpack(layer, table, table_at, count, width, chans, w_raw, earlier):
    depth = min(width, WIDE)
    pieces = count * width // depth
    per = 2 * chans // LANES
    return pl.pallas_call(
        functools.partial(unpack_kernel, count, layer, table_at, width),
        out_shape=[
            jax.ShapeDtypeStruct((2, count * width, chans), BF16),
            jax.ShapeDtypeStruct((8, LANES), F32),
        ],
        in_specs=[SMEM, HBM] + [ANY] * len(earlier),
        out_specs=[VMEM, VMEM],
        scratch_shapes=[
            pltpu.VMEM((pieces, depth * per, LANES), BF16),
            pltpu.VMEM((2, per * fold_stride(depth), LANES), F32),
            pltpu.SemaphoreType.DMA((pieces,)),
        ],
        compiler_params=params(24),
        cost_estimate=COST,
        name="unpack",
    )(table, w_raw, *earlier)


def ready_kernel(count, first, layer, table_at, table_ref, *refs):
    shards = refs[:count]
    gain_ref, w_ref = refs[count : count + 2]
    cur_ref, gate_ref, square_ref = refs[-3:]
    rows, width = shards[0].shape
    chans = cur_ref.shape[1]
    squares = jnp.zeros((rows, 1), F32) if first else square_ref[...]
    parts = []
    for j in range(count):
        values = shards[j][:, :width].astype(F32)
        begin = pl.multiple_of(table_ref[table_at + j] * width, width)
        parts.append((values * gain_ref[layer : layer + 1, pl.ds(begin, width)]).astype(BF16))
        squares = squares + jnp.sum(values * values, axis=1, keepdims=True)
    square_ref[...] = squares
    left = jnp.concatenate(parts, axis=1)
    for e, out in enumerate((cur_ref, gate_ref)):
        for begin in range(0, chans, WIDE):
            cols = slice(begin, begin + WIDE)
            product = jnp.dot(left, w_ref[e, :, cols], preferred_element_type=F32)
            if first:
                out[:, cols] = product
            else:
                out[:, cols] += product


def project_ready(layer, shards, table, table_at, norm_gain, weights, before, earlier):
    count = len(shards)
    rows, width = shards[0].shape
    chans = weights.shape[2]
    state = [jax.ShapeDtypeStruct(s, F32) for s in ((rows, chans), (rows, chans), (rows, 1))]
    operands = [table, *shards, norm_gain, weights]
    in_specs = [SMEM] + [VMEM] * (count + 2)
    aliases = {}
    if before is not None:
        aliases = {len(operands) + j: j for j in range(3)}
        in_specs += [VMEM] * 3
        operands += list(before)
    return pl.pallas_call(
        functools.partial(ready_kernel, count, before is None, layer, table_at),
        out_shape=state,
        in_specs=in_specs + [ANY] * len(earlier),
        out_specs=[VMEM] * 3,
        input_output_aliases=aliases,
        compiler_params=params(12),
        cost_estimate=LONG,
        name="project_ready",
    )(*operands, *earlier)


def low_kernel(layer, table_ref, rows_ref, gain_ref, w_ref, *refs):
    width = rows_ref.shape[1]
    begin = pl.multiple_of(table_ref[0] * width, width)
    gain = gain_ref[layer : layer + 1, pl.ds(begin, width)]
    scaled = (rows_ref[...].astype(F32) * gain).astype(BF16)
    product = lax.dot_general(
        scaled, w_ref[layer], (((1,), (1,)), ((), ())), preferred_element_type=F32
    )
    out_ref = refs[-1]
    before = out_ref.shape[1] - product.shape[1]
    if before:
        out_ref[:, :before] = rows_ref[...]
    out_ref[:, before:] = product.astype(BF16)


def project_low(layer, table, own_rows, norm_gain, w_low, before, earlier):
    rows = own_rows.shape[0]
    return pl.pallas_call(
        functools.partial(low_kernel, layer),
        out_shape=jax.ShapeDtypeStruct((rows, before + w_low.shape[1]), BF16),
        in_specs=[SMEM] + [VMEM] * 3 + [ANY] * len(earlier),
        out_specs=VMEM,
        compiler_params=params(12),
        cost_estimate=COST,
        name="project_low",
    )(table, own_rows, norm_gain, w_low, *earlier)


def relay_kernel(value_ref, *refs):
    refs[-1][...] = value_ref[...]


def relay(value, *others):
    return pl.pallas_call(
        relay_kernel,
        out_shape=jax.ShapeDtypeStruct(value.shape, value.dtype),
        in_specs=[VMEM] + [ANY] * len(others),
        out_specs=VMEM,
        compiler_params=params(8),
        cost_estimate=COST,
        name="relay",
    )(value, *others)


def scan_kernel(
    layer,
    states,
    width,
    sel_ref,
    low_ref,
    square_ref,
    cur_ref,
    w_dt_ref,
    bias_ref,
    rate_ref,
    out_ref,
    time_ref,
    final_ref,
    step_s,
    drive_s,
):
    rows, chans = cur_ref.shape
    fold = chans // LANES
    rank = w_dt_ref.shape[1]
    factor = row_factor(square_ref[...], width)
    rank_part = (low_ref[:, :rank] * factor).astype(BF16)
    apart = fold_stride(rows)
    twice = factor * factor
    for begin in range(0, chans, WIDE):
        cols = slice(begin, begin + WIDE)
        pre = jnp.dot(rank_part, w_dt_ref[layer, :, cols], preferred_element_type=F32)
        pre = pre + bias_ref[layer : layer + 1, cols]
        step = jnp.maximum(pre, 0.0) + jnp.log1p(jnp.exp(-jnp.abs(pre)))
        drive = step * (cur_ref[:, cols] * twice)
        for q in range(WIDE // LANES):
            part = slice(q * LANES, (q + 1) * LANES)
            place = pl.ds((begin // LANES + q) * apart, rows, stride=STRIDE)
            step_s[place, :] = step[:, part]
            drive_s[place, :] = drive[:, part]

    def advance(t, carried):
        time, held = carried
        here = pl.ds(t * STRIDE, fold, stride=apart)
        step = step_s[here, :]
        drive = drive_s[here, :]
        sums = [None] * 4
        after = []
        for s in range(states):
            decay = jnp.exp2(step * rate_ref[layer, s])
            now = decay * held[s] + drive * sel_ref[t, s]
            term = now * sel_ref[t, states + s]
            sums[s % 4] = term if sums[s % 4] is None else sums[s % 4] + term
            after.append(now)
        time = time + step
        out_ref[here, :] = (sums[0] + sums[1]) + (sums[2] + sums[3])
        time_ref[here, :] = time
        return time, tuple(after)

    zero = jnp.zeros((fold, LANES), F32)
    time, held = lax.fori_loop(0, rows, advance, (zero, (zero,) * states), unroll=8)
    for s in range(states):
        final_ref[s] = held[s].astype(BF16)
    final_ref[states] = time.astype(BF16)


def local_scan(layer, width, selectors, low, square, cur, w_dt, dt_bias, rate):
    rows, chans = cur.shape
    _, states, fold, _ = rate.shape
    folded = (fold * fold_stride(rows), LANES)
    return pl.pallas_call(
        functools.partial(scan_kernel, layer, states, width),
        out_shape=[
            jax.ShapeDtypeStruct(folded, F32),
            jax.ShapeDtypeStruct(folded, F32),
            jax.ShapeDtypeStruct((states + 1, fold, LANES), BF16),
        ],
        in_specs=[SMEM] + [VMEM] * 6,
        out_specs=[VMEM] * 3,
        scratch_shapes=[pltpu.VMEM(folded, F32), pltpu.VMEM(folded, F32)],
        compiler_params=params(20),
        cost_estimate=COST,
        name="local_scan",
    )(selectors, low, square, cur, w_dt, dt_bias, rate)


def emit_chunks(layer, table_at, feat, gated_ref, table_ref, w_ref, chunks, w_s, sems, before=None):
    def copy(j):
        begin = pl.multiple_of(table_ref[table_at[j]] * feat, feat)
        return pltpu.make_async_copy(w_ref.at[layer, :, pl.ds(begin, feat)], w_s.at[j], sems.at[j])

    for j in range(len(chunks)):
        copy(j).start()
    if before is not None:
        before()
    for j, chunk in enumerate(chunks):
        copy(j).wait()
        for begin in range(0, feat, WIDE):
            cols = slice(begin, begin + WIDE)
            chunk[:, cols] = jnp.dot(
                gated_ref[...], w_s[j, :, cols], preferred_element_type=F32
            ).astype(BF16)


def close_kernel(layer, states, table_at, feat, width, table_ref, place_ref, sel_ref, *refs):
    out_ref, time_ref, cur_ref, gate_ref, square_ref, final_ref = refs[:6]
    rate_ref, skip_ref, thresh_ref, w_ref, gated_ref = refs[6:11]
    chunks = refs[11 : 11 + len(table_at)]
    enter_s, mixed_s, w_s, sems = refs[-4:]
    rows, chans = cur_ref.shape
    fold = chans // LANES
    apart = fold_stride(rows)

    def gate_all():
        def enter(p, state):
            time = final_ref[p, states].astype(F32)
            return tuple(
                jnp.exp2(time * rate_ref[layer, s]) * state[s] + final_ref[p, s].astype(F32)
                for s in range(states)
            )

        zero = jnp.zeros((fold, LANES), F32)
        state = lax.fori_loop(0, place_ref[0], enter, (zero,) * states)
        for s in range(states):
            enter_s[s] = state[s]

        def correct(t, carried):
            here = pl.ds(t * STRIDE, fold, stride=apart)
            time = time_ref[here, :]
            sums = [out_ref[here, :], None, None, None]
            for s in range(states):
                term = jnp.exp2(time * rate_ref[layer, s]) * (enter_s[s] * sel_ref[t, states + s])
                sums[s % 4] = term if sums[s % 4] is None else sums[s % 4] + term
            mixed_s[here, :] = (sums[0] + sums[1]) + (sums[2] + sums[3])
            return carried

        lax.fori_loop(0, rows, correct, 0, unroll=8)

        factor = row_factor(square_ref[...], width)
        for r in range(fold):
            cols = slice(r * LANES, (r + 1) * LANES)
            skip = skip_ref[layer : layer + 1, cols]
            mixed = mixed_s[pl.ds(r * apart, rows, stride=STRIDE), :] + skip * cur_ref[:, cols]
            mixed = mixed * factor
            normal = mixed * lax.rsqrt(jnp.mean(mixed * mixed, axis=1, keepdims=True) + EPS)
            thresh = thresh_ref[layer : layer + 1, cols]
            shrunk = jnp.maximum(normal - thresh, 0.0) - jnp.maximum(-normal - thresh, 0.0)
            gate = gate_ref[:, cols] * factor
            gated_ref[:, cols] = (shrunk * (gate * jax.nn.sigmoid(gate))).astype(BF16)

    emit_chunks(layer, table_at, feat, gated_ref, table_ref, w_ref, chunks, w_s, sems, gate_all)


def close_layer(
    layer, width, table, table_at, feat, seq_place, selectors, values, rate, skip, thresh, w_out
):
    rows, chans = values[2].shape
    _, states, fold, _ = rate.shape
    count = len(table_at)
    chunk = jax.ShapeDtypeStruct((rows, feat), BF16)
    results = pl.pallas_call(
        functools.partial(close_kernel, layer, states, table_at, feat, width),
        out_shape=[jax.ShapeDtypeStruct((rows, chans), BF16)] + [chunk] * count,
        in_specs=[SMEM] * 3 + [VMEM] * 9 + [HBM],
        out_specs=[VMEM] * (1 + count),
        scratch_shapes=[
            pltpu.VMEM((states, fold, LANES), F32),
            pltpu.VMEM((fold * fold_stride(rows), LANES), F32),
            pltpu.VMEM((count, chans, feat), BF16),
            pltpu.SemaphoreType.DMA((count,)),
        ],
        compiler_params=params(40),
        cost_estimate=COST,
        name="close_layer",
    )(table, seq_place, selectors, *values, rate, skip, thresh, w_out)
    return results[0], results[1:]


def expand_kernel(layer, table_at, feat, table_ref, gated_ref, w_ref, *refs):
    chunks = refs[: len(table_at)]
    emit_chunks(layer, table_at, feat, gated_ref, table_ref, w_ref, chunks, *refs[-2:])


def expand(layer, table, table_at, feat, gated, w_out):
    rows, chans = gated.shape
    count = len(table_at)
    return pl.pallas_call(
        functools.partial(expand_kernel, layer, table_at, feat),
        out_shape=[jax.ShapeDtypeStruct((rows, feat), BF16)] * count,
        in_specs=[SMEM, VMEM, HBM],
        out_specs=[VMEM] * count,
        scratch_shapes=[
            pltpu.VMEM((count, chans, feat), BF16),
            pltpu.SemaphoreType.DMA((count,)),
        ],
        compiler_params=params(40),
        cost_estimate=COST,
        name="expand",
    )(table, gated, w_out)


def finish_kernel(rank, own_ref, arrived_ref, *refs):
    low_ref, selectors_ref = refs[-2:]
    total = own_ref[...].astype(F32) + arrived_ref[...].astype(F32)
    low_ref[...] = total
    selectors_ref[...] = total[:, rank:]


def finish_low(rank, own, arrived, earlier):
    rows, count = own.shape
    return pl.pallas_call(
        functools.partial(finish_kernel, rank),
        out_shape=[
            jax.ShapeDtypeStruct((rows, count), F32),
            jax.ShapeDtypeStruct((rows, count - rank), F32),
        ],
        in_specs=[VMEM] * 2 + [ANY] * len(earlier),
        out_specs=[VMEM] * 2,
        compiler_params=params(8),
        cost_estimate=COST,
        name="finish_low",
    )(own, arrived, *earlier)


def combine_kernel(count, *refs):
    total = refs[0][...].astype(F32)
    for ref in refs[1:count]:
        total = total + ref[...].astype(F32)
    refs[-1][...] = total.astype(BF16)


def combine(values, earlier):
    return pl.pallas_call(
        functools.partial(combine_kernel, len(values)),
        out_shape=jax.ShapeDtypeStruct(values[0].shape, BF16),
        in_specs=[VMEM] * len(values) + [ANY] * len(earlier),
        out_specs=VMEM,
        compiler_params=params(8),
        cost_estimate=COST,
        name="combine",
    )(*values, *earlier)


class Grid:
    def __init__(self, count):
        self.depth = DEPTH if count % DEPTH == 0 else 1
        self.side = count // self.depth

    def places(self):
        return [(z, y) for z in range(self.depth) for y in range(self.side)]

    def at(self, z, y):
        return (z % self.depth) * self.side + y % self.side

    def send(self, value, deep, across):
        pairs = [(self.at(z, y), self.at(z + deep, y + across)) for z, y in self.places()]
        return lax.ppermute(value, "tp", pairs)

    def swap(self, value, bit):
        pairs = [(self.at(z, y), self.at(z ^ bit, y)) for z, y in self.places()]
        return lax.ppermute(value, "tp", pairs)

    def table(self):
        own = lax.axis_index("tp")
        z, y = own // self.side, own % self.side
        offsets = jnp.arange(self.depth * self.side, dtype=jnp.int32)
        a, b = offsets // self.side, offsets % self.side
        both = []
        for sign in (-1, 1):
            deep = (z + sign * a + self.depth) % self.depth
            both.append(deep * self.side + (y + sign * b + self.side) % self.side)
        return jnp.concatenate(both).astype(jnp.int32)


def gather_columns(grid, own):
    columns = {0: own}
    half = grid.depth // 2
    for a in range(1, grid.depth - half + 1):
        columns[a] = grid.send(columns[a - 1], 1, 0)
        back = grid.depth - a
        if back > a:
            columns[back] = grid.send(columns[(back + 1) % grid.depth], -1, 0)
    return columns


def scatter_order(grid):
    order = []
    for a in range(grid.depth - grid.depth // 2, 0, -1):
        order.append(a)
        if grid.depth - a > a:
            order.append(grid.depth - a)
    return order + [0]


def scatter_sum(grid, own_rows, chunks, aside):
    order = scatter_order(grid)
    crossed = {
        a: [grid.send(chunks[a, b], 0, b) for b in range(1, grid.side)] for a in order
    }
    half = grid.depth - grid.depth // 2
    arriving = {a: [] for a in order}
    waiting = []
    for n, a in enumerate(order):
        parts = [chunks[a, 0], *crossed[a], *arriving[a]]
        if a == 0:
            aside(n, [*crossed[a], chunks[a, 0]][0])
            return combine([own_rows, *parts], waiting)
        part = combine(parts, waiting)
        step = 1 if a <= half else -1
        arriving[(a - step) % grid.depth].append(grid.send(part, step, 0))
        waiting = aside(n, part)


def sum_selectors(grid, partials):
    total = sum(partial.astype(F32) for partial in partials)
    pairs = []
    bit = 1
    while True:
        rounded = total.astype(BF16)
        arrived = grid.swap(rounded, bit) if bit < grid.depth else jnp.zeros_like(rounded)
        pairs.append((rounded, arrived))
        bit *= 2
        if bit >= grid.depth:
            return pairs
        total = rounded.astype(F32) + arrived.astype(F32)


def per_device(
    n_tp, tokens, norm_gain, w_in, w_low, w_dt, a_rate, dt_bias, skip_gain, threshold, w_out
):
    grid = Grid(n_tp)
    feat = tokens.shape[1]
    layers, width, _, chans = w_in.shape
    states = a_rate.shape[1]
    rank = w_dt.shape[1]
    fold = chans // LANES
    table = grid.table()
    forth = lambda a, b: n_tp + a * grid.side + b
    seq_place = lax.axis_index("seq").astype(jnp.int32).reshape(1)
    rates = (a_rate * (-math.log2(math.e))).reshape(layers, states, fold, LANES)
    w_raw = w_in.reshape(layers, width, 2, fold, LANES).transpose(0, 1, 3, 2, 4)
    w_raw = w_raw.reshape(layers, width * 2 * fold, LANES)
    order = scatter_order(grid)
    own_rows = tokens
    low_t = jnp.swapaxes(w_low, 1, 2)
    arrivals = [0] + [a for a in order if a not in (0, order[0])] + order[:1]
    weights = {}
    for layer in range(layers):
        columns = gather_columns(grid, own_rows)
        cross = lambda column: [grid.send(column, 0, b) for b in range(1, grid.side)]
        packed = layer > 0
        if packed:
            low = project_low(layer, table, own_rows, norm_gain, low_t, feat, [])
            beside = {0: cross(low)}
            lows = [each[:, feat:] for each in (low, *beside[0])]
        else:
            beside = {0: cross(own_rows)}
            low = project_low(layer, table, own_rows, norm_gain, low_t, 0, beside[0])
            lows = [low, *cross(low)]
            weights[0], _ = unpack(layer, table, 0, grid.side, feat, chans, w_raw, [])
        pairs = sum_selectors(grid, lows)
        stages = [own for own, _ in pairs]
        state = None
        for n, a in enumerate(arrivals):
            if n:
                last = n + 1 == len(arrivals)
                beside[a] = cross(relay(columns[a], *first) if last else columns[a])
            arrived = [columns[a], *beside[a]]
            place, earlier = a * grid.side, stages[n - 1 : n] if n else []
            if a in weights:
                state = project_ready(
                    layer, arrived, table, place, norm_gain, weights[a], state, earlier
                )
            else:
                state = project(
                    layer, arrived, table, place, norm_gain, w_raw, chans, state, earlier
                )
            if n == 0:
                first = [state[2], *stages[1:2]] if packed else [state[2]]
        cur, gate, square = state
        low, selectors = finish_low(rank, *pairs[-1], [square])
        out, time, final = local_scan(
            layer, width, selectors, low, square, cur, w_dt, dt_bias, rates
        )
        finals = lax.all_gather(final, "seq")
        keys = [(a, b) for a in order for b in range(1, grid.side)]
        keys += [(a, 0) for a in order]
        lead = grid.side - 1
        gated, chunks = close_layer(
            layer,
            width,
            table,
            [forth(*key) for key in keys[:lead]],
            feat,
            seq_place,
            selectors,
            (out, time, cur, gate, square, finals),
            rates,
            skip_gain,
            threshold,
            w_out,
        )
        chunks = dict(zip(keys, chunks))
        split = len(order) * lead + 1
        for part in (keys[lead:split], keys[split:]):
            more = expand(layer, table, [forth(*key) for key in part], feat, gated, w_out)
            chunks.update(zip(part, more))
        weights = {}

        def aside(n, value):
            left = [a for a in arrivals if a not in weights]
            wanted = [1, 0, len(left) - 1, 1][min(n, 3)] if layer + 1 < layers else 0
            tokens = []
            for a in left[:wanted]:
                weights[a], token = unpack(
                    layer + 1, table, a * grid.side, grid.side, feat, chans, w_raw, [value]
                )
                tokens.append(token)
            return tokens

        own_rows = scatter_sum(grid, own_rows, chunks, aside)
    return own_rows


def solution(mesh):
    in_specs = (
        P("seq", "tp"),
        P(),
        P(None, None, None, "tp"),
        P(None, "tp", None),
        P(None, None, "tp"),
        P(None, None, "tp"),
        P(None, "tp"),
        P(None, "tp"),
        P(None, "tp"),
        P(None, "tp", None),
    )
    return jax.shard_map(
        functools.partial(per_device, mesh.shape["tp"]),
        mesh=mesh,
        in_specs=in_specs,
        out_specs=P("seq", "tp"),
        check_vma=False,
    )
```

profile of v0, /device:TPU:0, one launch (start us, length us, event | category | flops | bytes accessed | tf_op | source)
XLA Modules:
  0.0 183.3 jit_solution(1143384746533294957)
XLA Ops:
  0.0 3.0 %collective-permute-start = (bf16[256,512]{1,0:T(8,128)(2,1)}, bf16[256,512]{1,0:T(8,128)(2,1)S(1)}, u32[]{:S(2)}, u32[]{:S(2)}) collective-permute-start(bf16[256,512]{1,0:T(8,128)(2,1)} %refs_0_.3), channel_id=1, source_target_pairs={{0,1},{1,0},{2,3},{3,2},{4,5},{5,4},{6,7},{7,6},{8,9},{9,8},{10,11... | collective-permute-start | bytes 786440 | tf_op jit(solution)/shard_map/ppermute | solution.py:538
  6.9 3.3 %unpack.5 = (bf16[2,1024,1024]{2,1,0:T(8,128)(2,1)S(1)}, f32[8,128]{1,0:T(8,128)}) custom-call(s32[16]{0:T(128)S(1)} %pad_add_fusion.table_ref, bf16[2,65536,128]{2,1,0:T(8,128)(2,1)} %bitcast.21), custom_call_target="tpu_custom_call" | custom-call | flops 1 | bytes 1 | tf_op jit(solution)/shard_map/unpack/pallas_call | solution.py:175
  21.2 3.4 %collective-permute-start.2 = (bf16[256,288]{1,0:T(8,128)(2,1)S(1)}, bf16[256,288]{1,0:T(8,128)(2,1)S(1)}, u32[]{:S(2)}, u32[]{:S(2)}) collective-permute-start(bf16[256,288]{1,0:T(8,128)(2,1)S(1)} %add_convert_fusion.3.refs_7_), channel_id=1, source_target_pairs={{0,2},{1,3},{2,0},{3,1},{4,6},{5,7},{6,4},{7,5},{8,10},{9,11},{10,... | collective-permute-start | bytes 442376 | tf_op jit(solution)/shard_map/ppermute | solution.py:542
  26.7 3.8 %project.3 = (f32[256,1024]{1,0:T(8,128)S(1)}, f32[256,1024]{1,0:T(8,128)S(1)}, f32[256,1]{1,0:T(8,128)S(1)}) custom-call(s32[16]{0:T(128)S(1)} %pad_add_fusion.table_ref, bf16[256,512]{1,0:T(8,128)(2,1)S(1)} %collective-permute-done.4.refs_0_, ...), custom_call_target="tpu_custom_call", output_to_operand_aliasing={{0}: (5, {}), {1}: (6, {}), {2}: (7, {})} | custom-call | flops 10000000000 | bytes 1 | tf_op jit(solution)/shard_map/project/pallas_call | solution.py:118
  32.7 3.8 %project.4 = (f32[256,1024]{1,0:T(8,128)S(1)}, f32[256,1024]{1,0:T(8,128)S(1)}, f32[256,1]{1,0:T(8,128)S(1)}) custom-call(s32[16]{0:T(128)S(1)} %pad_add_fusion.table_ref, bf16[256,512]{1,0:T(8,128)(2,1)S(1)} %collective-permute-done.7.refs_0_, ...), custom_call_target="tpu_custom_call", output_to_operand_aliasing={{0}: (5, {}), {1}: (6, {}), {2}: (7, {})} | custom-call | flops 10000000000 | bytes 1 | tf_op jit(solution)/shard_map/project/pallas_call | solution.py:118
  36.5 3.8 %project.5 = (f32[256,1024]{1,0:T(8,128)S(1)}, f32[256,1024]{1,0:T(8,128)S(1)}, f32[256,1]{1,0:T(8,128)S(1)}) custom-call(s32[16]{0:T(128)S(1)} %pad_add_fusion.table_ref, bf16[256,512]{1,0:T(8,128)(2,1)S(1)} %collective-permute-done.5.value_ref.refs_0_, ...), custom_call_target="tpu_custom_call", output_to_operand_aliasing={{0}: (5, {}), {1}: (6, {}), {2}: (7, {})} | custom-call | flops 10000000000 | bytes 1 | tf_op jit(solution)/shard_map/project/pallas_call | solution.py:118
  40.4 8.8 %local_scan.2 = (f32[6152,128]{1,0:T(8,128)S(1)}, f32[6152,128]{1,0:T(8,128)S(1)}, bf16[17,8,128]{2,1,0:T(8,128)(2,1)S(1)}) custom-call(f32[256,32]{1,0:T(8,128)S(1)} %get-tuple-element.76.sel_ref, f32[256,288]{1,0:T(8,128)S(1)} %get-tuple-element.77.low_ref, f32[256,1]{1,0:T(8,128)S(1)} %get-tuple-element.75.refs_0_.square_ref.refs_4_, ...), custom_call_target="tpu_custom_call" | custom-call | flops 1 | bytes 1 | tf_op jit(solution)/shard_map/local_scan/pallas_call | solution.py:352
  49.1 5.4 %all-gather = bf16[68,8,128]{2,1,0:T(8,128)(2,1)S(1)} all-gather(bf16[17,8,128]{2,1,0:T(8,128)(2,1)S(1)} %get-tuple-element.82), channel_id=2, replica_groups=mesh['seq'=4,'tp'=8] {'seq'}, dimensions={0}, use_global_device_ids=true | all-gather | bytes 174080 | tf_op jit(solution)/shard_map/all_gather | solution.py:666
  54.6 7.7 %close_layer.2 = (bf16[256,1024]{1,0:T(8,128)(2,1)S(1)}, bf16[256,512]{1,0:T(8,128)(2,1)S(1)}) custom-call(s32[16]{0:T(128)S(1)} %pad_add_fusion.table_ref, s32[1]{0:T(128)} %bitcast.place_ref, f32[256,32]{1,0:T(8,128)S(1)} %get-tuple-element.76.sel_ref, f32[6152,128]{1,0:T(8,128)S(1)} %get-tuple-element.79.refs_0_, ...), custom_call_target="tpu_custom_call" | custom-call | flops 1 | bytes 1 | tf_op jit(solution)/shard_map/close_layer/pallas_call | solution.py:442
  62.8 3.6 %expand.5 = (bf16[256,512]{1,0:T(8,128)(2,1)S(1)}, bf16[256,512]{1,0:T(8,128)(2,1)S(1)}, bf16[256,512]{1,0:T(8,128)(2,1)S(1)}, bf16[256,512]{1,0:T(8,128)(2,1)S(1)}) custom-call(s32[16]{0:T(128)S(1)} %pad_add_fusion.table_ref, bf16[256,1024]{1,0:T(8,128)(2,1)S(1)} %get-tuple-element.83.gated_ref, bf16[2,1024,4096]{2,1,0:T(8,128)(2,1)} %w_ref.7), custom_call_target="tpu_custom_call" | custom-call | flops 1 | bytes 1 | tf_op jit(solution)/shard_map/expand/pallas_call | solution.py:468
  68.5 3.0 %collective-permute-done.12.refs_1_ = bf16[256,512]{1,0:T(8,128)(2,1)S(1)} collective-permute-done((bf16[256,512]{1,0:T(8,128)(2,1)S(1)}, bf16[256,512]{1,0:T(8,128)(2,1)S(1)}, u32[]{:S(2)}, u32[]{:S(2)}) %collective-permute-start.12) | collective-permute-done | bytes 262176 | tf_op jit(solution)/shard_map/ppermute | solution.py:538
  72.0 3.1 %expand.4 = (bf16[256,512]{1,0:T(8,128)(2,1)S(1)}, bf16[256,512]{1,0:T(8,128)(2,1)S(1)}, bf16[256,512]{1,0:T(8,128)(2,1)S(1)}) custom-call(s32[16]{0:T(128)S(1)} %pad_add_fusion.table_ref, bf16[256,1024]{1,0:T(8,128)(2,1)S(1)} %get-tuple-element.83.gated_ref, bf16[2,1024,4096]{2,1,0:T(8,128)(2,1)} %w_ref.7), custom_call_target="tpu_custom_call" | custom-call | flops 1 | bytes 1 | tf_op jit(solution)/shard_map/expand/pallas_call | solution.py:468
  75.9 3.0 %unpack.6 = (bf16[2,1024,1024]{2,1,0:T(8,128)(2,1)S(1)}, f32[8,128]{1,0:T(8,128)S(1)}) custom-call(s32[16]{0:T(128)S(1)} %pad_add_fusion.table_ref, bf16[2,65536,128]{2,1,0:T(8,128)(2,1)} %bitcast.25, bf16[256,512]{1,0:T(8,128)(2,1)S(1)} %combine.8.refs_0_), custom_call_target="tpu_custom_call" | custom-call | flops 1 | bytes 1 | tf_op jit(solution)/shard_map/unpack/pallas_call | solution.py:175
  79.0 3.3 %collective-permute-start.16 = (bf16[256,512]{1,0:T(8,128)(2,1)S(1)}, bf16[256,512]{1,0:T(8,128)(2,1)S(1)}, u32[]{:S(2)}, u32[]{:S(2)}) collective-permute-start(bf16[256,512]{1,0:T(8,128)(2,1)S(1)} %combine.10.refs_0_), channel_id=1, source_target_pairs={{0,6},{1,7},{2,0},{3,1},{4,2},{5,3},{6,4},{7,5},{8,14},{9,15},{10,... | collective-permute-start | bytes 786440 | tf_op jit(solution)/shard_map/ppermute | solution.py:538
  83.2 3.0 %unpack.7 = (bf16[2,1024,1024]{2,1,0:T(8,128)(2,1)S(1)}, f32[8,128]{1,0:T(8,128)S(1)}) custom-call(s32[16]{0:T(128)S(1)} %pad_add_fusion.table_ref, bf16[2,65536,128]{2,1,0:T(8,128)(2,1)} %bitcast.26, bf16[256,512]{1,0:T(8,128)(2,1)S(1)} %combine.10.refs_0_), custom_call_target="tpu_custom_call" | custom-call | flops 1 | bytes 1 | tf_op jit(solution)/shard_map/unpack/pallas_call | solution.py:175
  86.3 3.1 %unpack.8 = (bf16[2,1024,1024]{2,1,0:T(8,128)(2,1)S(1)}, f32[8,128]{1,0:T(8,128)S(1)}) custom-call(s32[16]{0:T(128)S(1)} %pad_add_fusion.table_ref, bf16[2,65536,128]{2,1,0:T(8,128)(2,1)} %bitcast.27, bf16[256,512]{1,0:T(8,128)(2,1)S(1)} %combine.10.refs_0_), custom_call_target="tpu_custom_call" | custom-call | flops 1 | bytes 1 | tf_op jit(solution)/shard_map/unpack/pallas_call | solution.py:175
  89.4 3.4 %collective-permute-done.14.refs_3_ = bf16[256,512]{1,0:T(8,128)(2,1)S(1)} collective-permute-done((bf16[256,512]{1,0:T(8,128)(2,1)S(1)}, bf16[256,512]{1,0:T(8,128)(2,1)S(1)}, u32[]{:S(2)}, u32[]{:S(2)}) %collective-permute-start.14) | collective-permute-done | bytes 262176 | tf_op jit(solution)/shard_map/ppermute | solution.py:538
  99.3 3.3 %unpack.9 = (bf16[2,1024,1024]{2,1,0:T(8,128)(2,1)S(1)}, f32[8,128]{1,0:T(8,128)}) custom-call(s32[16]{0:T(128)S(1)} %pad_add_fusion.table_ref, bf16[2,65536,128]{2,1,0:T(8,128)(2,1)} %bitcast.28, bf16[256,512]{1,0:T(8,128)(2,1)S(1)} %collective-permute-done.10.refs_2_.refs_0_), custom_call_target="tpu_custom_call" | custom-call | flops 1 | bytes 1 | tf_op jit(solution)/shard_map/unpack/pallas_call | solution.py:175
  102.6 3.9 %collective-permute-done.20.refs_0_ = bf16[256,512]{1,0:T(8,128)(2,1)S(1)} collective-permute-done((bf16[256,512]{1,0:T(8,128)(2,1)S(1)}, bf16[256,512]{1,0:T(8,128)(2,1)S(1)}, u32[]{:S(2)}, u32[]{:S(2)}) %collective-permute-start.20) | collective-permute-done | bytes 262176 | tf_op jit(solution)/shard_map/ppermute | solution.py:538
  108.9 3.2 %collective-permute-done.23.refs_0_ = bf16[256,512]{1,0:T(8,128)(2,1)S(1)} collective-permute-done((bf16[256,512]{1,0:T(8,128)(2,1)S(1)}, bf16[256,512]{1,0:T(8,128)(2,1)S(1)}, u32[]{:S(2)}, u32[]{:S(2)}) %collective-permute-start.23) | collective-permute-done | bytes 262176 | tf_op jit(solution)/shard_map/ppermute | solution.py:538
  115.4 5.0 %collective-permute-done.18 = bf16[256,288]{1,0:T(8,128)(2,1)S(1)} collective-permute-done((bf16[256,288]{1,0:T(8,128)(2,1)S(1)}, bf16[256,288]{1,0:T(8,128)(2,1)S(1)}, u32[]{:S(2)}, u32[]{:S(2)}) %collective-permute-start.18) | collective-permute-done | bytes 147488 | tf_op jit(solution)/shard_map/ppermute | solution.py:542
  125.7 2.7 %collective-permute-done.22.refs_1_ = bf16[256,512]{1,0:T(8,128)(2,1)S(1)} collective-permute-done((bf16[256,512]{1,0:T(8,128)(2,1)S(1)}, bf16[256,512]{1,0:T(8,128)(2,1)S(1)}, u32[]{:S(2)}, u32[]{:S(2)}) %collective-permute-start.22) | collective-permute-done | bytes 262176 | tf_op jit(solution)/shard_map/ppermute | solution.py:538
  131.1 8.8 %local_scan.3 = (f32[6152,128]{1,0:T(8,128)S(1)}, f32[6152,128]{1,0:T(8,128)S(1)}, bf16[17,8,128]{2,1,0:T(8,128)(2,1)S(1)}) custom-call(f32[256,32]{1,0:T(8,128)S(1)} %get-tuple-element.109.sel_ref, f32[256,288]{1,0:T(8,128)S(1)} %get-tuple-element.110.low_ref, f32[256,1]{1,0:T(8,128)S(1)} %get-tuple-element.108.refs_0_.square_ref.refs_4_, ...), custom_call_target="tpu_custom_call" | custom-call | flops 1 | bytes 1 | tf_op jit(solution)/shard_map/local_scan/pallas_call | solution.py:352
  139.8 5.4 %all-gather.1 = bf16[68,8,128]{2,1,0:T(8,128)(2,1)S(1)} all-gather(bf16[17,8,128]{2,1,0:T(8,128)(2,1)S(1)} %get-tuple-element.115), channel_id=3, replica_groups=mesh['seq'=4,'tp'=8] {'seq'}, dimensions={0}, use_global_device_ids=true | all-gather | bytes 174080 | tf_op jit(solution)/shard_map/all_gather | solution.py:666
  145.3 7.5 %close_layer.3 = (bf16[256,1024]{1,0:T(8,128)(2,1)S(1)}, bf16[256,512]{1,0:T(8,128)(2,1)S(1)}) custom-call(s32[16]{0:T(128)S(1)} %pad_add_fusion.table_ref, s32[1]{0:T(128)} %bitcast.place_ref, f32[256,32]{1,0:T(8,128)S(1)} %get-tuple-element.109.sel_ref, f32[6152,128]{1,0:T(8,128)S(1)} %get-tuple-element.112.refs_0_, ...), custom_call_target="tpu_custom_call" | custom-call | flops 1 | bytes 1 | tf_op jit(solution)/shard_map/close_layer/pallas_call | solution.py:442
  154.1 3.6 %expand.7 = (bf16[256,512]{1,0:T(8,128)(2,1)S(1)}, bf16[256,512]{1,0:T(8,128)(2,1)S(1)}, bf16[256,512]{1,0:T(8,128)(2,1)S(1)}, bf16[256,512]{1,0:T(8,128)(2,1)S(1)}) custom-call(s32[16]{0:T(128)S(1)} %pad_add_fusion.table_ref, bf16[256,1024]{1,0:T(8,128)(2,1)S(1)} %get-tuple-element.116.gated_ref, bf16[2,1024,4096]{2,1,0:T(8,128)(2,1)} %w_ref.7), custom_call_target="tpu_custom_call" | custom-call | flops 1 | bytes 1 | tf_op jit(solution)/shard_map/expand/pallas_call | solution.py:468
  159.7 2.3 %collective-permute-done.28.refs_1_ = bf16[256,512]{1,0:T(8,128)(2,1)S(1)} collective-permute-done((bf16[256,512]{1,0:T(8,128)(2,1)S(1)}, bf16[256,512]{1,0:T(8,128)(2,1)S(1)}, u32[]{:S(2)}, u32[]{:S(2)}) %collective-permute-start.28) | collective-permute-done | bytes 262176 | tf_op jit(solution)/shard_map/ppermute | solution.py:538
  162.2 3.1 %expand.6 = (bf16[256,512]{1,0:T(8,128)(2,1)S(1)}, bf16[256,512]{1,0:T(8,128)(2,1)S(1)}, bf16[256,512]{1,0:T(8,128)(2,1)S(1)}) custom-call(s32[16]{0:T(128)S(1)} %pad_add_fusion.table_ref, bf16[256,1024]{1,0:T(8,128)(2,1)S(1)} %get-tuple-element.116.gated_ref, bf16[2,1024,4096]{2,1,0:T(8,128)(2,1)} %w_ref.7), custom_call_target="tpu_custom_call" | custom-call | flops 1 | bytes 1 | tf_op jit(solution)/shard_map/expand/pallas_call | solution.py:468
  167.7 2.7 %collective-permute-start.32 = (bf16[256,512]{1,0:T(8,128)(2,1)S(1)}, bf16[256,512]{1,0:T(8,128)(2,1)S(1)}, u32[]{:S(2)}, u32[]{:S(2)}) collective-permute-start(bf16[256,512]{1,0:T(8,128)(2,1)S(1)} %combine.14), channel_id=1, source_target_pairs={{0,6},{1,7},{2,0},{3,1},{4,2},{5,3},{6,4},{7,5},{8,14},{9,15},{10,... | collective-permute-start | bytes 786440 | tf_op jit(solution)/shard_map/ppermute | solution.py:538
  170.4 2.8 %collective-permute-done.27.refs_1_ = bf16[256,512]{1,0:T(8,128)(2,1)S(1)} collective-permute-done((bf16[256,512]{1,0:T(8,128)(2,1)S(1)}, bf16[256,512]{1,0:T(8,128)(2,1)S(1)}, u32[]{:S(2)}, u32[]{:S(2)}) %collective-permute-start.27) | collective-permute-done | bytes 262176 | tf_op jit(solution)/shard_map/ppermute | solution.py:538
  173.4 4.9 %collective-permute-done.26.refs_2_ = bf16[256,512]{1,0:T(8,128)(2,1)S(1)} collective-permute-done((bf16[256,512]{1,0:T(8,128)(2,1)S(1)}, bf16[256,512]{1,0:T(8,128)(2,1)S(1)}, u32[]{:S(2)}, u32[]{:S(2)}) %collective-permute-start.26) | collective-permute-done | bytes 262176 | tf_op jit(solution)/shard_map/ppermute | solution.py:538
  178.3 4.1 %collective-permute-done.30.refs_3_ = bf16[256,512]{1,0:T(8,128)(2,1)S(1)} collective-permute-done((bf16[256,512]{1,0:T(8,128)(2,1)S(1)}, bf16[256,512]{1,0:T(8,128)(2,1)S(1)}, u32[]{:S(2)}, u32[]{:S(2)}) %collective-permute-start.30) | collective-permute-done | bytes 262176 | tf_op jit(solution)/shard_map/ppermute | solution.py:538
  (99 shorter events, 51.0 us)
Async XLA Ops:
  0.0 12.3 %collective-permute-start = (bf16[256,512]{1,0:T(8,128)(2,1)}, bf16[256,512]{1,0:T(8,128)(2,1)S(1)}, u32[]{:S(2)}, u32[]{:S(2)}) collective-permute-start(bf16[256,512]{1,0:T(8,128)(2,1)} %refs_0_.3), channel_id=1, source_target_pairs={{0,1},{1,0},{2,3},{3,2},{4,5},{5,4},{6,7},{7,6},{8,9},{9,8},{10,11... | collective-permute-start | bytes 786440 | tf_op jit(solution)/shard_map/ppermute | solution.py:538
  3.0 11.3 %collective-permute-start.4 = (bf16[256,512]{1,0:T(8,128)(2,1)}, bf16[256,512]{1,0:T(8,128)(2,1)S(1)}, u32[]{:S(2)}, u32[]{:S(2)}) collective-permute-start(bf16[256,512]{1,0:T(8,128)(2,1)} %refs_0_.3), channel_id=1, source_target_pairs={{0,2},{1,3},{2,4},{3,5},{4,6},{5,7},{6,0},{7,1},{8,10},{9,11},{10,... | collective-permute-start | bytes 786440 | tf_op jit(solution)/shard_map/ppermute | solution.py:538
  4.5 14.8 %collective-permute-start.7 = (bf16[256,512]{1,0:T(8,128)(2,1)}, bf16[256,512]{1,0:T(8,128)(2,1)S(1)}, u32[]{:S(2)}, u32[]{:S(2)}) collective-permute-start(bf16[256,512]{1,0:T(8,128)(2,1)} %refs_0_.3), channel_id=1, source_target_pairs={{0,6},{1,7},{2,0},{3,1},{4,2},{5,3},{6,4},{7,5},{8,14},{9,15},{10,... | collective-permute-start | bytes 786440 | tf_op jit(solution)/shard_map/ppermute | solution.py:538
  13.2 7.9 %collective-permute-start.1 = (bf16[256,288]{1,0:T(8,128)(2,1)S(1)}, bf16[256,288]{1,0:T(8,128)(2,1)S(1)}, u32[]{:S(2)}, u32[]{:S(2)}) collective-permute-start(bf16[256,288]{1,0:T(8,128)(2,1)S(1)} %project_low.2), channel_id=1, source_target_pairs={{0,1},{1,0},{2,3},{3,2},{4,5},{5,4},{6,7},{7,6},{8,9},{9,8},{10,11... | collective-permute-start | bytes 442376 | tf_op jit(solution)/shard_map/ppermute | solution.py:538
  14.2 11.3 %collective-permute-start.5 = (bf16[256,512]{1,0:T(8,128)(2,1)S(1)}, bf16[256,512]{1,0:T(8,128)(2,1)S(1)}, u32[]{:S(2)}, u32[]{:S(2)}) collective-permute-start(bf16[256,512]{1,0:T(8,128)(2,1)S(1)} %collective-permute-done.4.refs_0_), channel_id=1, source_target_pairs={{0,2},{1,3},{2,4},{3,5},{4,6},{5,7},{6,0},{7,1},{8,10},{9,11},{10,... | collective-permute-start | bytes 786440 | tf_op jit(solution)/shard_map/ppermute | solution.py:538
  14.2 12.5 %collective-permute-start.9 = (bf16[256,512]{1,0:T(8,128)(2,1)S(1)}, bf16[256,512]{1,0:T(8,128)(2,1)S(1)}, u32[]{:S(2)}, u32[]{:S(2)}) collective-permute-start(bf16[256,512]{1,0:T(8,128)(2,1)S(1)} %collective-permute-done.4.refs_0_), channel_id=1, source_target_pairs={{0,1},{1,0},{2,3},{3,2},{4,5},{5,4},{6,7},{7,6},{8,9},{9,8},{10,11... | collective-permute-start | bytes 786440 | tf_op jit(solution)/shard_map/ppermute | solution.py:538
  19.3 13.3 %collective-permute-start.8 = (bf16[256,512]{1,0:T(8,128)(2,1)S(1)}, bf16[256,512]{1,0:T(8,128)(2,1)S(1)}, u32[]{:S(2)}, u32[]{:S(2)}) collective-permute-start(bf16[256,512]{1,0:T(8,128)(2,1)S(1)} %collective-permute-done.7.refs_0_), channel_id=1, source_target_pairs={{0,1},{1,0},{2,3},{3,2},{4,5},{5,4},{6,7},{7,6},{8,9},{9,8},{10,11... | collective-permute-start | bytes 786440 | tf_op jit(solution)/shard_map/ppermute | solution.py:538
  21.2 9.3 %collective-permute-start.2 = (bf16[256,288]{1,0:T(8,128)(2,1)S(1)}, bf16[256,288]{1,0:T(8,128)(2,1)S(1)}, u32[]{:S(2)}, u32[]{:S(2)}) collective-permute-start(bf16[256,288]{1,0:T(8,128)(2,1)S(1)} %add_convert_fusion.3.refs_7_), channel_id=1, source_target_pairs={{0,2},{1,3},{2,0},{3,1},{4,6},{5,7},{6,4},{7,5},{8,10},{9,11},{10,... | collective-permute-start | bytes 442376 | tf_op jit(solution)/shard_map/ppermute | solution.py:542
  25.6 10.9 %collective-permute-start.6 = (bf16[256,512]{1,0:T(8,128)(2,1)S(1)}, bf16[256,512]{1,0:T(8,128)(2,1)S(1)}, u32[]{:S(2)}, u32[]{:S(2)}) collective-permute-start(bf16[256,512]{1,0:T(8,128)(2,1)S(1)} %relay.2), channel_id=1, source_target_pairs={{0,1},{1,0},{2,3},{3,2},{4,5},{5,4},{6,7},{7,6},{8,9},{9,8},{10,11... | collective-permute-start | bytes 786440 | tf_op jit(solution)/shard_map/ppermute | solution.py:538
  30.6 9.7 %collective-permute-start.3 = (bf16[256,288]{1,0:T(8,128)(2,1)S(1)}, bf16[256,288]{1,0:T(8,128)(2,1)S(1)}, u32[]{:S(2)}, u32[]{:S(2)}) collective-permute-start(bf16[256,288]{1,0:T(8,128)(2,1)S(1)} %add_convert_fusion.2.refs_7_.own_ref), channel_id=1, source_target_pairs={{0,4},{1,5},{2,6},{3,7},{4,0},{5,1},{6,2},{7,3},{8,12},{9,13},{10,... | collective-permute-start | bytes 442376 | tf_op jit(solution)/shard_map/ppermute | solution.py:542
  62.3 9.2 %collective-permute-start.12 = (bf16[256,512]{1,0:T(8,128)(2,1)S(1)}, bf16[256,512]{1,0:T(8,128)(2,1)S(1)}, u32[]{:S(2)}, u32[]{:S(2)}) collective-permute-start(bf16[256,512]{1,0:T(8,128)(2,1)S(1)} %get-tuple-element.89), channel_id=1, source_target_pairs={{0,1},{1,0},{2,3},{3,2},{4,5},{5,4},{6,7},{7,6},{8,9},{9,8},{10,11... | collective-permute-start | bytes 786440 | tf_op jit(solution)/shard_map/ppermute | solution.py:538
  66.4 12.5 %collective-permute-start.15 = (bf16[256,512]{1,0:T(8,128)(2,1)S(1)}, bf16[256,512]{1,0:T(8,128)(2,1)S(1)}, u32[]{:S(2)}, u32[]{:S(2)}) collective-permute-start(bf16[256,512]{1,0:T(8,128)(2,1)S(1)} %get-tuple-element.92), channel_id=1, source_target_pairs={{0,1},{1,0},{2,3},{3,2},{4,5},{5,4},{6,7},{7,6},{8,9},{9,8},{10,11... | collective-permute-start | bytes 786440 | tf_op jit(solution)/shard_map/ppermute | solution.py:538
  68.0 14.7 %collective-permute-start.11 = (bf16[256,512]{1,0:T(8,128)(2,1)S(1)}, bf16[256,512]{1,0:T(8,128)(2,1)S(1)}, u32[]{:S(2)}, u32[]{:S(2)}) collective-permute-start(bf16[256,512]{1,0:T(8,128)(2,1)S(1)} %get-tuple-element.87), channel_id=1, source_target_pairs={{0,1},{1,0},{2,3},{3,2},{4,5},{5,4},{6,7},{7,6},{8,9},{9,8},{10,11... | collective-permute-start | bytes 786440 | tf_op jit(solution)/shard_map/ppermute | solution.py:538
  71.6 11.2 %collective-permute-start.13 = (bf16[256,512]{1,0:T(8,128)(2,1)S(1)}, bf16[256,512]{1,0:T(8,128)(2,1)S(1)}, u32[]{:S(2)}, u32[]{:S(2)}) collective-permute-start(bf16[256,512]{1,0:T(8,128)(2,1)S(1)} %combine.8.refs_0_), channel_id=1, source_target_pairs={{0,2},{1,3},{2,4},{3,5},{4,6},{5,7},{6,0},{7,1},{8,10},{9,11},{10,... | collective-permute-start | bytes 786440 | tf_op jit(solution)/shard_map/ppermute | solution.py:538
  75.1 14.3 %collective-permute-start.10 = (bf16[256,512]{1,0:T(8,128)(2,1)S(1)}, bf16[256,512]{1,0:T(8,128)(2,1)S(1)}, u32[]{:S(2)}, u32[]{:S(2)}) collective-permute-start(bf16[256,512]{1,0:T(8,128)(2,1)S(1)} %get-tuple-element.85), channel_id=1, source_target_pairs={{0,1},{1,0},{2,3},{3,2},{4,5},{5,4},{6,7},{7,6},{8,9},{9,8},{10,11... | collective-permute-start | bytes 786440 | tf_op jit(solution)/shard_map/ppermute | solution.py:538
  79.0 10.4 %collective-permute-start.16 = (bf16[256,512]{1,0:T(8,128)(2,1)S(1)}, bf16[256,512]{1,0:T(8,128)(2,1)S(1)}, u32[]{:S(2)}, u32[]{:S(2)}) collective-permute-start(bf16[256,512]{1,0:T(8,128)(2,1)S(1)} %combine.10.refs_0_), channel_id=1, source_target_pairs={{0,6},{1,7},{2,0},{3,1},{4,2},{5,3},{6,4},{7,5},{8,14},{9,15},{10,... | collective-permute-start | bytes 786440 | tf_op jit(solution)/shard_map/ppermute | solution.py:538
  82.8 9.9 %collective-permute-start.14 = (bf16[256,512]{1,0:T(8,128)(2,1)S(1)}, bf16[256,512]{1,0:T(8,128)(2,1)S(1)}, u32[]{:S(2)}, u32[]{:S(2)}) collective-permute-start(bf16[256,512]{1,0:T(8,128)(2,1)S(1)} %combine.9), channel_id=1, source_target_pairs={{0,2},{1,3},{2,4},{3,5},{4,6},{5,7},{6,0},{7,1},{8,10},{9,11},{10,... | collective-permute-start | bytes 786440 | tf_op jit(solution)/shard_map/ppermute | solution.py:538
  93.8 18.3 %collective-permute-start.17 = (bf16[256,800]{1,0:T(8,128)(2,1)S(1)}, bf16[256,800]{1,0:T(8,128)(2,1)S(1)}, u32[]{:S(2)}, u32[]{:S(2)}) collective-permute-start(bf16[256,800]{1,0:T(8,128)(2,1)S(1)} %project_low.3), channel_id=1, source_target_pairs={{0,1},{1,0},{2,3},{3,2},{4,5},{5,4},{6,7},{7,6},{8,9},{9,8},{10,11... | collective-permute-start | bytes 1228808 | tf_op jit(solution)/shard_map/ppermute | solution.py:538
  95.5 11.1 %collective-permute-start.20 = (bf16[256,512]{1,0:T(8,128)(2,1)S(1)}, bf16[256,512]{1,0:T(8,128)(2,1)S(1)}, u32[]{:S(2)}, u32[]{:S(2)}) collective-permute-start(bf16[256,512]{1,0:T(8,128)(2,1)S(1)} %combine.11.rows_ref.refs_0_), channel_id=1, source_target_pairs={{0,2},{1,3},{2,4},{3,5},{4,6},{5,7},{6,0},{7,1},{8,10},{9,11},{10,... | collective-permute-start | bytes 786440 | tf_op jit(solution)/shard_map/ppermute | solution.py:538
  97.2 14.8 %collective-permute-start.23 = (bf16[256,512]{1,0:T(8,128)(2,1)S(1)}, bf16[256,512]{1,0:T(8,128)(2,1)S(1)}, u32[]{:S(2)}, u32[]{:S(2)}) collective-permute-start(bf16[256,512]{1,0:T(8,128)(2,1)S(1)} %combine.11.rows_ref.refs_0_), channel_id=1, source_target_pairs={{0,6},{1,7},{2,0},{3,1},{4,2},{5,3},{6,4},{7,5},{8,14},{9,15},{10,... | collective-permute-start | bytes 786440 | tf_op jit(solution)/shard_map/ppermute | solution.py:538
  106.5 14.2 %collective-permute-start.21 = (bf16[256,512]{1,0:T(8,128)(2,1)S(1)}, bf16[256,512]{1,0:T(8,128)(2,1)S(1)}, u32[]{:S(2)}, u32[]{:S(2)}) collective-permute-start(bf16[256,512]{1,0:T(8,128)(2,1)S(1)} %collective-permute-done.20.refs_0_), channel_id=1, source_target_pairs={{0,2},{1,3},{2,4},{3,5},{4,6},{5,7},{6,0},{7,1},{8,10},{9,11},{10,... | collective-permute-start | bytes 786440 | tf_op jit(solution)/shard_map/ppermute | solution.py:538
  108.5 13.6 %collective-permute-start.25 = (bf16[256,512]{1,0:T(8,128)(2,1)S(1)}, bf16[256,512]{1,0:T(8,128)(2,1)S(1)}, u32[]{:S(2)}, u32[]{:S(2)}) collective-permute-start(bf16[256,512]{1,0:T(8,128)(2,1)S(1)} %collective-permute-done.20.refs_0_), channel_id=1, source_target_pairs={{0,1},{1,0},{2,3},{3,2},{4,5},{5,4},{6,7},{7,6},{8,9},{9,8},{10,11... | collective-permute-start | bytes 786440 | tf_op jit(solution)/shard_map/ppermute | solution.py:538
  112.1 11.8 %collective-permute-start.24 = (bf16[256,512]{1,0:T(8,128)(2,1)S(1)}, bf16[256,512]{1,0:T(8,128)(2,1)S(1)}, u32[]{:S(2)}, u32[]{:S(2)}) collective-permute-start(bf16[256,512]{1,0:T(8,128)(2,1)S(1)} %collective-permute-done.23.refs_0_), channel_id=1, source_target_pairs={{0,1},{1,0},{2,3},{3,2},{4,5},{5,4},{6,7},{7,6},{8,9},{9,8},{10,11... | collective-permute-start | bytes 786440 | tf_op jit(solution)/shard_map/ppermute | solution.py:538
  112.1 8.3 %collective-permute-start.18 = (bf16[256,288]{1,0:T(8,128)(2,1)S(1)}, bf16[256,288]{1,0:T(8,128)(2,1)S(1)}, u32[]{:S(2)}, u32[]{:S(2)}) collective-permute-start(bf16[256,288]{1,0:T(8,128)(2,1)S(1)} %add_convert_fusion.1.refs_7_), channel_id=1, source_target_pairs={{0,2},{1,3},{2,0},{3,1},{4,6},{5,7},{6,4},{7,5},{8,10},{9,11},{10,... | collective-permute-start | bytes 442376 | tf_op jit(solution)/shard_map/ppermute | solution.py:542
  120.5 10.5 %collective-permute-start.19 = (bf16[256,288]{1,0:T(8,128)(2,1)S(1)}, bf16[256,288]{1,0:T(8,128)(2,1)S(1)}, u32[]{:S(2)}, u32[]{:S(2)}) collective-permute-start(bf16[256,288]{1,0:T(8,128)(2,1)S(1)} %add_convert_fusion.refs_1_.refs_7_.own_ref), channel_id=1, source_target_pairs={{0,4},{1,5},{2,6},{3,7},{4,0},{5,1},{6,2},{7,3},{8,12},{9,13},{10,... | collective-permute-start | bytes 442376 | tf_op jit(solution)/shard_map/ppermute | solution.py:542
  152.8 9.2 %collective-permute-start.28 = (bf16[256,512]{1,0:T(8,128)(2,1)S(1)}, bf16[256,512]{1,0:T(8,128)(2,1)S(1)}, u32[]{:S(2)}, u32[]{:S(2)}) collective-permute-start(bf16[256,512]{1,0:T(8,128)(2,1)S(1)} %get-tuple-element.122), channel_id=1, source_target_pairs={{0,1},{1,0},{2,3},{3,2},{4,5},{5,4},{6,7},{7,6},{8,9},{9,8},{10,11... | collective-permute-start | bytes 786440 | tf_op jit(solution)/shard_map/ppermute | solution.py:538
  157.6 10.0 %collective-permute-start.31 = (bf16[256,512]{1,0:T(8,128)(2,1)S(1)}, bf16[256,512]{1,0:T(8,128)(2,1)S(1)}, u32[]{:S(2)}, u32[]{:S(2)}) collective-permute-start(bf16[256,512]{1,0:T(8,128)(2,1)S(1)} %get-tuple-element.124), channel_id=1, source_target_pairs={{0,1},{1,0},{2,3},{3,2},{4,5},{5,4},{6,7},{7,6},{8,9},{9,8},{10,11... | collective-permute-start | bytes 786440 | tf_op jit(solution)/shard_map/ppermute | solution.py:538
  158.5 14.7 %collective-permute-start.27 = (bf16[256,512]{1,0:T(8,128)(2,1)S(1)}, bf16[256,512]{1,0:T(8,128)(2,1)S(1)}, u32[]{:S(2)}, u32[]{:S(2)}) collective-permute-start(bf16[256,512]{1,0:T(8,128)(2,1)S(1)} %get-tuple-element.120), channel_id=1, source_target_pairs={{0,1},{1,0},{2,3},{3,2},{4,5},{5,4},{6,7},{7,6},{8,9},{9,8},{10,11... | collective-permute-start | bytes 786440 | tf_op jit(solution)/shard_map/ppermute | solution.py:538
  162.1 11.2 %collective-permute-start.29 = (bf16[256,512]{1,0:T(8,128)(2,1)S(1)}, bf16[256,512]{1,0:T(8,128)(2,1)S(1)}, u32[]{:S(2)}, u32[]{:S(2)}) collective-permute-start(bf16[256,512]{1,0:T(8,128)(2,1)S(1)} %combine.12), channel_id=1, source_target_pairs={{0,2},{1,3},{2,4},{3,5},{4,6},{5,7},{6,0},{7,1},{8,10},{9,11},{10,... | collective-permute-start | bytes 786440 | tf_op jit(solution)/shard_map/ppermute | solution.py:538
  165.3 13.0 %collective-permute-start.26 = (bf16[256,512]{1,0:T(8,128)(2,1)S(1)}, bf16[256,512]{1,0:T(8,128)(2,1)S(1)}, u32[]{:S(2)}, u32[]{:S(2)}) collective-permute-start(bf16[256,512]{1,0:T(8,128)(2,1)S(1)} %get-tuple-element.118), channel_id=1, source_target_pairs={{0,1},{1,0},{2,3},{3,2},{4,5},{5,4},{6,7},{7,6},{8,9},{9,8},{10,11... | collective-permute-start | bytes 786440 | tf_op jit(solution)/shard_map/ppermute | solution.py:538
  167.7 10.6 %collective-permute-start.32 = (bf16[256,512]{1,0:T(8,128)(2,1)S(1)}, bf16[256,512]{1,0:T(8,128)(2,1)S(1)}, u32[]{:S(2)}, u32[]{:S(2)}) collective-permute-start(bf16[256,512]{1,0:T(8,128)(2,1)S(1)} %combine.14), channel_id=1, source_target_pairs={{0,6},{1,7},{2,0},{3,1},{4,2},{5,3},{6,4},{7,5},{8,14},{9,15},{10,... | collective-permute-start | bytes 786440 | tf_op jit(solution)/shard_map/ppermute | solution.py:538
  173.4 9.0 %collective-permute-start.30 = (bf16[256,512]{1,0:T(8,128)(2,1)S(1)}, bf16[256,512]{1,0:T(8,128)(2,1)S(1)}, u32[]{:S(2)}, u32[]{:S(2)}) collective-permute-start(bf16[256,512]{1,0:T(8,128)(2,1)S(1)} %combine.13), channel_id=1, source_target_pairs={{0,2},{1,3},{2,4},{3,5},{4,6},{5,7},{6,0},{7,1},{8,10},{9,11},{10,... | collective-permute-start | bytes 786440 | tf_op jit(solution)/shard_map/ppermute | solution.py:538
  (11 other events, 77.6 us)
where the time goes:
time: 183 us
  Pallas kernels  85.6 us (47%)
  waiting for transfers between devices  41.2 us (23%)
  starting transfers between devices  40.5 us (22%)
  blocking collectives  10.9 us (6%)
  local copies, waits for them, and re-layouts  4.23 us (2%)
    ppermute x29, waiting for transfers between devices, send(): return lax.ppermute(value, 'tp', pairs)  35.4 us
    ppermute x29, starting transfers between devices, send(): return lax.ppermute(value, 'tp', pairs)  33.4 us
    pallas_call x2, Pallas kernels, local_scan(): pl.pallas_call(functools.partial(scan_kernel, layer, states, width), out_...  17.5 us
    pallas_call x5, Pallas kernels, unpack(): pl.pallas_call(functools.partial(unpack_kernel, count, layer, table_at, w...  15.8 us
    pallas_call x2, Pallas kernels, close_layer(): pl.pallas_call(functools.partial(close_kernel, layer, states, table_at, f...  15.2 us
    pallas_call x4, Pallas kernels, expand(): pl.pallas_call(functools.partial(expand_kernel, layer, table_at, feat), o...  13.3 us
    pallas_call x3, Pallas kernels, project(): pl.pallas_call(functools.partial(proj_kernel, count, before is None, laye...  11.3 us
    all_gather x2, blocking collectives, per_device(): finals = lax.all_gather(final, 'seq')  10.9 us
  transfers between devices with their start and end apart: 33, of which 17 were waited for; matrix products, arithmetic and copies ran while one was open for 0% of the time, Pallas kernels for 28%

commit v1 on v0

--- a/solution.py
+++ b/solution.py
@@ -638,7 +638,7 @@
             beside = {0: cross(own_rows)}
             low = project_low(layer, table, own_rows, norm_gain, low_t, 0, beside[0])
             lows = [low, *cross(low)]
-            weights[0], _ = unpack(layer, table, 0, grid.side, feat, chans, w_raw, [])
+            weights[0], _ = unpack(layer, table, 0, grid.side, feat, chans, w_raw, [rates])
         pairs = sum_selectors(grid, lows)
         stages = [own for own, _ in pairs]
         state = None
@@ -647,7 +647,7 @@
                 last = n + 1 == len(arrivals)
                 beside[a] = cross(relay(columns[a], *first) if last else columns[a])
             arrived = [columns[a], *beside[a]]
-            place, earlier = a * grid.side, stages[n - 1 : n] if n else []
+            place, earlier = a * grid.side, stages[n - 1 + packed : n + packed] if n else []
             if a in weights:
                 state = project_ready(
                     layer, arrived, table, place, norm_gain, weights[a], state, earlier
@@ -657,7 +657,7 @@
                     layer, arrived, table, place, norm_gain, w_raw, chans, state, earlier
                 )
             if n == 0:
-                first = [state[2], *stages[1:2]] if packed else [state[2]]
+                first = [state[2]]
         cur, gate, square = state
         low, selectors = finish_low(rank, *pairs[-1], [square])
         out, time, final = local_scan(

time: 183 us -> 184 us (level)
    unnamed x21 -> x19, local copies, waits for them, and re-layouts: 4.23 us -> 4.23 us
  transfers between devices with their start and end apart: 33 -> 33, of which waited for: 17 -> 18; matrix products, arithmetic and copies ran while one was open for 0% -> 1% of each run, Pallas kernels for 28% -> 28%
where the time goes in v1:
time: 184 us
  Pallas kernels  85.6 us (47%)
  waiting for transfers between devices  41.8 us (23%)
  starting transfers between devices  39.7 us (22%)
  blocking collectives  10.9 us (6%)
  local copies, waits for them, and re-layouts  4.23 us (2%)
    ppermute x29, waiting for transfers between devices, send(): return lax.ppermute(value, 'tp', pairs)  37.1 us
    ppermute x29, starting transfers between devices, send(): return lax.ppermute(value, 'tp', pairs)  33.2 us
    pallas_call x2, Pallas kernels, local_scan(): pl.pallas_call(functools.partial(scan_kernel, layer, states, width), out_...  17.5 us
    pallas_call x5, Pallas kernels, unpack(): pl.pallas_call(functools.partial(unpack_kernel, count, layer, table_at, w...  15.8 us
    pallas_call x2, Pallas kernels, close_layer(): pl.pallas_call(functools.partial(close_kernel, layer, states, table_at, f...  15.2 us
    pallas_call x4, Pallas kernels, expand(): pl.pallas_call(functools.partial(expand_kernel, layer, table_at, feat), o...  13.3 us
    pallas_call x3, Pallas kernels, project(): pl.pallas_call(functools.partial(proj_kernel, count, before is None, laye...  11.3 us
    all_gather x2, blocking collectives, per_device(): finals = lax.all_gather(final, 'seq')  10.9 us
  transfers between devices with their start and end apart: 33, of which 18 were waited for; matrix products, arithmetic and copies ran while one was open for 1% of the time, Pallas kernels for 28%

profile of v1, /device:TPU:0, one launch (start us, length us, event | category | flops | bytes accessed | tf_op | source)
XLA Modules:
  0.0 183.9 jit_solution(10604771970273526855)
XLA Ops:
  0.0 3.0 %collective-permute-start = (bf16[256,512]{1,0:T(8,128)(2,1)}, bf16[256,512]{1,0:T(8,128)(2,1)S(1)}, u32[]{:S(2)}, u32[]{:S(2)}) collective-permute-start(bf16[256,512]{1,0:T(8,128)(2,1)} %refs_0_.3), channel_id=1, source_target_pairs={{0,1},{1,0},{2,3},{3,2},{4,5},{5,4},{6,7},{7,6},{8,9},{9,8},{10,11... | collective-permute-start | bytes 786440 | tf_op jit(solution)/shard_map/ppermute | solution.py:538
  7.9 3.3 %unpack.5 = (bf16[2,1024,1024]{2,1,0:T(8,128)(2,1)S(1)}, f32[8,128]{1,0:T(8,128)}) custom-call(s32[16]{0:T(128)S(1)} %pad_add_fusion.table_ref, bf16[2,65536,128]{2,1,0:T(8,128)(2,1)} %bitcast.22, f32[2,16,8,128]{3,2,1,0:T(8,128)S(1)} %bitcast.13), custom_call_target="tpu_custom_call" | custom-call | flops 1 | bytes 1 | tf_op jit(solution)/shard_map/unpack/pallas_call | solution.py:175
  22.1 2.5 %collective-permute-start.2 = (bf16[256,288]{1,0:T(8,128)(2,1)S(1)}, bf16[256,288]{1,0:T(8,128)(2,1)S(1)}, u32[]{:S(2)}, u32[]{:S(2)}) collective-permute-start(bf16[256,288]{1,0:T(8,128)(2,1)S(1)} %add_convert_fusion.3.refs_7_), channel_id=1, source_target_pairs={{0,2},{1,3},{2,0},{3,1},{4,6},{5,7},{6,4},{7,5},{8,10},{9,11},{10,... | collective-permute-start | bytes 442376 | tf_op jit(solution)/shard_map/ppermute | solution.py:542
  27.6 3.8 %project.3 = (f32[256,1024]{1,0:T(8,128)S(1)}, f32[256,1024]{1,0:T(8,128)S(1)}, f32[256,1]{1,0:T(8,128)S(1)}) custom-call(s32[16]{0:T(128)S(1)} %pad_add_fusion.table_ref, bf16[256,512]{1,0:T(8,128)(2,1)S(1)} %collective-permute-done.4.refs_0_, ...), custom_call_target="tpu_custom_call", output_to_operand_aliasing={{0}: (5, {}), {1}: (6, {}), {2}: (7, {})} | custom-call | flops 10000000000 | bytes 1 | tf_op jit(solution)/shard_map/project/pallas_call | solution.py:118
  33.2 3.8 %project.4 = (f32[256,1024]{1,0:T(8,128)S(1)}, f32[256,1024]{1,0:T(8,128)S(1)}, f32[256,1]{1,0:T(8,128)S(1)}) custom-call(s32[16]{0:T(128)S(1)} %pad_add_fusion.table_ref, bf16[256,512]{1,0:T(8,128)(2,1)S(1)} %collective-permute-done.7.refs_0_, ...), custom_call_target="tpu_custom_call", output_to_operand_aliasing={{0}: (5, {}), {1}: (6, {}), {2}: (7, {})} | custom-call | flops 10000000000 | bytes 1 | tf_op jit(solution)/shard_map/project/pallas_call | solution.py:118
  37.1 3.8 %project.5 = (f32[256,1024]{1,0:T(8,128)S(1)}, f32[256,1024]{1,0:T(8,128)S(1)}, f32[256,1]{1,0:T(8,128)S(1)}) custom-call(s32[16]{0:T(128)S(1)} %pad_add_fusion.table_ref, bf16[256,512]{1,0:T(8,128)(2,1)S(1)} %collective-permute-done.5.value_ref.refs_0_, ...), custom_call_target="tpu_custom_call", output_to_operand_aliasing={{0}: (5, {}), {1}: (6, {}), {2}: (7, {})} | custom-call | flops 10000000000 | bytes 1 | tf_op jit(solution)/shard_map/project/pallas_call | solution.py:118
  41.0 8.8 %local_scan.2 = (f32[6152,128]{1,0:T(8,128)S(1)}, f32[6152,128]{1,0:T(8,128)S(1)}, bf16[17,8,128]{2,1,0:T(8,128)(2,1)S(1)}) custom-call(f32[256,32]{1,0:T(8,128)S(1)} %get-tuple-element.76.sel_ref, f32[256,288]{1,0:T(8,128)S(1)} %get-tuple-element.77.low_ref, f32[256,1]{1,0:T(8,128)S(1)} %get-tuple-element.75.refs_0_.square_ref.refs_4_, ...), custom_call_target="tpu_custom_call" | custom-call | flops 1 | bytes 1 | tf_op jit(solution)/shard_map/local_scan/pallas_call | solution.py:352
  49.7 5.4 %all-gather = bf16[68,8,128]{2,1,0:T(8,128)(2,1)S(1)} all-gather(bf16[17,8,128]{2,1,0:T(8,128)(2,1)S(1)} %get-tuple-element.82), channel_id=2, replica_groups=mesh['seq'=4,'tp'=8] {'seq'}, dimensions={0}, use_global_device_ids=true | all-gather | bytes 174080 | tf_op jit(solution)/shard_map/all_gather | solution.py:666
  55.2 7.7 %close_layer.2 = (bf16[256,1024]{1,0:T(8,128)(2,1)S(1)}, bf16[256,512]{1,0:T(8,128)(2,1)S(1)}) custom-call(s32[16]{0:T(128)S(1)} %pad_add_fusion.table_ref, s32[1]{0:T(128)} %bitcast.place_ref, f32[256,32]{1,0:T(8,128)S(1)} %get-tuple-element.76.sel_ref, f32[6152,128]{1,0:T(8,128)S(1)} %get-tuple-element.79.refs_0_, ...), custom_call_target="tpu_custom_call" | custom-call | flops 1 | bytes 1 | tf_op jit(solution)/shard_map/close_layer/pallas_call | solution.py:442
  63.5 3.6 %expand.5 = (bf16[256,512]{1,0:T(8,128)(2,1)S(1)}, bf16[256,512]{1,0:T(8,128)(2,1)S(1)}, bf16[256,512]{1,0:T(8,128)(2,1)S(1)}, bf16[256,512]{1,0:T(8,128)(2,1)S(1)}) custom-call(s32[16]{0:T(128)S(1)} %pad_add_fusion.table_ref, bf16[256,1024]{1,0:T(8,128)(2,1)S(1)} %get-tuple-element.83.gated_ref, bf16[2,1024,4096]{2,1,0:T(8,128)(2,1)} %w_ref.7), custom_call_target="tpu_custom_call" | custom-call | flops 1 | bytes 1 | tf_op jit(solution)/shard_map/expand/pallas_call | solution.py:468
  69.2 2.9 %collective-permute-done.12.refs_1_ = bf16[256,512]{1,0:T(8,128)(2,1)S(1)} collective-permute-done((bf16[256,512]{1,0:T(8,128)(2,1)S(1)}, bf16[256,512]{1,0:T(8,128)(2,1)S(1)}, u32[]{:S(2)}, u32[]{:S(2)}) %collective-permute-start.12) | collective-permute-done | bytes 262176 | tf_op jit(solution)/shard_map/ppermute | solution.py:538
  72.9 3.1 %expand.4 = (bf16[256,512]{1,0:T(8,128)(2,1)S(1)}, bf16[256,512]{1,0:T(8,128)(2,1)S(1)}, bf16[256,512]{1,0:T(8,128)(2,1)S(1)}) custom-call(s32[16]{0:T(128)S(1)} %pad_add_fusion.table_ref, bf16[256,1024]{1,0:T(8,128)(2,1)S(1)} %get-tuple-element.83.gated_ref, bf16[2,1024,4096]{2,1,0:T(8,128)(2,1)} %w_ref.7), custom_call_target="tpu_custom_call" | custom-call | flops 1 | bytes 1 | tf_op jit(solution)/shard_map/expand/pallas_call | solution.py:468
  76.4 3.0 %unpack.6 = (bf16[2,1024,1024]{2,1,0:T(8,128)(2,1)S(1)}, f32[8,128]{1,0:T(8,128)S(1)}) custom-call(s32[16]{0:T(128)S(1)} %pad_add_fusion.table_ref, bf16[2,65536,128]{2,1,0:T(8,128)(2,1)} %bitcast.26, bf16[256,512]{1,0:T(8,128)(2,1)S(1)} %combine.8.refs_0_), custom_call_target="tpu_custom_call" | custom-call | flops 1 | bytes 1 | tf_op jit(solution)/shard_map/unpack/pallas_call | solution.py:175
  79.6 3.4 %collective-permute-start.16 = (bf16[256,512]{1,0:T(8,128)(2,1)S(1)}, bf16[256,512]{1,0:T(8,128)(2,1)S(1)}, u32[]{:S(2)}, u32[]{:S(2)}) collective-permute-start(bf16[256,512]{1,0:T(8,128)(2,1)S(1)} %combine.10.refs_0_), channel_id=1, source_target_pairs={{0,6},{1,7},{2,0},{3,1},{4,2},{5,3},{6,4},{7,5},{8,14},{9,15},{10,... | collective-permute-start | bytes 786440 | tf_op jit(solution)/shard_map/ppermute | solution.py:538
  84.2 3.0 %unpack.7 = (bf16[2,1024,1024]{2,1,0:T(8,128)(2,1)S(1)}, f32[8,128]{1,0:T(8,128)S(1)}) custom-call(s32[16]{0:T(128)S(1)} %pad_add_fusion.table_ref, bf16[2,65536,128]{2,1,0:T(8,128)(2,1)} %bitcast.27, bf16[256,512]{1,0:T(8,128)(2,1)S(1)} %combine.10.refs_0_), custom_call_target="tpu_custom_call" | custom-call | flops 1 | bytes 1 | tf_op jit(solution)/shard_map/unpack/pallas_call | solution.py:175
  87.2 3.1 %unpack.8 = (bf16[2,1024,1024]{2,1,0:T(8,128)(2,1)S(1)}, f32[8,128]{1,0:T(8,128)S(1)}) custom-call(s32[16]{0:T(128)S(1)} %pad_add_fusion.table_ref, bf16[2,65536,128]{2,1,0:T(8,128)(2,1)} %bitcast.28, bf16[256,512]{1,0:T(8,128)(2,1)S(1)} %combine.10.refs_0_), custom_call_target="tpu_custom_call" | custom-call | flops 1 | bytes 1 | tf_op jit(solution)/shard_map/unpack/pallas_call | solution.py:175
  90.3 3.2 %collective-permute-done.14.refs_3_ = bf16[256,512]{1,0:T(8,128)(2,1)S(1)} collective-permute-done((bf16[256,512]{1,0:T(8,128)(2,1)S(1)}, bf16[256,512]{1,0:T(8,128)(2,1)S(1)}, u32[]{:S(2)}, u32[]{:S(2)}) %collective-permute-start.14) | collective-permute-done | bytes 262176 | tf_op jit(solution)/shard_map/ppermute | solution.py:538
  99.9 3.3 %unpack.9 = (bf16[2,1024,1024]{2,1,0:T(8,128)(2,1)S(1)}, f32[8,128]{1,0:T(8,128)}) custom-call(s32[16]{0:T(128)S(1)} %pad_add_fusion.table_ref, bf16[2,65536,128]{2,1,0:T(8,128)(2,1)} %bitcast.29, bf16[256,512]{1,0:T(8,128)(2,1)S(1)} %collective-permute-done.10.refs_2_.refs_0_), custom_call_target="tpu_custom_call" | custom-call | flops 1 | bytes 1 | tf_op jit(solution)/shard_map/unpack/pallas_call | solution.py:175
  103.2 3.9 %collective-permute-done.20.refs_0_ = bf16[256,512]{1,0:T(8,128)(2,1)S(1)} collective-permute-done((bf16[256,512]{1,0:T(8,128)(2,1)S(1)}, bf16[256,512]{1,0:T(8,128)(2,1)S(1)}, u32[]{:S(2)}, u32[]{:S(2)}) %collective-permute-start.20) | collective-permute-done | bytes 262176 | tf_op jit(solution)/shard_map/ppermute | solution.py:538
  111.9 2.3 %collective-permute-start.18 = (bf16[256,288]{1,0:T(8,128)(2,1)S(1)}, bf16[256,288]{1,0:T(8,128)(2,1)S(1)}, u32[]{:S(2)}, u32[]{:S(2)}) collective-permute-start(bf16[256,288]{1,0:T(8,128)(2,1)S(1)} %add_convert_fusion.1), channel_id=1, source_target_pairs={{0,2},{1,3},{2,0},{3,1},{4,6},{5,7},{6,4},{7,5},{8,10},{9,11},{10,... | collective-permute-start | bytes 442376 | tf_op jit(solution)/shard_map/ppermute | solution.py:542
  116.0 3.2 %collective-permute-done.21.value_ref.refs_0_ = bf16[256,512]{1,0:T(8,128)(2,1)S(1)} collective-permute-done((bf16[256,512]{1,0:T(8,128)(2,1)S(1)}, bf16[256,512]{1,0:T(8,128)(2,1)S(1)}, u32[]{:S(2)}, u32[]{:S(2)}) %collective-permute-start.21) | collective-permute-done | bytes 262176 | tf_op jit(solution)/shard_map/ppermute | solution.py:538
  128.5 3.1 %collective-permute-done.19.arrived_ref = bf16[256,288]{1,0:T(8,128)(2,1)S(1)} collective-permute-done((bf16[256,288]{1,0:T(8,128)(2,1)S(1)}, bf16[256,288]{1,0:T(8,128)(2,1)S(1)}, u32[]{:S(2)}, u32[]{:S(2)}) %collective-permute-start.19) | collective-permute-done | bytes 147488 | tf_op jit(solution)/shard_map/ppermute | solution.py:542
  131.7 8.8 %local_scan.3 = (f32[6152,128]{1,0:T(8,128)S(1)}, f32[6152,128]{1,0:T(8,128)S(1)}, bf16[17,8,128]{2,1,0:T(8,128)(2,1)S(1)}) custom-call(f32[256,32]{1,0:T(8,128)S(1)} %get-tuple-element.109.sel_ref, f32[256,288]{1,0:T(8,128)S(1)} %get-tuple-element.110.low_ref, f32[256,1]{1,0:T(8,128)S(1)} %get-tuple-element.108.refs_0_.square_ref.refs_4_, ...), custom_call_target="tpu_custom_call" | custom-call | flops 1 | bytes 1 | tf_op jit(solution)/shard_map/local_scan/pallas_call | solution.py:352
  140.5 5.4 %all-gather.1 = bf16[68,8,128]{2,1,0:T(8,128)(2,1)S(1)} all-gather(bf16[17,8,128]{2,1,0:T(8,128)(2,1)S(1)} %get-tuple-element.115), channel_id=3, replica_groups=mesh['seq'=4,'tp'=8] {'seq'}, dimensions={0}, use_global_device_ids=true | all-gather | bytes 174080 | tf_op jit(solution)/shard_map/all_gather | solution.py:666
  145.9 7.5 %close_layer.3 = (bf16[256,1024]{1,0:T(8,128)(2,1)S(1)}, bf16[256,512]{1,0:T(8,128)(2,1)S(1)}) custom-call(s32[16]{0:T(128)S(1)} %pad_add_fusion.table_ref, s32[1]{0:T(128)} %bitcast.place_ref, f32[256,32]{1,0:T(8,128)S(1)} %get-tuple-element.109.sel_ref, f32[6152,128]{1,0:T(8,128)S(1)} %get-tuple-element.112.refs_0_, ...), custom_call_target="tpu_custom_call" | custom-call | flops 1 | bytes 1 | tf_op jit(solution)/shard_map/close_layer/pallas_call | solution.py:442
  154.2 3.6 %expand.7 = (bf16[256,512]{1,0:T(8,128)(2,1)S(1)}, bf16[256,512]{1,0:T(8,128)(2,1)S(1)}, bf16[256,512]{1,0:T(8,128)(2,1)S(1)}, bf16[256,512]{1,0:T(8,128)(2,1)S(1)}) custom-call(s32[16]{0:T(128)S(1)} %pad_add_fusion.table_ref, bf16[256,1024]{1,0:T(8,128)(2,1)S(1)} %get-tuple-element.116.gated_ref, bf16[2,1024,4096]{2,1,0:T(8,128)(2,1)} %w_ref.7), custom_call_target="tpu_custom_call" | custom-call | flops 1 | bytes 1 | tf_op jit(solution)/shard_map/expand/pallas_call | solution.py:468
  159.9 2.8 %collective-permute-done.28.refs_1_ = bf16[256,512]{1,0:T(8,128)(2,1)S(1)} collective-permute-done((bf16[256,512]{1,0:T(8,128)(2,1)S(1)}, bf16[256,512]{1,0:T(8,128)(2,1)S(1)}, u32[]{:S(2)}, u32[]{:S(2)}) %collective-permute-start.28) | collective-permute-done | bytes 262176 | tf_op jit(solution)/shard_map/ppermute | solution.py:538
  162.8 3.1 %expand.6 = (bf16[256,512]{1,0:T(8,128)(2,1)S(1)}, bf16[256,512]{1,0:T(8,128)(2,1)S(1)}, bf16[256,512]{1,0:T(8,128)(2,1)S(1)}) custom-call(s32[16]{0:T(128)S(1)} %pad_add_fusion.table_ref, bf16[256,1024]{1,0:T(8,128)(2,1)S(1)} %get-tuple-element.116.gated_ref, bf16[2,1024,4096]{2,1,0:T(8,128)(2,1)} %w_ref.7), custom_call_target="tpu_custom_call" | custom-call | flops 1 | bytes 1 | tf_op jit(solution)/shard_map/expand/pallas_call | solution.py:468
  168.3 2.3 %collective-permute-start.32 = (bf16[256,512]{1,0:T(8,128)(2,1)S(1)}, bf16[256,512]{1,0:T(8,128)(2,1)S(1)}, u32[]{:S(2)}, u32[]{:S(2)}) collective-permute-start(bf16[256,512]{1,0:T(8,128)(2,1)S(1)} %combine.14), channel_id=1, source_target_pairs={{0,6},{1,7},{2,0},{3,1},{4,2},{5,3},{6,4},{7,5},{8,14},{9,15},{10,... | collective-permute-start | bytes 786440 | tf_op jit(solution)/shard_map/ppermute | solution.py:538
  170.6 3.3 %collective-permute-done.27.refs_1_ = bf16[256,512]{1,0:T(8,128)(2,1)S(1)} collective-permute-done((bf16[256,512]{1,0:T(8,128)(2,1)S(1)}, bf16[256,512]{1,0:T(8,128)(2,1)S(1)}, u32[]{:S(2)}, u32[]{:S(2)}) %collective-permute-start.27) | collective-permute-done | bytes 262176 | tf_op jit(solution)/shard_map/ppermute | solution.py:538
  174.0 4.9 %collective-permute-done.26.refs_2_ = bf16[256,512]{1,0:T(8,128)(2,1)S(1)} collective-permute-done((bf16[256,512]{1,0:T(8,128)(2,1)S(1)}, bf16[256,512]{1,0:T(8,128)(2,1)S(1)}, u32[]{:S(2)}, u32[]{:S(2)}) %collective-permute-start.26) | collective-permute-done | bytes 262176 | tf_op jit(solution)/shard_map/ppermute | solution.py:538
  178.9 4.1 %collective-permute-done.30.refs_3_ = bf16[256,512]{1,0:T(8,128)(2,1)S(1)} collective-permute-done((bf16[256,512]{1,0:T(8,128)(2,1)S(1)}, bf16[256,512]{1,0:T(8,128)(2,1)S(1)}, u32[]{:S(2)}, u32[]{:S(2)}) %collective-permute-start.30) | collective-permute-done | bytes 262176 | tf_op jit(solution)/shard_map/ppermute | solution.py:538
  (97 shorter events, 54.7 us)
Async XLA Ops:
  0.0 13.2 %collective-permute-start = (bf16[256,512]{1,0:T(8,128)(2,1)}, bf16[256,512]{1,0:T(8,128)(2,1)S(1)}, u32[]{:S(2)}, u32[]{:S(2)}) collective-permute-start(bf16[256,512]{1,0:T(8,128)(2,1)} %refs_0_.3), channel_id=1, source_target_pairs={{0,1},{1,0},{2,3},{3,2},{4,5},{5,4},{6,7},{7,6},{8,9},{9,8},{10,11... | collective-permute-start | bytes 786440 | tf_op jit(solution)/shard_map/ppermute | solution.py:538
  3.0 11.5 %collective-permute-start.4 = (bf16[256,512]{1,0:T(8,128)(2,1)}, bf16[256,512]{1,0:T(8,128)(2,1)S(1)}, u32[]{:S(2)}, u32[]{:S(2)}) collective-permute-start(bf16[256,512]{1,0:T(8,128)(2,1)} %refs_0_.3), channel_id=1, source_target_pairs={{0,2},{1,3},{2,4},{3,5},{4,6},{5,7},{6,0},{7,1},{8,10},{9,11},{10,... | collective-permute-start | bytes 786440 | tf_op jit(solution)/shard_map/ppermute | solution.py:538
  4.5 15.7 %collective-permute-start.7 = (bf16[256,512]{1,0:T(8,128)(2,1)}, bf16[256,512]{1,0:T(8,128)(2,1)S(1)}, u32[]{:S(2)}, u32[]{:S(2)}) collective-permute-start(bf16[256,512]{1,0:T(8,128)(2,1)} %refs_0_.3), channel_id=1, source_target_pairs={{0,6},{1,7},{2,0},{3,1},{4,2},{5,3},{6,4},{7,5},{8,14},{9,15},{10,... | collective-permute-start | bytes 786440 | tf_op jit(solution)/shard_map/ppermute | solution.py:538
  14.1 7.9 %collective-permute-start.1 = (bf16[256,288]{1,0:T(8,128)(2,1)S(1)}, bf16[256,288]{1,0:T(8,128)(2,1)S(1)}, u32[]{:S(2)}, u32[]{:S(2)}) collective-permute-start(bf16[256,288]{1,0:T(8,128)(2,1)S(1)} %project_low.2), channel_id=1, source_target_pairs={{0,1},{1,0},{2,3},{3,2},{4,5},{5,4},{6,7},{7,6},{8,9},{9,8},{10,11... | collective-permute-start | bytes 442376 | tf_op jit(solution)/shard_map/ppermute | solution.py:538
  14.5 10.2 %collective-permute-start.5 = (bf16[256,512]{1,0:T(8,128)(2,1)S(1)}, bf16[256,512]{1,0:T(8,128)(2,1)S(1)}, u32[]{:S(2)}, u32[]{:S(2)}) collective-permute-start(bf16[256,512]{1,0:T(8,128)(2,1)S(1)} %collective-permute-done.4.refs_0_), channel_id=1, source_target_pairs={{0,2},{1,3},{2,4},{3,5},{4,6},{5,7},{6,0},{7,1},{8,10},{9,11},{10,... | collective-permute-start | bytes 786440 | tf_op jit(solution)/shard_map/ppermute | solution.py:538
  14.5 13.2 %collective-permute-start.9 = (bf16[256,512]{1,0:T(8,128)(2,1)S(1)}, bf16[256,512]{1,0:T(8,128)(2,1)S(1)}, u32[]{:S(2)}, u32[]{:S(2)}) collective-permute-start(bf16[256,512]{1,0:T(8,128)(2,1)S(1)} %collective-permute-done.4.refs_0_), channel_id=1, source_target_pairs={{0,1},{1,0},{2,3},{3,2},{4,5},{5,4},{6,7},{7,6},{8,9},{9,8},{10,11... | collective-permute-start | bytes 786440 | tf_op jit(solution)/shard_map/ppermute | solution.py:538
  20.2 13.0 %collective-permute-start.8 = (bf16[256,512]{1,0:T(8,128)(2,1)S(1)}, bf16[256,512]{1,0:T(8,128)(2,1)S(1)}, u32[]{:S(2)}, u32[]{:S(2)}) collective-permute-start(bf16[256,512]{1,0:T(8,128)(2,1)S(1)} %collective-permute-done.7.refs_0_), channel_id=1, source_target_pairs={{0,1},{1,0},{2,3},{3,2},{4,5},{5,4},{6,7},{7,6},{8,9},{9,8},{10,11... | collective-permute-start | bytes 786440 | tf_op jit(solution)/shard_map/ppermute | solution.py:538
  22.1 9.3 %collective-permute-start.2 = (bf16[256,288]{1,0:T(8,128)(2,1)S(1)}, bf16[256,288]{1,0:T(8,128)(2,1)S(1)}, u32[]{:S(2)}, u32[]{:S(2)}) collective-permute-start(bf16[256,288]{1,0:T(8,128)(2,1)S(1)} %add_convert_fusion.3.refs_7_), channel_id=1, source_target_pairs={{0,2},{1,3},{2,0},{3,1},{4,6},{5,7},{6,4},{7,5},{8,10},{9,11},{10,... | collective-permute-start | bytes 442376 | tf_op jit(solution)/shard_map/ppermute | solution.py:542
  24.7 12.4 %collective-permute-start.6 = (bf16[256,512]{1,0:T(8,128)(2,1)S(1)}, bf16[256,512]{1,0:T(8,128)(2,1)S(1)}, u32[]{:S(2)}, u32[]{:S(2)}) collective-permute-start(bf16[256,512]{1,0:T(8,128)(2,1)S(1)} %relay.2), channel_id=1, source_target_pairs={{0,1},{1,0},{2,3},{3,2},{4,5},{5,4},{6,7},{7,6},{8,9},{9,8},{10,11... | collective-permute-start | bytes 786440 | tf_op jit(solution)/shard_map/ppermute | solution.py:538
  31.5 9.4 %collective-permute-start.3 = (bf16[256,288]{1,0:T(8,128)(2,1)S(1)}, bf16[256,288]{1,0:T(8,128)(2,1)S(1)}, u32[]{:S(2)}, u32[]{:S(2)}) collective-permute-start(bf16[256,288]{1,0:T(8,128)(2,1)S(1)} %add_convert_fusion.2.refs_7_.own_ref), channel_id=1, source_target_pairs={{0,4},{1,5},{2,6},{3,7},{4,0},{5,1},{6,2},{7,3},{8,12},{9,13},{10,... | collective-permute-start | bytes 442376 | tf_op jit(solution)/shard_map/ppermute | solution.py:542
  62.9 9.2 %collective-permute-start.12 = (bf16[256,512]{1,0:T(8,128)(2,1)S(1)}, bf16[256,512]{1,0:T(8,128)(2,1)S(1)}, u32[]{:S(2)}, u32[]{:S(2)}) collective-permute-start(bf16[256,512]{1,0:T(8,128)(2,1)S(1)} %get-tuple-element.89), channel_id=1, source_target_pairs={{0,1},{1,0},{2,3},{3,2},{4,5},{5,4},{6,7},{7,6},{8,9},{9,8},{10,11... | collective-permute-start | bytes 786440 | tf_op jit(solution)/shard_map/ppermute | solution.py:538
  67.1 12.4 %collective-permute-start.15 = (bf16[256,512]{1,0:T(8,128)(2,1)S(1)}, bf16[256,512]{1,0:T(8,128)(2,1)S(1)}, u32[]{:S(2)}, u32[]{:S(2)}) collective-permute-start(bf16[256,512]{1,0:T(8,128)(2,1)S(1)} %get-tuple-element.92), channel_id=1, source_target_pairs={{0,1},{1,0},{2,3},{3,2},{4,5},{5,4},{6,7},{7,6},{8,9},{9,8},{10,11... | collective-permute-start | bytes 786440 | tf_op jit(solution)/shard_map/ppermute | solution.py:538
  68.6 14.7 %collective-permute-start.11 = (bf16[256,512]{1,0:T(8,128)(2,1)S(1)}, bf16[256,512]{1,0:T(8,128)(2,1)S(1)}, u32[]{:S(2)}, u32[]{:S(2)}) collective-permute-start(bf16[256,512]{1,0:T(8,128)(2,1)S(1)} %get-tuple-element.87), channel_id=1, source_target_pairs={{0,1},{1,0},{2,3},{3,2},{4,5},{5,4},{6,7},{7,6},{8,9},{9,8},{10,11... | collective-permute-start | bytes 786440 | tf_op jit(solution)/shard_map/ppermute | solution.py:538
  72.1 11.2 %collective-permute-start.13 = (bf16[256,512]{1,0:T(8,128)(2,1)S(1)}, bf16[256,512]{1,0:T(8,128)(2,1)S(1)}, u32[]{:S(2)}, u32[]{:S(2)}) collective-permute-start(bf16[256,512]{1,0:T(8,128)(2,1)S(1)} %combine.8.refs_0_), channel_id=1, source_target_pairs={{0,2},{1,3},{2,4},{3,5},{4,6},{5,7},{6,0},{7,1},{8,10},{9,11},{10,... | collective-permute-start | bytes 786440 | tf_op jit(solution)/shard_map/ppermute | solution.py:538
  76.0 14.3 %collective-permute-start.10 = (bf16[256,512]{1,0:T(8,128)(2,1)S(1)}, bf16[256,512]{1,0:T(8,128)(2,1)S(1)}, u32[]{:S(2)}, u32[]{:S(2)}) collective-permute-start(bf16[256,512]{1,0:T(8,128)(2,1)S(1)} %get-tuple-element.85), channel_id=1, source_target_pairs={{0,1},{1,0},{2,3},{3,2},{4,5},{5,4},{6,7},{7,6},{8,9},{9,8},{10,11... | collective-permute-start | bytes 786440 | tf_op jit(solution)/shard_map/ppermute | solution.py:538
  79.6 10.7 %collective-permute-start.16 = (bf16[256,512]{1,0:T(8,128)(2,1)S(1)}, bf16[256,512]{1,0:T(8,128)(2,1)S(1)}, u32[]{:S(2)}, u32[]{:S(2)}) collective-permute-start(bf16[256,512]{1,0:T(8,128)(2,1)S(1)} %combine.10.refs_0_), channel_id=1, source_target_pairs={{0,6},{1,7},{2,0},{3,1},{4,2},{5,3},{6,4},{7,5},{8,14},{9,15},{10,... | collective-permute-start | bytes 786440 | tf_op jit(solution)/shard_map/ppermute | solution.py:538
  83.4 10.1 %collective-permute-start.14 = (bf16[256,512]{1,0:T(8,128)(2,1)S(1)}, bf16[256,512]{1,0:T(8,128)(2,1)S(1)}, u32[]{:S(2)}, u32[]{:S(2)}) collective-permute-start(bf16[256,512]{1,0:T(8,128)(2,1)S(1)} %combine.9), channel_id=1, source_target_pairs={{0,2},{1,3},{2,4},{3,5},{4,6},{5,7},{6,0},{7,1},{8,10},{9,11},{10,... | collective-permute-start | bytes 786440 | tf_op jit(solution)/shard_map/ppermute | solution.py:538
  94.5 17.4 %collective-permute-start.17 = (bf16[256,800]{1,0:T(8,128)(2,1)S(1)}, bf16[256,800]{1,0:T(8,128)(2,1)S(1)}, u32[]{:S(2)}, u32[]{:S(2)}) collective-permute-start(bf16[256,800]{1,0:T(8,128)(2,1)S(1)} %project_low.3), channel_id=1, source_target_pairs={{0,1},{1,0},{2,3},{3,2},{4,5},{5,4},{6,7},{7,6},{8,9},{9,8},{10,11... | collective-permute-start | bytes 1228808 | tf_op jit(solution)/shard_map/ppermute | solution.py:538
  96.0 11.1 %collective-permute-start.20 = (bf16[256,512]{1,0:T(8,128)(2,1)S(1)}, bf16[256,512]{1,0:T(8,128)(2,1)S(1)}, u32[]{:S(2)}, u32[]{:S(2)}) collective-permute-start(bf16[256,512]{1,0:T(8,128)(2,1)S(1)} %combine.11.rows_ref.refs_0_), channel_id=1, source_target_pairs={{0,2},{1,3},{2,4},{3,5},{4,6},{5,7},{6,0},{7,1},{8,10},{9,11},{10,... | collective-permute-start | bytes 786440 | tf_op jit(solution)/shard_map/ppermute | solution.py:538
  97.8 13.7 %collective-permute-start.23 = (bf16[256,512]{1,0:T(8,128)(2,1)S(1)}, bf16[256,512]{1,0:T(8,128)(2,1)S(1)}, u32[]{:S(2)}, u32[]{:S(2)}) collective-permute-start(bf16[256,512]{1,0:T(8,128)(2,1)S(1)} %combine.11.rows_ref.refs_0_), channel_id=1, source_target_pairs={{0,6},{1,7},{2,0},{3,1},{4,2},{5,3},{6,4},{7,5},{8,14},{9,15},{10,... | collective-permute-start | bytes 786440 | tf_op jit(solution)/shard_map/ppermute | solution.py:538
  107.1 12.1 %collective-permute-start.21 = (bf16[256,512]{1,0:T(8,128)(2,1)S(1)}, bf16[256,512]{1,0:T(8,128)(2,1)S(1)}, u32[]{:S(2)}, u32[]{:S(2)}) collective-permute-start(bf16[256,512]{1,0:T(8,128)(2,1)S(1)} %collective-permute-done.20.refs_0_), channel_id=1, source_target_pairs={{0,2},{1,3},{2,4},{3,5},{4,6},{5,7},{6,0},{7,1},{8,10},{9,11},{10,... | collective-permute-start | bytes 786440 | tf_op jit(solution)/shard_map/ppermute | solution.py:538
  109.1 12.8 %collective-permute-start.25 = (bf16[256,512]{1,0:T(8,128)(2,1)S(1)}, bf16[256,512]{1,0:T(8,128)(2,1)S(1)}, u32[]{:S(2)}, u32[]{:S(2)}) collective-permute-start(bf16[256,512]{1,0:T(8,128)(2,1)S(1)} %collective-permute-done.20.refs_0_), channel_id=1, source_target_pairs={{0,1},{1,0},{2,3},{3,2},{4,5},{5,4},{6,7},{7,6},{8,9},{9,8},{10,11... | collective-permute-start | bytes 786440 | tf_op jit(solution)/shard_map/ppermute | solution.py:538
  111.5 12.3 %collective-permute-start.24 = (bf16[256,512]{1,0:T(8,128)(2,1)S(1)}, bf16[256,512]{1,0:T(8,128)(2,1)S(1)}, u32[]{:S(2)}, u32[]{:S(2)}) collective-permute-start(bf16[256,512]{1,0:T(8,128)(2,1)S(1)} %collective-permute-done.23.refs_0_), channel_id=1, source_target_pairs={{0,1},{1,0},{2,3},{3,2},{4,5},{5,4},{6,7},{7,6},{8,9},{9,8},{10,11... | collective-permute-start | bytes 786440 | tf_op jit(solution)/shard_map/ppermute | solution.py:538
  111.9 9.3 %collective-permute-start.18 = (bf16[256,288]{1,0:T(8,128)(2,1)S(1)}, bf16[256,288]{1,0:T(8,128)(2,1)S(1)}, u32[]{:S(2)}, u32[]{:S(2)}) collective-permute-start(bf16[256,288]{1,0:T(8,128)(2,1)S(1)} %add_convert_fusion.1), channel_id=1, source_target_pairs={{0,2},{1,3},{2,0},{3,1},{4,6},{5,7},{6,4},{7,5},{8,10},{9,11},{10,... | collective-permute-start | bytes 442376 | tf_op jit(solution)/shard_map/ppermute | solution.py:542
  121.3 10.4 %collective-permute-start.19 = (bf16[256,288]{1,0:T(8,128)(2,1)S(1)}, bf16[256,288]{1,0:T(8,128)(2,1)S(1)}, u32[]{:S(2)}, u32[]{:S(2)}) collective-permute-start(bf16[256,288]{1,0:T(8,128)(2,1)S(1)} %add_convert_fusion.refs_7_.own_ref), channel_id=1, source_target_pairs={{0,4},{1,5},{2,6},{3,7},{4,0},{5,1},{6,2},{7,3},{8,12},{9,13},{10,... | collective-permute-start | bytes 442376 | tf_op jit(solution)/shard_map/ppermute | solution.py:542
  153.4 9.2 %collective-permute-start.28 = (bf16[256,512]{1,0:T(8,128)(2,1)S(1)}, bf16[256,512]{1,0:T(8,128)(2,1)S(1)}, u32[]{:S(2)}, u32[]{:S(2)}) collective-permute-start(bf16[256,512]{1,0:T(8,128)(2,1)S(1)} %get-tuple-element.122), channel_id=1, source_target_pairs={{0,1},{1,0},{2,3},{3,2},{4,5},{5,4},{6,7},{7,6},{8,9},{9,8},{10,11... | collective-permute-start | bytes 786440 | tf_op jit(solution)/shard_map/ppermute | solution.py:538
  157.8 10.5 %collective-permute-start.31 = (bf16[256,512]{1,0:T(8,128)(2,1)S(1)}, bf16[256,512]{1,0:T(8,128)(2,1)S(1)}, u32[]{:S(2)}, u32[]{:S(2)}) collective-permute-start(bf16[256,512]{1,0:T(8,128)(2,1)S(1)} %get-tuple-element.124), channel_id=1, source_target_pairs={{0,1},{1,0},{2,3},{3,2},{4,5},{5,4},{6,7},{7,6},{8,9},{9,8},{10,11... | collective-permute-start | bytes 786440 | tf_op jit(solution)/shard_map/ppermute | solution.py:538
  159.2 14.7 %collective-permute-start.27 = (bf16[256,512]{1,0:T(8,128)(2,1)S(1)}, bf16[256,512]{1,0:T(8,128)(2,1)S(1)}, u32[]{:S(2)}, u32[]{:S(2)}) collective-permute-start(bf16[256,512]{1,0:T(8,128)(2,1)S(1)} %get-tuple-element.120), channel_id=1, source_target_pairs={{0,1},{1,0},{2,3},{3,2},{4,5},{5,4},{6,7},{7,6},{8,9},{9,8},{10,11... | collective-permute-start | bytes 786440 | tf_op jit(solution)/shard_map/ppermute | solution.py:538
  162.7 11.2 %collective-permute-start.29 = (bf16[256,512]{1,0:T(8,128)(2,1)S(1)}, bf16[256,512]{1,0:T(8,128)(2,1)S(1)}, u32[]{:S(2)}, u32[]{:S(2)}) collective-permute-start(bf16[256,512]{1,0:T(8,128)(2,1)S(1)} %combine.12), channel_id=1, source_target_pairs={{0,2},{1,3},{2,4},{3,5},{4,6},{5,7},{6,0},{7,1},{8,10},{9,11},{10,... | collective-permute-start | bytes 786440 | tf_op jit(solution)/shard_map/ppermute | solution.py:538
  165.9 13.0 %collective-permute-start.26 = (bf16[256,512]{1,0:T(8,128)(2,1)S(1)}, bf16[256,512]{1,0:T(8,128)(2,1)S(1)}, u32[]{:S(2)}, u32[]{:S(2)}) collective-permute-start(bf16[256,512]{1,0:T(8,128)(2,1)S(1)} %get-tuple-element.118), channel_id=1, source_target_pairs={{0,1},{1,0},{2,3},{3,2},{4,5},{5,4},{6,7},{7,6},{8,9},{9,8},{10,11... | collective-permute-start | bytes 786440 | tf_op jit(solution)/shard_map/ppermute | solution.py:538
  168.3 10.6 %collective-permute-start.32 = (bf16[256,512]{1,0:T(8,128)(2,1)S(1)}, bf16[256,512]{1,0:T(8,128)(2,1)S(1)}, u32[]{:S(2)}, u32[]{:S(2)}) collective-permute-start(bf16[256,512]{1,0:T(8,128)(2,1)S(1)} %combine.14), channel_id=1, source_target_pairs={{0,6},{1,7},{2,0},{3,1},{4,2},{5,3},{6,4},{7,5},{8,14},{9,15},{10,... | collective-permute-start | bytes 786440 | tf_op jit(solution)/shard_map/ppermute | solution.py:538
  174.0 9.1 %collective-permute-start.30 = (bf16[256,512]{1,0:T(8,128)(2,1)S(1)}, bf16[256,512]{1,0:T(8,128)(2,1)S(1)}, u32[]{:S(2)}, u32[]{:S(2)}) collective-permute-start(bf16[256,512]{1,0:T(8,128)(2,1)S(1)} %combine.13), channel_id=1, source_target_pairs={{0,2},{1,3},{2,4},{3,5},{4,6},{5,7},{6,0},{7,1},{8,10},{9,11},{10,... | collective-permute-start | bytes 786440 | tf_op jit(solution)/shard_map/ppermute | solution.py:538
  (10 other events, 71.7 us)

commit v2 on v1

--- a/solution.py
+++ b/solution.py
@@ -595,13 +595,13 @@
 def sum_selectors(grid, partials):
     total = sum(partial.astype(F32) for partial in partials)
     pairs = []
-    bit = 1
+    bit = grid.depth // 2
     while True:
         rounded = total.astype(BF16)
-        arrived = grid.swap(rounded, bit) if bit < grid.depth else jnp.zeros_like(rounded)
+        arrived = grid.swap(rounded, bit) if bit else jnp.zeros_like(rounded)
         pairs.append((rounded, arrived))
-        bit *= 2
-        if bit >= grid.depth:
+        bit //= 2
+        if not bit:
             return pairs
         total = rounded.astype(F32) + arrived.astype(F32)
 
@@ -630,24 +630,28 @@
         columns = gather_columns(grid, own_rows)
         cross = lambda column: [grid.send(column, 0, b) for b in range(1, grid.side)]
         packed = layer > 0
+        state = None
         if packed:
             low = project_low(layer, table, own_rows, norm_gain, low_t, feat, [])
             beside = {0: cross(low)}
             lows = [each[:, feat:] for each in (low, *beside[0])]
         else:
             beside = {0: cross(own_rows)}
-            low = project_low(layer, table, own_rows, norm_gain, low_t, 0, beside[0])
+            state = project(layer, [own_rows], table, 0, norm_gain, w_raw, chans, None, [rates])
+            low = project_low(
+                layer, table, own_rows, norm_gain, low_t, 0, [*beside[0], state[2]]
+            )
             lows = [low, *cross(low)]
-            weights[0], _ = unpack(layer, table, 0, grid.side, feat, chans, w_raw, [rates])
         pairs = sum_selectors(grid, lows)
         stages = [own for own, _ in pairs]
-        state = None
         for n, a in enumerate(arrivals):
             if n:
                 last = n + 1 == len(arrivals)
                 beside[a] = cross(relay(columns[a], *first) if last else columns[a])
             arrived = [columns[a], *beside[a]]
-            place, earlier = a * grid.side, stages[n - 1 + packed : n + packed] if n else []
+            if not n and state is not None:
+                arrived = beside[a]
+            place, earlier = (a + 1) * grid.side - len(arrived), stages[n - 1 + packed : n + packed] if n else []
             if a in weights:
                 state = project_ready(
                     layer, arrived, table, place, norm_gain, weights[a], state, earlier

time: 184 us -> 185 us (level)
  starting transfers between devices: 39.7 us -> 48.6 us
  waiting for transfers between devices: 41.8 us -> 34.6 us
  local copies, waits for them, and re-layouts: 4.23 us -> 1.77 us
    ppermute x29, waiting for transfers between devices: 37.1 us -> 26.6 us  [send(): return lax.ppermute(value, 'tp', pairs)]
    ppermute x29, starting transfers between devices: 33.2 us -> 43.4 us  [send(): return lax.ppermute(value, 'tp', pairs)]
    pallas_call x3 -> x5, Pallas kernels: 11.3 us -> 18 us  [project(): pl.pallas_call(functools.partial(proj_kernel, count, before is None, laye...]
    pallas_call x5 -> x4, Pallas kernels: 15.8 us -> 12.5 us  [unpack(): pl.pallas_call(functools.partial(unpack_kernel, count, layer, table_at, w...]
    ppermute x4, waiting for transfers between devices: 4.64 us -> 7.94 us  [swap(): return lax.ppermute(value, 'tp', pairs)]
    unnamed x19, local copies, waits for them, and re-layouts: 4.23 us -> 1.77 us
    pallas_call x5 -> x4, Pallas kernels: 9.07 us -> 7.27 us  [project_ready(): pl.pallas_call(functools.partial(ready_kernel, count, before is None, lay...]
  transfers between devices with their start and end apart: 33 -> 33, of which waited for: 18 -> 14; matrix products, arithmetic and copies ran while one was open for 1% -> 1% of each run, Pallas kernels for 28% -> 28%
where the time goes in v2:
time: 185 us
  Pallas kernels  86.9 us (47%)
  starting transfers between devices  48.6 us (26%)
  waiting for transfers between devices  34.6 us (19%)
  blocking collectives  11.1 us (6%)
    ppermute x29, starting transfers between devices, send(): return lax.ppermute(value, 'tp', pairs)  43.4 us
    ppermute x29, waiting for transfers between devices, send(): return lax.ppermute(value, 'tp', pairs)  26.6 us
    pallas_call x5, Pallas kernels, project(): pl.pallas_call(functools.partial(proj_kernel, count, before is None, laye...  18 us
    pallas_call x2, Pallas kernels, local_scan(): pl.pallas_call(functools.partial(scan_kernel, layer, states, width), out_...  17.5 us
    pallas_call x2, Pallas kernels, close_layer(): pl.pallas_call(functools.partial(close_kernel, layer, states, table_at, f...  15 us
    pallas_call x4, Pallas kernels, expand(): pl.pallas_call(functools.partial(expand_kernel, layer, table_at, feat), o...  13.3 us
    pallas_call x4, Pallas kernels, unpack(): pl.pallas_call(functools.partial(unpack_kernel, count, layer, table_at, w...  12.5 us
    all_gather x2, blocking collectives, per_device(): finals = lax.all_gather(final, 'seq')  11.1 us
  transfers between devices with their start and end apart: 33, of which 14 were waited for; matrix products, arithmetic and copies ran while one was open for 1% of the time, Pallas kernels for 28%

profile of v2, /device:TPU:0, one launch (start us, length us, event | category | flops | bytes accessed | tf_op | source)
XLA Modules:
  0.0 184.8 jit_solution(8179476309858517504)
XLA Ops:
  0.0 3.0 %collective-permute-start = (bf16[256,512]{1,0:T(8,128)(2,1)}, bf16[256,512]{1,0:T(8,128)(2,1)S(1)}, u32[]{:S(2)}, u32[]{:S(2)}) collective-permute-start(bf16[256,512]{1,0:T(8,128)(2,1)} %refs_0_.3), channel_id=1, source_target_pairs={{0,1},{1,0},{2,3},{3,2},{4,5},{5,4},{6,7},{7,6},{8,9},{9,8},{10,11... | collective-permute-start | bytes 786440 | tf_op jit(solution)/shard_map/ppermute | solution.py:538
  4.5 2.2 %collective-permute-start.7 = (bf16[256,512]{1,0:T(8,128)(2,1)}, bf16[256,512]{1,0:T(8,128)(2,1)}, u32[]{:S(2)}, u32[]{:S(2)}) collective-permute-start(bf16[256,512]{1,0:T(8,128)(2,1)} %refs_0_.3), channel_id=1, source_target_pairs={{0,6},{1,7},{2,0},{3,1},{4,2},{5,3},{6,4},{7,5},{8,14},{9,15},{10,... | collective-permute-start | bytes 786440 | tf_op jit(solution)/shard_map/ppermute | solution.py:538
  9.6 3.0 %project.5 = (f32[256,1024]{1,0:T(8,128)S(1)}, f32[256,1024]{1,0:T(8,128)S(1)}, f32[256,1]{1,0:T(8,128)S(1)}) custom-call(s32[16]{0:T(128)S(1)} %pad_add_fusion.table_ref, bf16[256,512]{1,0:T(8,128)(2,1)S(1)} %copy-done.2, f32[2,4096]{1,0:T(2,128)S(1)} %copy-done.4, bf16[2,65536,128]{2,1,0:T(8,128)(2,1)} %bitcast.22, f32[2,16,8,128]{3,2,1,0:T(8,128)S(1)} %bitcast.13), custom_call_target="tpu_custom_call" | custom-call | flops 10000000000 | bytes 1 | tf_op jit(solution)/shard_map/project/pallas_call | solution.py:118
  15.6 2.8 %collective-permute-done.7.refs_0_ = bf16[256,512]{1,0:T(8,128)(2,1)} collective-permute-done((bf16[256,512]{1,0:T(8,128)(2,1)}, bf16[256,512]{1,0:T(8,128)(2,1)}, u32[]{:S(2)}, u32[]{:S(2)}) %collective-permute-start.7) | collective-permute-done | bytes 262176 | tf_op jit(solution)/shard_map/ppermute | solution.py:538
  18.5 2.9 %project.6 = (f32[256,1024]{1,0:T(8,128)S(1)}, f32[256,1024]{1,0:T(8,128)S(1)}, f32[256,1]{1,0:T(8,128)S(1)}) custom-call(s32[16]{0:T(128)S(1)} %pad_add_fusion.table_ref, bf16[256,512]{1,0:T(8,128)(2,1)S(1)} %collective-permute-done.refs_0_, f32[2,4096]{1,0:T(2,128)S(1)} %copy-done.5, ...), custom_call_target="tpu_custom_call", output_to_operand_aliasing={{0}: (4, {}), {1}: (5, {}), {2}: (6, {})} | custom-call | flops 10000000000 | bytes 1 | tf_op jit(solution)/shard_map/project/pallas_call | solution.py:118
  21.5 3.2 %collective-permute-start.2 = (bf16[256,288]{1,0:T(8,128)(2,1)S(1)}, bf16[256,288]{1,0:T(8,128)(2,1)S(1)}, u32[]{:S(2)}, u32[]{:S(2)}) collective-permute-start(bf16[256,288]{1,0:T(8,128)(2,1)S(1)} %add_convert_fusion.3.refs_7_), channel_id=1, source_target_pairs={{0,4},{1,5},{2,6},{3,7},{4,0},{5,1},{6,2},{7,3},{8,12},{9,13},{10,... | collective-permute-start | bytes 442376 | tf_op jit(solution)/shard_map/ppermute | solution.py:542
  27.0 4.2 %project.7 = (f32[256,1024]{1,0:T(8,128)S(1)}, f32[256,1024]{1,0:T(8,128)S(1)}, f32[256,1]{1,0:T(8,128)S(1)}) custom-call(s32[16]{0:T(128)S(1)} %pad_add_fusion.table_ref, bf16[256,512]{1,0:T(8,128)(2,1)} %collective-permute-done.4.refs_0_, ...), custom_call_target="tpu_custom_call", output_to_operand_aliasing={{0}: (5, {}), {1}: (6, {}), {2}: (7, {})} | custom-call | flops 10000000000 | bytes 1 | tf_op jit(solution)/shard_map/project/pallas_call | solution.py:118
  32.7 4.2 %project.8 = (f32[256,1024]{1,0:T(8,128)S(1)}, f32[256,1024]{1,0:T(8,128)S(1)}, f32[256,1]{1,0:T(8,128)S(1)}) custom-call(s32[16]{0:T(128)S(1)} %pad_add_fusion.table_ref, bf16[256,512]{1,0:T(8,128)(2,1)} %collective-permute-done.7.refs_0_, ...), custom_call_target="tpu_custom_call", output_to_operand_aliasing={{0}: (5, {}), {1}: (6, {}), {2}: (7, {})} | custom-call | flops 10000000000 | bytes 1 | tf_op jit(solution)/shard_map/project/pallas_call | solution.py:118
  36.9 3.8 %project.9 = (f32[256,1024]{1,0:T(8,128)S(1)}, f32[256,1024]{1,0:T(8,128)S(1)}, f32[256,1]{1,0:T(8,128)S(1)}) custom-call(s32[16]{0:T(128)S(1)} %pad_add_fusion.table_ref, bf16[256,512]{1,0:T(8,128)(2,1)S(1)} %collective-permute-done.5.value_ref.refs_0_, ...), custom_call_target="tpu_custom_call", output_to_operand_aliasing={{0}: (5, {}), {1}: (6, {}), {2}: (7, {})} | custom-call | flops 10000000000 | bytes 1 | tf_op jit(solution)/shard_map/project/pallas_call | solution.py:118
  40.8 8.8 %local_scan.2 = (f32[6152,128]{1,0:T(8,128)S(1)}, f32[6152,128]{1,0:T(8,128)S(1)}, bf16[17,8,128]{2,1,0:T(8,128)(2,1)S(1)}) custom-call(f32[256,32]{1,0:T(8,128)S(1)} %get-tuple-element.80.sel_ref, f32[256,288]{1,0:T(8,128)S(1)} %get-tuple-element.81.low_ref, f32[256,1]{1,0:T(8,128)S(1)} %get-tuple-element.79.refs_0_.square_ref.refs_4_, ...), custom_call_target="tpu_custom_call" | custom-call | flops 1 | bytes 1 | tf_op jit(solution)/shard_map/local_scan/pallas_call | solution.py:352
  49.6 5.4 %all-gather = bf16[68,8,128]{2,1,0:T(8,128)(2,1)S(1)} all-gather(bf16[17,8,128]{2,1,0:T(8,128)(2,1)S(1)} %get-tuple-element.86), channel_id=2, replica_groups=mesh['seq'=4,'tp'=8] {'seq'}, dimensions={0}, use_global_device_ids=true | all-gather | bytes 174080 | tf_op jit(solution)/shard_map/all_gather | solution.py:670
  55.0 7.5 %close_layer.2 = (bf16[256,1024]{1,0:T(8,128)(2,1)S(1)}, bf16[256,512]{1,0:T(8,128)(2,1)S(1)}) custom-call(s32[16]{0:T(128)S(1)} %pad_add_fusion.table_ref, s32[1]{0:T(128)} %bitcast.place_ref, f32[256,32]{1,0:T(8,128)S(1)} %get-tuple-element.80.sel_ref, f32[6152,128]{1,0:T(8,128)S(1)} %get-tuple-element.83.refs_0_, ...), custom_call_target="tpu_custom_call" | custom-call | flops 1 | bytes 1 | tf_op jit(solution)/shard_map/close_layer/pallas_call | solution.py:442
  64.2 3.6 %expand.5 = (bf16[256,512]{1,0:T(8,128)(2,1)S(1)}, bf16[256,512]{1,0:T(8,128)(2,1)S(1)}, bf16[256,512]{1,0:T(8,128)(2,1)S(1)}, bf16[256,512]{1,0:T(8,128)(2,1)S(1)}) custom-call(s32[16]{0:T(128)S(1)} %pad_add_fusion.table_ref, bf16[256,1024]{1,0:T(8,128)(2,1)S(1)} %get-tuple-element.87.gated_ref, bf16[2,1024,4096]{2,1,0:T(8,128)(2,1)} %w_ref.7), custom_call_target="tpu_custom_call" | custom-call | flops 1 | bytes 1 | tf_op jit(solution)/shard_map/expand/pallas_call | solution.py:468
  71.8 2.2 %collective-permute-start.13 = (bf16[256,512]{1,0:T(8,128)(2,1)S(1)}, bf16[256,512]{1,0:T(8,128)(2,1)S(1)}, u32[]{:S(2)}, u32[]{:S(2)}) collective-permute-start(bf16[256,512]{1,0:T(8,128)(2,1)S(1)} %combine.8.refs_0_), channel_id=1, source_target_pairs={{0,2},{1,3},{2,4},{3,5},{4,6},{5,7},{6,0},{7,1},{8,10},{9,11},{10,... | collective-permute-start | bytes 786440 | tf_op jit(solution)/shard_map/ppermute | solution.py:538
  74.0 3.1 %expand.4 = (bf16[256,512]{1,0:T(8,128)(2,1)S(1)}, bf16[256,512]{1,0:T(8,128)(2,1)S(1)}, bf16[256,512]{1,0:T(8,128)(2,1)S(1)}) custom-call(s32[16]{0:T(128)S(1)} %pad_add_fusion.table_ref, bf16[256,1024]{1,0:T(8,128)(2,1)S(1)} %get-tuple-element.87.gated_ref, bf16[2,1024,4096]{2,1,0:T(8,128)(2,1)} %w_ref.7), custom_call_target="tpu_custom_call" | custom-call | flops 1 | bytes 1 | tf_op jit(solution)/shard_map/expand/pallas_call | solution.py:468
  78.8 3.0 %unpack.4 = (bf16[2,1024,1024]{2,1,0:T(8,128)(2,1)S(1)}, f32[8,128]{1,0:T(8,128)S(1)}) custom-call(s32[16]{0:T(128)S(1)} %pad_add_fusion.table_ref, bf16[2,65536,128]{2,1,0:T(8,128)(2,1)} %bitcast.27, bf16[256,512]{1,0:T(8,128)(2,1)S(1)} %combine.8.refs_0_), custom_call_target="tpu_custom_call" | custom-call | flops 1 | bytes 1 | tf_op jit(solution)/shard_map/unpack/pallas_call | solution.py:175
  85.1 3.0 %unpack.5 = (bf16[2,1024,1024]{2,1,0:T(8,128)(2,1)S(1)}, f32[8,128]{1,0:T(8,128)S(1)}) custom-call(s32[16]{0:T(128)S(1)} %pad_add_fusion.table_ref, bf16[2,65536,128]{2,1,0:T(8,128)(2,1)} %bitcast.28, bf16[256,512]{1,0:T(8,128)(2,1)S(1)} %combine.10.refs_0_), custom_call_target="tpu_custom_call" | custom-call | flops 1 | bytes 1 | tf_op jit(solution)/shard_map/unpack/pallas_call | solution.py:175
  88.2 3.1 %unpack.6 = (bf16[2,1024,1024]{2,1,0:T(8,128)(2,1)S(1)}, f32[8,128]{1,0:T(8,128)S(1)}) custom-call(s32[16]{0:T(128)S(1)} %pad_add_fusion.table_ref, bf16[2,65536,128]{2,1,0:T(8,128)(2,1)} %bitcast.29, bf16[256,512]{1,0:T(8,128)(2,1)S(1)} %combine.10.refs_0_), custom_call_target="tpu_custom_call" | custom-call | flops 1 | bytes 1 | tf_op jit(solution)/shard_map/unpack/pallas_call | solution.py:175
  91.2 3.4 %collective-permute-done.14.refs_3_ = bf16[256,512]{1,0:T(8,128)(2,1)S(1)} collective-permute-done((bf16[256,512]{1,0:T(8,128)(2,1)S(1)}, bf16[256,512]{1,0:T(8,128)(2,1)S(1)}, u32[]{:S(2)}, u32[]{:S(2)}) %collective-permute-start.14) | collective-permute-done | bytes 262176 | tf_op jit(solution)/shard_map/ppermute | solution.py:538
  97.6 2.2 %collective-permute-start.23 = (bf16[256,512]{1,0:T(8,128)(2,1)S(1)}, bf16[256,512]{1,0:T(8,128)(2,1)S(1)}, u32[]{:S(2)}, u32[]{:S(2)}) collective-permute-start(bf16[256,512]{1,0:T(8,128)(2,1)S(1)} %combine.11.rows_ref.refs_0_), channel_id=1, source_target_pairs={{0,6},{1,7},{2,0},{3,1},{4,2},{5,3},{6,4},{7,5},{8,14},{9,15},{10,... | collective-permute-start | bytes 786440 | tf_op jit(solution)/shard_map/ppermute | solution.py:538
  99.8 3.3 %unpack.7 = (bf16[2,1024,1024]{2,1,0:T(8,128)(2,1)S(1)}, f32[8,128]{1,0:T(8,128)}) custom-call(s32[16]{0:T(128)S(1)} %pad_add_fusion.table_ref, bf16[2,65536,128]{2,1,0:T(8,128)(2,1)} %bitcast.30, bf16[256,512]{1,0:T(8,128)(2,1)S(1)} %collective-permute-done.10.refs_2_.refs_0_), custom_call_target="tpu_custom_call" | custom-call | flops 1 | bytes 1 | tf_op jit(solution)/shard_map/unpack/pallas_call | solution.py:175
  103.2 3.9 %collective-permute-done.20.refs_0_ = bf16[256,512]{1,0:T(8,128)(2,1)S(1)} collective-permute-done((bf16[256,512]{1,0:T(8,128)(2,1)S(1)}, bf16[256,512]{1,0:T(8,128)(2,1)S(1)}, u32[]{:S(2)}, u32[]{:S(2)}) %collective-permute-start.20) | collective-permute-done | bytes 262176 | tf_op jit(solution)/shard_map/ppermute | solution.py:538
  119.2 6.1 %collective-permute-done.18 = bf16[256,288]{1,0:T(8,128)(2,1)S(1)} collective-permute-done((bf16[256,288]{1,0:T(8,128)(2,1)S(1)}, bf16[256,288]{1,0:T(8,128)(2,1)S(1)}, u32[]{:S(2)}, u32[]{:S(2)}) %collective-permute-start.18) | collective-permute-done | bytes 147488 | tf_op jit(solution)/shard_map/ppermute | solution.py:542
  131.5 8.8 %local_scan.3 = (f32[6152,128]{1,0:T(8,128)S(1)}, f32[6152,128]{1,0:T(8,128)S(1)}, bf16[17,8,128]{2,1,0:T(8,128)(2,1)S(1)}) custom-call(f32[256,32]{1,0:T(8,128)S(1)} %get-tuple-element.113.sel_ref, f32[256,288]{1,0:T(8,128)S(1)} %get-tuple-element.114.low_ref, f32[256,1]{1,0:T(8,128)S(1)} %get-tuple-element.112.refs_0_.square_ref.refs_4_, ...), custom_call_target="tpu_custom_call" | custom-call | flops 1 | bytes 1 | tf_op jit(solution)/shard_map/local_scan/pallas_call | solution.py:352
  140.2 5.7 %all-gather.1 = bf16[68,8,128]{2,1,0:T(8,128)(2,1)S(1)} all-gather(bf16[17,8,128]{2,1,0:T(8,128)(2,1)S(1)} %get-tuple-element.119), channel_id=3, replica_groups=mesh['seq'=4,'tp'=8] {'seq'}, dimensions={0}, use_global_device_ids=true | all-gather | bytes 174080 | tf_op jit(solution)/shard_map/all_gather | solution.py:670
  145.9 7.5 %close_layer.3 = (bf16[256,1024]{1,0:T(8,128)(2,1)S(1)}, bf16[256,512]{1,0:T(8,128)(2,1)S(1)}) custom-call(s32[16]{0:T(128)S(1)} %pad_add_fusion.table_ref, s32[1]{0:T(128)} %bitcast.place_ref, f32[256,32]{1,0:T(8,128)S(1)} %get-tuple-element.113.sel_ref, f32[6152,128]{1,0:T(8,128)S(1)} %get-tuple-element.116.refs_0_, ...), custom_call_target="tpu_custom_call" | custom-call | flops 1 | bytes 1 | tf_op jit(solution)/shard_map/close_layer/pallas_call | solution.py:442
  153.4 2.5 %collective-permute-start.28 = (bf16[256,512]{1,0:T(8,128)(2,1)S(1)}, bf16[256,512]{1,0:T(8,128)(2,1)S(1)}, u32[]{:S(2)}, u32[]{:S(2)}) collective-permute-start(bf16[256,512]{1,0:T(8,128)(2,1)S(1)} %get-tuple-element.126), channel_id=1, source_target_pairs={{0,1},{1,0},{2,3},{3,2},{4,5},{5,4},{6,7},{7,6},{8,9},{9,8},{10,11... | collective-permute-start | bytes 786440 | tf_op jit(solution)/shard_map/ppermute | solution.py:538
  155.9 3.6 %expand.7 = (bf16[256,512]{1,0:T(8,128)(2,1)S(1)}, bf16[256,512]{1,0:T(8,128)(2,1)S(1)}, bf16[256,512]{1,0:T(8,128)(2,1)S(1)}, bf16[256,512]{1,0:T(8,128)(2,1)S(1)}) custom-call(s32[16]{0:T(128)S(1)} %pad_add_fusion.table_ref, bf16[256,1024]{1,0:T(8,128)(2,1)S(1)} %get-tuple-element.120.gated_ref, bf16[2,1024,4096]{2,1,0:T(8,128)(2,1)} %w_ref.7), custom_call_target="tpu_custom_call" | custom-call | flops 1 | bytes 1 | tf_op jit(solution)/shard_map/expand/pallas_call | solution.py:468
  164.3 3.1 %expand.6 = (bf16[256,512]{1,0:T(8,128)(2,1)S(1)}, bf16[256,512]{1,0:T(8,128)(2,1)S(1)}, bf16[256,512]{1,0:T(8,128)(2,1)S(1)}) custom-call(s32[16]{0:T(128)S(1)} %pad_add_fusion.table_ref, bf16[256,1024]{1,0:T(8,128)(2,1)S(1)} %get-tuple-element.120.gated_ref, bf16[2,1024,4096]{2,1,0:T(8,128)(2,1)} %w_ref.7), custom_call_target="tpu_custom_call" | custom-call | flops 1 | bytes 1 | tf_op jit(solution)/shard_map/expand/pallas_call | solution.py:468
  169.1 3.1 %collective-permute-start.32 = (bf16[256,512]{1,0:T(8,128)(2,1)S(1)}, bf16[256,512]{1,0:T(8,128)(2,1)S(1)}, u32[]{:S(2)}, u32[]{:S(2)}) collective-permute-start(bf16[256,512]{1,0:T(8,128)(2,1)S(1)} %combine.14), channel_id=1, source_target_pairs={{0,6},{1,7},{2,0},{3,1},{4,2},{5,3},{6,4},{7,5},{8,14},{9,15},{10,... | collective-permute-start | bytes 786440 | tf_op jit(solution)/shard_map/ppermute | solution.py:538
  175.6 4.0 %collective-permute-done.26.refs_2_ = bf16[256,512]{1,0:T(8,128)(2,1)S(1)} collective-permute-done((bf16[256,512]{1,0:T(8,128)(2,1)S(1)}, bf16[256,512]{1,0:T(8,128)(2,1)S(1)}, u32[]{:S(2)}, u32[]{:S(2)}) %collective-permute-start.26) | collective-permute-done | bytes 262176 | tf_op jit(solution)/shard_map/ppermute | solution.py:538
  179.6 4.3 %collective-permute-done.30.refs_3_ = bf16[256,512]{1,0:T(8,128)(2,1)S(1)} collective-permute-done((bf16[256,512]{1,0:T(8,128)(2,1)S(1)}, bf16[256,512]{1,0:T(8,128)(2,1)S(1)}, u32[]{:S(2)}, u32[]{:S(2)}) %collective-permute-start.30) | collective-permute-done | bytes 262176 | tf_op jit(solution)/shard_map/ppermute | solution.py:538
  (97 shorter events, 53.8 us)
Async XLA Ops:
  0.0 12.6 %collective-permute-start = (bf16[256,512]{1,0:T(8,128)(2,1)}, bf16[256,512]{1,0:T(8,128)(2,1)S(1)}, u32[]{:S(2)}, u32[]{:S(2)}) collective-permute-start(bf16[256,512]{1,0:T(8,128)(2,1)} %refs_0_.3), channel_id=1, source_target_pairs={{0,1},{1,0},{2,3},{3,2},{4,5},{5,4},{6,7},{7,6},{8,9},{9,8},{10,11... | collective-permute-start | bytes 786440 | tf_op jit(solution)/shard_map/ppermute | solution.py:538
  3.0 11.4 %collective-permute-start.4 = (bf16[256,512]{1,0:T(8,128)(2,1)}, bf16[256,512]{1,0:T(8,128)(2,1)}, u32[]{:S(2)}, u32[]{:S(2)}) collective-permute-start(bf16[256,512]{1,0:T(8,128)(2,1)} %refs_0_.3), channel_id=1, source_target_pairs={{0,2},{1,3},{2,4},{3,5},{4,6},{5,7},{6,0},{7,1},{8,10},{9,11},{10,... | collective-permute-start | bytes 786440 | tf_op jit(solution)/shard_map/ppermute | solution.py:538
  4.5 13.8 %collective-permute-start.7 = (bf16[256,512]{1,0:T(8,128)(2,1)}, bf16[256,512]{1,0:T(8,128)(2,1)}, u32[]{:S(2)}, u32[]{:S(2)}) collective-permute-start(bf16[256,512]{1,0:T(8,128)(2,1)} %refs_0_.3), channel_id=1, source_target_pairs={{0,6},{1,7},{2,0},{3,1},{4,2},{5,3},{6,4},{7,5},{8,14},{9,15},{10,... | collective-permute-start | bytes 786440 | tf_op jit(solution)/shard_map/ppermute | solution.py:538
  13.5 7.9 %collective-permute-start.1 = (bf16[256,288]{1,0:T(8,128)(2,1)S(1)}, bf16[256,288]{1,0:T(8,128)(2,1)S(1)}, u32[]{:S(2)}, u32[]{:S(2)}) collective-permute-start(bf16[256,288]{1,0:T(8,128)(2,1)S(1)} %project_low.2), channel_id=1, source_target_pairs={{0,1},{1,0},{2,3},{3,2},{4,5},{5,4},{6,7},{7,6},{8,9},{9,8},{10,11... | collective-permute-start | bytes 442376 | tf_op jit(solution)/shard_map/ppermute | solution.py:538
  14.3 10.3 %collective-permute-start.5 = (bf16[256,512]{1,0:T(8,128)(2,1)}, bf16[256,512]{1,0:T(8,128)(2,1)S(1)}, u32[]{:S(2)}, u32[]{:S(2)}) collective-permute-start(bf16[256,512]{1,0:T(8,128)(2,1)} %collective-permute-done.4.refs_0_), channel_id=1, source_target_pairs={{0,2},{1,3},{2,4},{3,5},{4,6},{5,7},{6,0},{7,1},{8,10},{9,11},{10,... | collective-permute-start | bytes 786440 | tf_op jit(solution)/shard_map/ppermute | solution.py:538
  14.4 12.6 %collective-permute-start.9 = (bf16[256,512]{1,0:T(8,128)(2,1)}, bf16[256,512]{1,0:T(8,128)(2,1)S(1)}, u32[]{:S(2)}, u32[]{:S(2)}) collective-permute-start(bf16[256,512]{1,0:T(8,128)(2,1)} %collective-permute-done.4.refs_0_), channel_id=1, source_target_pairs={{0,1},{1,0},{2,3},{3,2},{4,5},{5,4},{6,7},{7,6},{8,9},{9,8},{10,11... | collective-permute-start | bytes 786440 | tf_op jit(solution)/shard_map/ppermute | solution.py:538
  18.3 14.3 %collective-permute-start.8 = (bf16[256,512]{1,0:T(8,128)(2,1)}, bf16[256,512]{1,0:T(8,128)(2,1)S(1)}, u32[]{:S(2)}, u32[]{:S(2)}) collective-permute-start(bf16[256,512]{1,0:T(8,128)(2,1)} %collective-permute-done.7.refs_0_), channel_id=1, source_target_pairs={{0,1},{1,0},{2,3},{3,2},{4,5},{5,4},{6,7},{7,6},{8,9},{9,8},{10,11... | collective-permute-start | bytes 786440 | tf_op jit(solution)/shard_map/ppermute | solution.py:538
  21.5 11.1 %collective-permute-start.2 = (bf16[256,288]{1,0:T(8,128)(2,1)S(1)}, bf16[256,288]{1,0:T(8,128)(2,1)S(1)}, u32[]{:S(2)}, u32[]{:S(2)}) collective-permute-start(bf16[256,288]{1,0:T(8,128)(2,1)S(1)} %add_convert_fusion.3.refs_7_), channel_id=1, source_target_pairs={{0,4},{1,5},{2,6},{3,7},{4,0},{5,1},{6,2},{7,3},{8,12},{9,13},{10,... | collective-permute-start | bytes 442376 | tf_op jit(solution)/shard_map/ppermute | solution.py:542
  24.7 12.2 %collective-permute-start.6 = (bf16[256,512]{1,0:T(8,128)(2,1)S(1)}, bf16[256,512]{1,0:T(8,128)(2,1)S(1)}, u32[]{:S(2)}, u32[]{:S(2)}) collective-permute-start(bf16[256,512]{1,0:T(8,128)(2,1)S(1)} %relay.2), channel_id=1, source_target_pairs={{0,1},{1,0},{2,3},{3,2},{4,5},{5,4},{6,7},{7,6},{8,9},{9,8},{10,11... | collective-permute-start | bytes 786440 | tf_op jit(solution)/shard_map/ppermute | solution.py:538
  32.6 8.1 %collective-permute-start.3 = (bf16[256,288]{1,0:T(8,128)(2,1)S(1)}, bf16[256,288]{1,0:T(8,128)(2,1)S(1)}, u32[]{:S(2)}, u32[]{:S(2)}) collective-permute-start(bf16[256,288]{1,0:T(8,128)(2,1)S(1)} %add_convert_fusion.2.refs_7_.own_ref), channel_id=1, source_target_pairs={{0,2},{1,3},{2,0},{3,1},{4,6},{5,7},{6,4},{7,5},{8,10},{9,11},{10,... | collective-permute-start | bytes 442376 | tf_op jit(solution)/shard_map/ppermute | solution.py:542
  62.5 9.2 %collective-permute-start.12 = (bf16[256,512]{1,0:T(8,128)(2,1)S(1)}, bf16[256,512]{1,0:T(8,128)(2,1)S(1)}, u32[]{:S(2)}, u32[]{:S(2)}) collective-permute-start(bf16[256,512]{1,0:T(8,128)(2,1)S(1)} %get-tuple-element.93), channel_id=1, source_target_pairs={{0,1},{1,0},{2,3},{3,2},{4,5},{5,4},{6,7},{7,6},{8,9},{9,8},{10,11... | collective-permute-start | bytes 786440 | tf_op jit(solution)/shard_map/ppermute | solution.py:538
  67.8 14.1 %collective-permute-start.15 = (bf16[256,512]{1,0:T(8,128)(2,1)S(1)}, bf16[256,512]{1,0:T(8,128)(2,1)S(1)}, u32[]{:S(2)}, u32[]{:S(2)}) collective-permute-start(bf16[256,512]{1,0:T(8,128)(2,1)S(1)} %get-tuple-element.96), channel_id=1, source_target_pairs={{0,1},{1,0},{2,3},{3,2},{4,5},{5,4},{6,7},{7,6},{8,9},{9,8},{10,11... | collective-permute-start | bytes 786440 | tf_op jit(solution)/shard_map/ppermute | solution.py:538
  68.2 15.6 %collective-permute-start.11 = (bf16[256,512]{1,0:T(8,128)(2,1)S(1)}, bf16[256,512]{1,0:T(8,128)(2,1)S(1)}, u32[]{:S(2)}, u32[]{:S(2)}) collective-permute-start(bf16[256,512]{1,0:T(8,128)(2,1)S(1)} %get-tuple-element.91), channel_id=1, source_target_pairs={{0,1},{1,0},{2,3},{3,2},{4,5},{5,4},{6,7},{7,6},{8,9},{9,8},{10,11... | collective-permute-start | bytes 786440 | tf_op jit(solution)/shard_map/ppermute | solution.py:538
  71.8 12.0 %collective-permute-start.13 = (bf16[256,512]{1,0:T(8,128)(2,1)S(1)}, bf16[256,512]{1,0:T(8,128)(2,1)S(1)}, u32[]{:S(2)}, u32[]{:S(2)}) collective-permute-start(bf16[256,512]{1,0:T(8,128)(2,1)S(1)} %combine.8.refs_0_), channel_id=1, source_target_pairs={{0,2},{1,3},{2,4},{3,5},{4,6},{5,7},{6,0},{7,1},{8,10},{9,11},{10,... | collective-permute-start | bytes 786440 | tf_op jit(solution)/shard_map/ppermute | solution.py:538
  77.1 14.1 %collective-permute-start.10 = (bf16[256,512]{1,0:T(8,128)(2,1)S(1)}, bf16[256,512]{1,0:T(8,128)(2,1)S(1)}, u32[]{:S(2)}, u32[]{:S(2)}) collective-permute-start(bf16[256,512]{1,0:T(8,128)(2,1)S(1)} %get-tuple-element.89), channel_id=1, source_target_pairs={{0,1},{1,0},{2,3},{3,2},{4,5},{5,4},{6,7},{7,6},{8,9},{9,8},{10,11... | collective-permute-start | bytes 786440 | tf_op jit(solution)/shard_map/ppermute | solution.py:538
  81.9 9.3 %collective-permute-start.16 = (bf16[256,512]{1,0:T(8,128)(2,1)S(1)}, bf16[256,512]{1,0:T(8,128)(2,1)S(1)}, u32[]{:S(2)}, u32[]{:S(2)}) collective-permute-start(bf16[256,512]{1,0:T(8,128)(2,1)S(1)} %combine.10.refs_0_), channel_id=1, source_target_pairs={{0,6},{1,7},{2,0},{3,1},{4,2},{5,3},{6,4},{7,5},{8,14},{9,15},{10,... | collective-permute-start | bytes 786440 | tf_op jit(solution)/shard_map/ppermute | solution.py:538
  83.9 10.7 %collective-permute-start.14 = (bf16[256,512]{1,0:T(8,128)(2,1)S(1)}, bf16[256,512]{1,0:T(8,128)(2,1)S(1)}, u32[]{:S(2)}, u32[]{:S(2)}) collective-permute-start(bf16[256,512]{1,0:T(8,128)(2,1)S(1)} %combine.9), channel_id=1, source_target_pairs={{0,2},{1,3},{2,4},{3,5},{4,6},{5,7},{6,0},{7,1},{8,10},{9,11},{10,... | collective-permute-start | bytes 786440 | tf_op jit(solution)/shard_map/ppermute | solution.py:538
  95.6 17.5 %collective-permute-start.17 = (bf16[256,800]{1,0:T(8,128)(2,1)S(1)}, bf16[256,800]{1,0:T(8,128)(2,1)S(1)}, u32[]{:S(2)}, u32[]{:S(2)}) collective-permute-start(bf16[256,800]{1,0:T(8,128)(2,1)S(1)} %project_low.3), channel_id=1, source_target_pairs={{0,1},{1,0},{2,3},{3,2},{4,5},{5,4},{6,7},{7,6},{8,9},{9,8},{10,11... | collective-permute-start | bytes 1228808 | tf_op jit(solution)/shard_map/ppermute | solution.py:538
  96.0 11.1 %collective-permute-start.20 = (bf16[256,512]{1,0:T(8,128)(2,1)S(1)}, bf16[256,512]{1,0:T(8,128)(2,1)S(1)}, u32[]{:S(2)}, u32[]{:S(2)}) collective-permute-start(bf16[256,512]{1,0:T(8,128)(2,1)S(1)} %combine.11.rows_ref.refs_0_), channel_id=1, source_target_pairs={{0,2},{1,3},{2,4},{3,5},{4,6},{5,7},{6,0},{7,1},{8,10},{9,11},{10,... | collective-permute-start | bytes 786440 | tf_op jit(solution)/shard_map/ppermute | solution.py:538
  97.6 13.6 %collective-permute-start.23 = (bf16[256,512]{1,0:T(8,128)(2,1)S(1)}, bf16[256,512]{1,0:T(8,128)(2,1)S(1)}, u32[]{:S(2)}, u32[]{:S(2)}) collective-permute-start(bf16[256,512]{1,0:T(8,128)(2,1)S(1)} %combine.11.rows_ref.refs_0_), channel_id=1, source_target_pairs={{0,6},{1,7},{2,0},{3,1},{4,2},{5,3},{6,4},{7,5},{8,14},{9,15},{10,... | collective-permute-start | bytes 786440 | tf_op jit(solution)/shard_map/ppermute | solution.py:538
  107.1 9.9 %collective-permute-start.21 = (bf16[256,512]{1,0:T(8,128)(2,1)S(1)}, bf16[256,512]{1,0:T(8,128)(2,1)S(1)}, u32[]{:S(2)}, u32[]{:S(2)}) collective-permute-start(bf16[256,512]{1,0:T(8,128)(2,1)S(1)} %collective-permute-done.20.refs_0_), channel_id=1, source_target_pairs={{0,2},{1,3},{2,4},{3,5},{4,6},{5,7},{6,0},{7,1},{8,10},{9,11},{10,... | collective-permute-start | bytes 786440 | tf_op jit(solution)/shard_map/ppermute | solution.py:538
  108.9 16.5 %collective-permute-start.25 = (bf16[256,512]{1,0:T(8,128)(2,1)S(1)}, bf16[256,512]{1,0:T(8,128)(2,1)S(1)}, u32[]{:S(2)}, u32[]{:S(2)}) collective-permute-start(bf16[256,512]{1,0:T(8,128)(2,1)S(1)} %collective-permute-done.20.refs_0_), channel_id=1, source_target_pairs={{0,1},{1,0},{2,3},{3,2},{4,5},{5,4},{6,7},{7,6},{8,9},{9,8},{10,11... | collective-permute-start | bytes 786440 | tf_op jit(solution)/shard_map/ppermute | solution.py:538
  111.2 16.0 %collective-permute-start.24 = (bf16[256,512]{1,0:T(8,128)(2,1)S(1)}, bf16[256,512]{1,0:T(8,128)(2,1)S(1)}, u32[]{:S(2)}, u32[]{:S(2)}) collective-permute-start(bf16[256,512]{1,0:T(8,128)(2,1)S(1)} %collective-permute-done.23.refs_0_), channel_id=1, source_target_pairs={{0,1},{1,0},{2,3},{3,2},{4,5},{5,4},{6,7},{7,6},{8,9},{9,8},{10,11... | collective-permute-start | bytes 786440 | tf_op jit(solution)/shard_map/ppermute | solution.py:538
  113.2 12.1 %collective-permute-start.18 = (bf16[256,288]{1,0:T(8,128)(2,1)S(1)}, bf16[256,288]{1,0:T(8,128)(2,1)S(1)}, u32[]{:S(2)}, u32[]{:S(2)}) collective-permute-start(bf16[256,288]{1,0:T(8,128)(2,1)S(1)} %add_convert_fusion.1), channel_id=1, source_target_pairs={{0,4},{1,5},{2,6},{3,7},{4,0},{5,1},{6,2},{7,3},{8,12},{9,13},{10,... | collective-permute-start | bytes 442376 | tf_op jit(solution)/shard_map/ppermute | solution.py:542
  117.0 12.1 %collective-permute-start.22 = (bf16[256,512]{1,0:T(8,128)(2,1)S(1)}, bf16[256,512]{1,0:T(8,128)(2,1)S(1)}, u32[]{:S(2)}, u32[]{:S(2)}) collective-permute-start(bf16[256,512]{1,0:T(8,128)(2,1)S(1)} %relay.3), channel_id=1, source_target_pairs={{0,1},{1,0},{2,3},{3,2},{4,5},{5,4},{6,7},{7,6},{8,9},{9,8},{10,11... | collective-permute-start | bytes 786440 | tf_op jit(solution)/shard_map/ppermute | solution.py:538
  153.4 9.6 %collective-permute-start.28 = (bf16[256,512]{1,0:T(8,128)(2,1)S(1)}, bf16[256,512]{1,0:T(8,128)(2,1)S(1)}, u32[]{:S(2)}, u32[]{:S(2)}) collective-permute-start(bf16[256,512]{1,0:T(8,128)(2,1)S(1)} %get-tuple-element.126), channel_id=1, source_target_pairs={{0,1},{1,0},{2,3},{3,2},{4,5},{5,4},{6,7},{7,6},{8,9},{9,8},{10,11... | collective-permute-start | bytes 786440 | tf_op jit(solution)/shard_map/ppermute | solution.py:538
  159.5 9.6 %collective-permute-start.31 = (bf16[256,512]{1,0:T(8,128)(2,1)S(1)}, bf16[256,512]{1,0:T(8,128)(2,1)S(1)}, u32[]{:S(2)}, u32[]{:S(2)}) collective-permute-start(bf16[256,512]{1,0:T(8,128)(2,1)S(1)} %get-tuple-element.128), channel_id=1, source_target_pairs={{0,1},{1,0},{2,3},{3,2},{4,5},{5,4},{6,7},{7,6},{8,9},{9,8},{10,11... | collective-permute-start | bytes 786440 | tf_op jit(solution)/shard_map/ppermute | solution.py:538
  159.6 14.8 %collective-permute-start.27 = (bf16[256,512]{1,0:T(8,128)(2,1)S(1)}, bf16[256,512]{1,0:T(8,128)(2,1)S(1)}, u32[]{:S(2)}, u32[]{:S(2)}) collective-permute-start(bf16[256,512]{1,0:T(8,128)(2,1)S(1)} %get-tuple-element.124), channel_id=1, source_target_pairs={{0,1},{1,0},{2,3},{3,2},{4,5},{5,4},{6,7},{7,6},{8,9},{9,8},{10,11... | collective-permute-start | bytes 786440 | tf_op jit(solution)/shard_map/ppermute | solution.py:538
  163.1 11.3 %collective-permute-start.29 = (bf16[256,512]{1,0:T(8,128)(2,1)S(1)}, bf16[256,512]{1,0:T(8,128)(2,1)S(1)}, u32[]{:S(2)}, u32[]{:S(2)}) collective-permute-start(bf16[256,512]{1,0:T(8,128)(2,1)S(1)} %combine.12), channel_id=1, source_target_pairs={{0,2},{1,3},{2,4},{3,5},{4,6},{5,7},{6,0},{7,1},{8,10},{9,11},{10,... | collective-permute-start | bytes 786440 | tf_op jit(solution)/shard_map/ppermute | solution.py:538
  167.4 12.2 %collective-permute-start.26 = (bf16[256,512]{1,0:T(8,128)(2,1)S(1)}, bf16[256,512]{1,0:T(8,128)(2,1)S(1)}, u32[]{:S(2)}, u32[]{:S(2)}) collective-permute-start(bf16[256,512]{1,0:T(8,128)(2,1)S(1)} %get-tuple-element.122), channel_id=1, source_target_pairs={{0,1},{1,0},{2,3},{3,2},{4,5},{5,4},{6,7},{7,6},{8,9},{9,8},{10,11... | collective-permute-start | bytes 786440 | tf_op jit(solution)/shard_map/ppermute | solution.py:538
  169.1 10.5 %collective-permute-start.32 = (bf16[256,512]{1,0:T(8,128)(2,1)S(1)}, bf16[256,512]{1,0:T(8,128)(2,1)S(1)}, u32[]{:S(2)}, u32[]{:S(2)}) collective-permute-start(bf16[256,512]{1,0:T(8,128)(2,1)S(1)} %combine.14), channel_id=1, source_target_pairs={{0,6},{1,7},{2,0},{3,1},{4,2},{5,3},{6,4},{7,5},{8,14},{9,15},{10,... | collective-permute-start | bytes 786440 | tf_op jit(solution)/shard_map/ppermute | solution.py:538
  174.5 9.4 %collective-permute-start.30 = (bf16[256,512]{1,0:T(8,128)(2,1)S(1)}, bf16[256,512]{1,0:T(8,128)(2,1)S(1)}, u32[]{:S(2)}, u32[]{:S(2)}) collective-permute-start(bf16[256,512]{1,0:T(8,128)(2,1)S(1)} %combine.13), channel_id=1, source_target_pairs={{0,2},{1,3},{2,4},{3,5},{4,6},{5,7},{6,0},{7,1},{8,10},{9,11},{10,... | collective-permute-start | bytes 786440 | tf_op jit(solution)/shard_map/ppermute | solution.py:538
  (10 other events, 60.7 us)

commit v3 on v1

--- a/solution.py
+++ b/solution.py
@@ -644,8 +644,8 @@
         state = None
         for n, a in enumerate(arrivals):
             if n:
-                last = n + 1 == len(arrivals)
-                beside[a] = cross(relay(columns[a], *first) if last else columns[a])
+                late = n > 1 if packed else n + 1 == len(arrivals)
+                beside[a] = cross(relay(columns[a], *first) if late else columns[a])
             arrived = [columns[a], *beside[a]]
             place, earlier = a * grid.side, stages[n - 1 + packed : n + packed] if n else []
             if a in weights:

time: 184 us -> 185 us (level)
  transfers between devices with their start and end apart: 33 -> 33, of which waited for: 18 -> 19; matrix products, arithmetic and copies ran while one was open for 1% -> 1% of each run, Pallas kernels for 28% -> 28%
where the time goes in v3:
time: 185 us
  Pallas kernels  85.6 us (46%)
  waiting for transfers between devices  41.4 us (22%)
  starting transfers between devices  40.7 us (22%)
  blocking collectives  10.9 us (6%)
  local copies, waits for them, and re-layouts  4.23 us (2%)
    ppermute x29, waiting for transfers between devices, send(): return lax.ppermute(value, 'tp', pairs)  36.5 us
    ppermute x29, starting transfers between devices, send(): return lax.ppermute(value, 'tp', pairs)  33.4 us
    pallas_call x2, Pallas kernels, local_scan(): pl.pallas_call(functools.partial(scan_kernel, layer, states, width), out_...  17.5 us
    pallas_call x5, Pallas kernels, unpack(): pl.pallas_call(functools.partial(unpack_kernel, count, layer, table_at, w...  15.8 us
    pallas_call x2, Pallas kernels, close_layer(): pl.pallas_call(functools.partial(close_kernel, layer, states, table_at, f...  15.2 us
    pallas_call x4, Pallas kernels, expand(): pl.pallas_call(functools.partial(expand_kernel, layer, table_at, feat), o...  13.3 us
    pallas_call x3, Pallas kernels, project(): pl.pallas_call(functools.partial(proj_kernel, count, before is None, laye...  11.3 us
    all_gather x2, blocking collectives, per_device(): finals = lax.all_gather(final, 'seq')  10.9 us
  transfers between devices with their start and end apart: 33, of which 19 were waited for; matrix products, arithmetic and copies ran while one was open for 1% of the time, Pallas kernels for 28%

profile of v3, /device:TPU:0, one launch (start us, length us, event | category | flops | bytes accessed | tf_op | source)
XLA Modules:
  0.0 184.5 jit_solution(13039411150263689600)
XLA Ops:
  0.0 3.0 %collective-permute-start = (bf16[256,512]{1,0:T(8,128)(2,1)}, bf16[256,512]{1,0:T(8,128)(2,1)S(1)}, u32[]{:S(2)}, u32[]{:S(2)}) collective-permute-start(bf16[256,512]{1,0:T(8,128)(2,1)} %refs_0_.3), channel_id=1, source_target_pairs={{0,1},{1,0},{2,3},{3,2},{4,5},{5,4},{6,7},{7,6},{8,9},{9,8},{10,11... | collective-permute-start | bytes 786440 | tf_op jit(solution)/shard_map/ppermute | solution.py:538
  7.9 3.3 %unpack.5 = (bf16[2,1024,1024]{2,1,0:T(8,128)(2,1)S(1)}, f32[8,128]{1,0:T(8,128)}) custom-call(s32[16]{0:T(128)S(1)} %pad_add_fusion.table_ref, bf16[2,65536,128]{2,1,0:T(8,128)(2,1)} %bitcast.22, f32[2,16,8,128]{3,2,1,0:T(8,128)S(1)} %bitcast.13), custom_call_target="tpu_custom_call" | custom-call | flops 1 | bytes 1 | tf_op jit(solution)/shard_map/unpack/pallas_call | solution.py:175
  22.1 2.5 %collective-permute-start.2 = (bf16[256,288]{1,0:T(8,128)(2,1)S(1)}, bf16[256,288]{1,0:T(8,128)(2,1)S(1)}, u32[]{:S(2)}, u32[]{:S(2)}) collective-permute-start(bf16[256,288]{1,0:T(8,128)(2,1)S(1)} %add_convert_fusion.3.refs_7_), channel_id=1, source_target_pairs={{0,2},{1,3},{2,0},{3,1},{4,6},{5,7},{6,4},{7,5},{8,10},{9,11},{10,... | collective-permute-start | bytes 442376 | tf_op jit(solution)/shard_map/ppermute | solution.py:542
  27.6 3.8 %project.3 = (f32[256,1024]{1,0:T(8,128)S(1)}, f32[256,1024]{1,0:T(8,128)S(1)}, f32[256,1]{1,0:T(8,128)S(1)}) custom-call(s32[16]{0:T(128)S(1)} %pad_add_fusion.table_ref, bf16[256,512]{1,0:T(8,128)(2,1)S(1)} %collective-permute-done.4.refs_0_, ...), custom_call_target="tpu_custom_call", output_to_operand_aliasing={{0}: (5, {}), {1}: (6, {}), {2}: (7, {})} | custom-call | flops 10000000000 | bytes 1 | tf_op jit(solution)/shard_map/project/pallas_call | solution.py:118
  33.2 3.8 %project.4 = (f32[256,1024]{1,0:T(8,128)S(1)}, f32[256,1024]{1,0:T(8,128)S(1)}, f32[256,1]{1,0:T(8,128)S(1)}) custom-call(s32[16]{0:T(128)S(1)} %pad_add_fusion.table_ref, bf16[256,512]{1,0:T(8,128)(2,1)S(1)} %collective-permute-done.7.refs_0_, ...), custom_call_target="tpu_custom_call", output_to_operand_aliasing={{0}: (5, {}), {1}: (6, {}), {2}: (7, {})} | custom-call | flops 10000000000 | bytes 1 | tf_op jit(solution)/shard_map/project/pallas_call | solution.py:118
  37.1 3.8 %project.5 = (f32[256,1024]{1,0:T(8,128)S(1)}, f32[256,1024]{1,0:T(8,128)S(1)}, f32[256,1]{1,0:T(8,128)S(1)}) custom-call(s32[16]{0:T(128)S(1)} %pad_add_fusion.table_ref, bf16[256,512]{1,0:T(8,128)(2,1)S(1)} %collective-permute-done.5.value_ref.refs_0_, ...), custom_call_target="tpu_custom_call", output_to_operand_aliasing={{0}: (5, {}), {1}: (6, {}), {2}: (7, {})} | custom-call | flops 10000000000 | bytes 1 | tf_op jit(solution)/shard_map/project/pallas_call | solution.py:118
  41.0 8.8 %local_scan.2 = (f32[6152,128]{1,0:T(8,128)S(1)}, f32[6152,128]{1,0:T(8,128)S(1)}, bf16[17,8,128]{2,1,0:T(8,128)(2,1)S(1)}) custom-call(f32[256,32]{1,0:T(8,128)S(1)} %get-tuple-element.76.sel_ref, f32[256,288]{1,0:T(8,128)S(1)} %get-tuple-element.77.low_ref, f32[256,1]{1,0:T(8,128)S(1)} %get-tuple-element.75.refs_0_.square_ref.refs_4_, ...), custom_call_target="tpu_custom_call" | custom-call | flops 1 | bytes 1 | tf_op jit(solution)/shard_map/local_scan/pallas_call | solution.py:352
  49.7 5.4 %all-gather = bf16[68,8,128]{2,1,0:T(8,128)(2,1)S(1)} all-gather(bf16[17,8,128]{2,1,0:T(8,128)(2,1)S(1)} %get-tuple-element.82), channel_id=2, replica_groups=mesh['seq'=4,'tp'=8] {'seq'}, dimensions={0}, use_global_device_ids=true | all-gather | bytes 174080 | tf_op jit(solution)/shard_map/all_gather | solution.py:666
  55.2 7.7 %close_layer.2 = (bf16[256,1024]{1,0:T(8,128)(2,1)S(1)}, bf16[256,512]{1,0:T(8,128)(2,1)S(1)}) custom-call(s32[16]{0:T(128)S(1)} %pad_add_fusion.table_ref, s32[1]{0:T(128)} %bitcast.place_ref, f32[256,32]{1,0:T(8,128)S(1)} %get-tuple-element.76.sel_ref, f32[6152,128]{1,0:T(8,128)S(1)} %get-tuple-element.79.refs_0_, ...), custom_call_target="tpu_custom_call" | custom-call | flops 1 | bytes 1 | tf_op jit(solution)/shard_map/close_layer/pallas_call | solution.py:442
  63.5 3.6 %expand.5 = (bf16[256,512]{1,0:T(8,128)(2,1)S(1)}, bf16[256,512]{1,0:T(8,128)(2,1)S(1)}, bf16[256,512]{1,0:T(8,128)(2,1)S(1)}, bf16[256,512]{1,0:T(8,128)(2,1)S(1)}) custom-call(s32[16]{0:T(128)S(1)} %pad_add_fusion.table_ref, bf16[256,1024]{1,0:T(8,128)(2,1)S(1)} %get-tuple-element.83.gated_ref, bf16[2,1024,4096]{2,1,0:T(8,128)(2,1)} %w_ref.7), custom_call_target="tpu_custom_call" | custom-call | flops 1 | bytes 1 | tf_op jit(solution)/shard_map/expand/pallas_call | solution.py:468
  69.2 2.9 %collective-permute-done.12.refs_1_ = bf16[256,512]{1,0:T(8,128)(2,1)S(1)} collective-permute-done((bf16[256,512]{1,0:T(8,128)(2,1)S(1)}, bf16[256,512]{1,0:T(8,128)(2,1)S(1)}, u32[]{:S(2)}, u32[]{:S(2)}) %collective-permute-start.12) | collective-permute-done | bytes 262176 | tf_op jit(solution)/shard_map/ppermute | solution.py:538
  72.9 3.1 %expand.4 = (bf16[256,512]{1,0:T(8,128)(2,1)S(1)}, bf16[256,512]{1,0:T(8,128)(2,1)S(1)}, bf16[256,512]{1,0:T(8,128)(2,1)S(1)}) custom-call(s32[16]{0:T(128)S(1)} %pad_add_fusion.table_ref, bf16[256,1024]{1,0:T(8,128)(2,1)S(1)} %get-tuple-element.83.gated_ref, bf16[2,1024,4096]{2,1,0:T(8,128)(2,1)} %w_ref.7), custom_call_target="tpu_custom_call" | custom-call | flops 1 | bytes 1 | tf_op jit(solution)/shard_map/expand/pallas_call | solution.py:468
  76.4 3.0 %unpack.6 = (bf16[2,1024,1024]{2,1,0:T(8,128)(2,1)S(1)}, f32[8,128]{1,0:T(8,128)S(1)}) custom-call(s32[16]{0:T(128)S(1)} %pad_add_fusion.table_ref, bf16[2,65536,128]{2,1,0:T(8,128)(2,1)} %bitcast.26, bf16[256,512]{1,0:T(8,128)(2,1)S(1)} %combine.8.refs_0_), custom_call_target="tpu_custom_call" | custom-call | flops 1 | bytes 1 | tf_op jit(solution)/shard_map/unpack/pallas_call | solution.py:175
  79.6 3.4 %collective-permute-start.16 = (bf16[256,512]{1,0:T(8,128)(2,1)S(1)}, bf16[256,512]{1,0:T(8,128)(2,1)S(1)}, u32[]{:S(2)}, u32[]{:S(2)}) collective-permute-start(bf16[256,512]{1,0:T(8,128)(2,1)S(1)} %combine.10.refs_0_), channel_id=1, source_target_pairs={{0,6},{1,7},{2,0},{3,1},{4,2},{5,3},{6,4},{7,5},{8,14},{9,15},{10,... | collective-permute-start | bytes 786440 | tf_op jit(solution)/shard_map/ppermute | solution.py:538
  84.2 3.0 %unpack.7 = (bf16[2,1024,1024]{2,1,0:T(8,128)(2,1)S(1)}, f32[8,128]{1,0:T(8,128)S(1)}) custom-call(s32[16]{0:T(128)S(1)} %pad_add_fusion.table_ref, bf16[2,65536,128]{2,1,0:T(8,128)(2,1)} %bitcast.27, bf16[256,512]{1,0:T(8,128)(2,1)S(1)} %combine.10.refs_0_), custom_call_target="tpu_custom_call" | custom-call | flops 1 | bytes 1 | tf_op jit(solution)/shard_map/unpack/pallas_call | solution.py:175
  87.2 3.1 %unpack.8 = (bf16[2,1024,1024]{2,1,0:T(8,128)(2,1)S(1)}, f32[8,128]{1,0:T(8,128)S(1)}) custom-call(s32[16]{0:T(128)S(1)} %pad_add_fusion.table_ref, bf16[2,65536,128]{2,1,0:T(8,128)(2,1)} %bitcast.28, bf16[256,512]{1,0:T(8,128)(2,1)S(1)} %combine.10.refs_0_), custom_call_target="tpu_custom_call" | custom-call | flops 1 | bytes 1 | tf_op jit(solution)/shard_map/unpack/pallas_call | solution.py:175
  90.3 3.2 %collective-permute-done.14.refs_3_ = bf16[256,512]{1,0:T(8,128)(2,1)S(1)} collective-permute-done((bf16[256,512]{1,0:T(8,128)(2,1)S(1)}, bf16[256,512]{1,0:T(8,128)(2,1)S(1)}, u32[]{:S(2)}, u32[]{:S(2)}) %collective-permute-start.14) | collective-permute-done | bytes 262176 | tf_op jit(solution)/shard_map/ppermute | solution.py:538
  97.8 3.3 %unpack.9 = (bf16[2,1024,1024]{2,1,0:T(8,128)(2,1)S(1)}, f32[8,128]{1,0:T(8,128)}) custom-call(s32[16]{0:T(128)S(1)} %pad_add_fusion.table_ref, bf16[2,65536,128]{2,1,0:T(8,128)(2,1)} %bitcast.29, bf16[256,512]{1,0:T(8,128)(2,1)S(1)} %collective-permute-done.10.refs_2_.refs_0_), custom_call_target="tpu_custom_call" | custom-call | flops 1 | bytes 1 | tf_op jit(solution)/shard_map/unpack/pallas_call | solution.py:175
  103.3 3.1 %collective-permute-done.20.refs_0_ = bf16[256,512]{1,0:T(8,128)(2,1)S(1)} collective-permute-done((bf16[256,512]{1,0:T(8,128)(2,1)S(1)}, bf16[256,512]{1,0:T(8,128)(2,1)S(1)}, u32[]{:S(2)}, u32[]{:S(2)}) %collective-permute-start.20) | collective-permute-done | bytes 262176 | tf_op jit(solution)/shard_map/ppermute | solution.py:538
  106.4 2.8 %collective-permute-start.21 = (bf16[256,512]{1,0:T(8,128)(2,1)S(1)}, bf16[256,512]{1,0:T(8,128)(2,1)S(1)}, u32[]{:S(2)}, u32[]{:S(2)}) collective-permute-start(bf16[256,512]{1,0:T(8,128)(2,1)S(1)} %collective-permute-done.20.refs_0_), channel_id=1, source_target_pairs={{0,2},{1,3},{2,4},{3,5},{4,6},{5,7},{6,0},{7,1},{8,10},{9,11},{10,... | collective-permute-start | bytes 786440 | tf_op jit(solution)/shard_map/ppermute | solution.py:538
  109.5 3.0 %collective-permute-start.18 = (bf16[256,288]{1,0:T(8,128)(2,1)S(1)}, bf16[256,288]{1,0:T(8,128)(2,1)S(1)}, u32[]{:S(2)}, u32[]{:S(2)}) collective-permute-start(bf16[256,288]{1,0:T(8,128)(2,1)S(1)} %add_convert_fusion.1), channel_id=1, source_target_pairs={{0,2},{1,3},{2,0},{3,1},{4,6},{5,7},{6,4},{7,5},{8,10},{9,11},{10,... | collective-permute-start | bytes 442376 | tf_op jit(solution)/shard_map/ppermute | solution.py:542
  116.3 2.8 %collective-permute-done.21.value_ref.refs_0_ = bf16[256,512]{1,0:T(8,128)(2,1)S(1)} collective-permute-done((bf16[256,512]{1,0:T(8,128)(2,1)S(1)}, bf16[256,512]{1,0:T(8,128)(2,1)S(1)}, u32[]{:S(2)}, u32[]{:S(2)}) %collective-permute-start.21) | collective-permute-done | bytes 262176 | tf_op jit(solution)/shard_map/ppermute | solution.py:538
  128.7 3.5 %collective-permute-done.19.arrived_ref = bf16[256,288]{1,0:T(8,128)(2,1)S(1)} collective-permute-done((bf16[256,288]{1,0:T(8,128)(2,1)S(1)}, bf16[256,288]{1,0:T(8,128)(2,1)S(1)}, u32[]{:S(2)}, u32[]{:S(2)}) %collective-permute-start.19) | collective-permute-done | bytes 147488 | tf_op jit(solution)/shard_map/ppermute | solution.py:542
  132.3 8.8 %local_scan.3 = (f32[6152,128]{1,0:T(8,128)S(1)}, f32[6152,128]{1,0:T(8,128)S(1)}, bf16[17,8,128]{2,1,0:T(8,128)(2,1)S(1)}) custom-call(f32[256,32]{1,0:T(8,128)S(1)} %get-tuple-element.109.sel_ref, f32[256,288]{1,0:T(8,128)S(1)} %get-tuple-element.110.low_ref, f32[256,1]{1,0:T(8,128)S(1)} %get-tuple-element.108.refs_0_.square_ref.refs_4_, ...), custom_call_target="tpu_custom_call" | custom-call | flops 1 | bytes 1 | tf_op jit(solution)/shard_map/local_scan/pallas_call | solution.py:352
  141.0 5.4 %all-gather.1 = bf16[68,8,128]{2,1,0:T(8,128)(2,1)S(1)} all-gather(bf16[17,8,128]{2,1,0:T(8,128)(2,1)S(1)} %get-tuple-element.115), channel_id=3, replica_groups=mesh['seq'=4,'tp'=8] {'seq'}, dimensions={0}, use_global_device_ids=true | all-gather | bytes 174080 | tf_op jit(solution)/shard_map/all_gather | solution.py:666
  146.5 7.5 %close_layer.3 = (bf16[256,1024]{1,0:T(8,128)(2,1)S(1)}, bf16[256,512]{1,0:T(8,128)(2,1)S(1)}) custom-call(s32[16]{0:T(128)S(1)} %pad_add_fusion.table_ref, s32[1]{0:T(128)} %bitcast.place_ref, f32[256,32]{1,0:T(8,128)S(1)} %get-tuple-element.109.sel_ref, f32[6152,128]{1,0:T(8,128)S(1)} %get-tuple-element.112.refs_0_, ...), custom_call_target="tpu_custom_call" | custom-call | flops 1 | bytes 1 | tf_op jit(solution)/shard_map/close_layer/pallas_call | solution.py:442
  154.2 3.6 %expand.7 = (bf16[256,512]{1,0:T(8,128)(2,1)S(1)}, bf16[256,512]{1,0:T(8,128)(2,1)S(1)}, bf16[256,512]{1,0:T(8,128)(2,1)S(1)}, bf16[256,512]{1,0:T(8,128)(2,1)S(1)}) custom-call(s32[16]{0:T(128)S(1)} %pad_add_fusion.table_ref, bf16[256,1024]{1,0:T(8,128)(2,1)S(1)} %get-tuple-element.116.gated_ref, bf16[2,1024,4096]{2,1,0:T(8,128)(2,1)} %w_ref.7), custom_call_target="tpu_custom_call" | custom-call | flops 1 | bytes 1 | tf_op jit(solution)/shard_map/expand/pallas_call | solution.py:468
  159.9 3.3 %collective-permute-done.28.refs_1_ = bf16[256,512]{1,0:T(8,128)(2,1)S(1)} collective-permute-done((bf16[256,512]{1,0:T(8,128)(2,1)S(1)}, bf16[256,512]{1,0:T(8,128)(2,1)S(1)}, u32[]{:S(2)}, u32[]{:S(2)}) %collective-permute-start.28) | collective-permute-done | bytes 262176 | tf_op jit(solution)/shard_map/ppermute | solution.py:538
  163.3 3.1 %expand.6 = (bf16[256,512]{1,0:T(8,128)(2,1)S(1)}, bf16[256,512]{1,0:T(8,128)(2,1)S(1)}, bf16[256,512]{1,0:T(8,128)(2,1)S(1)}) custom-call(s32[16]{0:T(128)S(1)} %pad_add_fusion.table_ref, bf16[256,1024]{1,0:T(8,128)(2,1)S(1)} %get-tuple-element.116.gated_ref, bf16[2,1024,4096]{2,1,0:T(8,128)(2,1)} %w_ref.7), custom_call_target="tpu_custom_call" | custom-call | flops 1 | bytes 1 | tf_op jit(solution)/shard_map/expand/pallas_call | solution.py:468
  170.6 3.9 %collective-permute-done.27.refs_1_ = bf16[256,512]{1,0:T(8,128)(2,1)S(1)} collective-permute-done((bf16[256,512]{1,0:T(8,128)(2,1)S(1)}, bf16[256,512]{1,0:T(8,128)(2,1)S(1)}, u32[]{:S(2)}, u32[]{:S(2)}) %collective-permute-start.27) | collective-permute-done | bytes 262176 | tf_op jit(solution)/shard_map/ppermute | solution.py:538
  174.6 4.9 %collective-permute-done.26.refs_2_ = bf16[256,512]{1,0:T(8,128)(2,1)S(1)} collective-permute-done((bf16[256,512]{1,0:T(8,128)(2,1)S(1)}, bf16[256,512]{1,0:T(8,128)(2,1)S(1)}, u32[]{:S(2)}, u32[]{:S(2)}) %collective-permute-start.26) | collective-permute-done | bytes 262176 | tf_op jit(solution)/shard_map/ppermute | solution.py:538
  179.5 4.2 %collective-permute-done.30.refs_3_ = bf16[256,512]{1,0:T(8,128)(2,1)S(1)} collective-permute-done((bf16[256,512]{1,0:T(8,128)(2,1)S(1)}, bf16[256,512]{1,0:T(8,128)(2,1)S(1)}, u32[]{:S(2)}, u32[]{:S(2)}) %collective-permute-start.30) | collective-permute-done | bytes 262176 | tf_op jit(solution)/shard_map/ppermute | solution.py:538
  (98 shorter events, 53.5 us)
Async XLA Ops:
  0.0 13.2 %collective-permute-start = (bf16[256,512]{1,0:T(8,128)(2,1)}, bf16[256,512]{1,0:T(8,128)(2,1)S(1)}, u32[]{:S(2)}, u32[]{:S(2)}) collective-permute-start(bf16[256,512]{1,0:T(8,128)(2,1)} %refs_0_.3), channel_id=1, source_target_pairs={{0,1},{1,0},{2,3},{3,2},{4,5},{5,4},{6,7},{7,6},{8,9},{9,8},{10,11... | collective-permute-start | bytes 786440 | tf_op jit(solution)/shard_map/ppermute | solution.py:538
  3.0 11.5 %collective-permute-start.4 = (bf16[256,512]{1,0:T(8,128)(2,1)}, bf16[256,512]{1,0:T(8,128)(2,1)S(1)}, u32[]{:S(2)}, u32[]{:S(2)}) collective-permute-start(bf16[256,512]{1,0:T(8,128)(2,1)} %refs_0_.3), channel_id=1, source_target_pairs={{0,2},{1,3},{2,4},{3,5},{4,6},{5,7},{6,0},{7,1},{8,10},{9,11},{10,... | collective-permute-start | bytes 786440 | tf_op jit(solution)/shard_map/ppermute | solution.py:538
  4.5 15.7 %collective-permute-start.7 = (bf16[256,512]{1,0:T(8,128)(2,1)}, bf16[256,512]{1,0:T(8,128)(2,1)S(1)}, u32[]{:S(2)}, u32[]{:S(2)}) collective-permute-start(bf16[256,512]{1,0:T(8,128)(2,1)} %refs_0_.3), channel_id=1, source_target_pairs={{0,6},{1,7},{2,0},{3,1},{4,2},{5,3},{6,4},{7,5},{8,14},{9,15},{10,... | collective-permute-start | bytes 786440 | tf_op jit(solution)/shard_map/ppermute | solution.py:538
  14.1 7.9 %collective-permute-start.1 = (bf16[256,288]{1,0:T(8,128)(2,1)S(1)}, bf16[256,288]{1,0:T(8,128)(2,1)S(1)}, u32[]{:S(2)}, u32[]{:S(2)}) collective-permute-start(bf16[256,288]{1,0:T(8,128)(2,1)S(1)} %project_low.2), channel_id=1, source_target_pairs={{0,1},{1,0},{2,3},{3,2},{4,5},{5,4},{6,7},{7,6},{8,9},{9,8},{10,11... | collective-permute-start | bytes 442376 | tf_op jit(solution)/shard_map/ppermute | solution.py:538
  14.5 10.2 %collective-permute-start.5 = (bf16[256,512]{1,0:T(8,128)(2,1)S(1)}, bf16[256,512]{1,0:T(8,128)(2,1)S(1)}, u32[]{:S(2)}, u32[]{:S(2)}) collective-permute-start(bf16[256,512]{1,0:T(8,128)(2,1)S(1)} %collective-permute-done.4.refs_0_), channel_id=1, source_target_pairs={{0,2},{1,3},{2,4},{3,5},{4,6},{5,7},{6,0},{7,1},{8,10},{9,11},{10,... | collective-permute-start | bytes 786440 | tf_op jit(solution)/shard_map/ppermute | solution.py:538
  14.5 13.2 %collective-permute-start.9 = (bf16[256,512]{1,0:T(8,128)(2,1)S(1)}, bf16[256,512]{1,0:T(8,128)(2,1)S(1)}, u32[]{:S(2)}, u32[]{:S(2)}) collective-permute-start(bf16[256,512]{1,0:T(8,128)(2,1)S(1)} %collective-permute-done.4.refs_0_), channel_id=1, source_target_pairs={{0,1},{1,0},{2,3},{3,2},{4,5},{5,4},{6,7},{7,6},{8,9},{9,8},{10,11... | collective-permute-start | bytes 786440 | tf_op jit(solution)/shard_map/ppermute | solution.py:538
  20.2 13.0 %collective-permute-start.8 = (bf16[256,512]{1,0:T(8,128)(2,1)S(1)}, bf16[256,512]{1,0:T(8,128)(2,1)S(1)}, u32[]{:S(2)}, u32[]{:S(2)}) collective-permute-start(bf16[256,512]{1,0:T(8,128)(2,1)S(1)} %collective-permute-done.7.refs_0_), channel_id=1, source_target_pairs={{0,1},{1,0},{2,3},{3,2},{4,5},{5,4},{6,7},{7,6},{8,9},{9,8},{10,11... | collective-permute-start | bytes 786440 | tf_op jit(solution)/shard_map/ppermute | solution.py:538
  22.1 9.3 %collective-permute-start.2 = (bf16[256,288]{1,0:T(8,128)(2,1)S(1)}, bf16[256,288]{1,0:T(8,128)(2,1)S(1)}, u32[]{:S(2)}, u32[]{:S(2)}) collective-permute-start(bf16[256,288]{1,0:T(8,128)(2,1)S(1)} %add_convert_fusion.3.refs_7_), channel_id=1, source_target_pairs={{0,2},{1,3},{2,0},{3,1},{4,6},{5,7},{6,4},{7,5},{8,10},{9,11},{10,... | collective-permute-start | bytes 442376 | tf_op jit(solution)/shard_map/ppermute | solution.py:542
  24.7 12.4 %collective-permute-start.6 = (bf16[256,512]{1,0:T(8,128)(2,1)S(1)}, bf16[256,512]{1,0:T(8,128)(2,1)S(1)}, u32[]{:S(2)}, u32[]{:S(2)}) collective-permute-start(bf16[256,512]{1,0:T(8,128)(2,1)S(1)} %relay.3), channel_id=1, source_target_pairs={{0,1},{1,0},{2,3},{3,2},{4,5},{5,4},{6,7},{7,6},{8,9},{9,8},{10,11... | collective-permute-start | bytes 786440 | tf_op jit(solution)/shard_map/ppermute | solution.py:538
  31.5 9.4 %collective-permute-start.3 = (bf16[256,288]{1,0:T(8,128)(2,1)S(1)}, bf16[256,288]{1,0:T(8,128)(2,1)S(1)}, u32[]{:S(2)}, u32[]{:S(2)}) collective-permute-start(bf16[256,288]{1,0:T(8,128)(2,1)S(1)} %add_convert_fusion.2.refs_7_.own_ref), channel_id=1, source_target_pairs={{0,4},{1,5},{2,6},{3,7},{4,0},{5,1},{6,2},{7,3},{8,12},{9,13},{10,... | collective-permute-start | bytes 442376 | tf_op jit(solution)/shard_map/ppermute | solution.py:542
  62.9 9.2 %collective-permute-start.12 = (bf16[256,512]{1,0:T(8,128)(2,1)S(1)}, bf16[256,512]{1,0:T(8,128)(2,1)S(1)}, u32[]{:S(2)}, u32[]{:S(2)}) collective-permute-start(bf16[256,512]{1,0:T(8,128)(2,1)S(1)} %get-tuple-element.89), channel_id=1, source_target_pairs={{0,1},{1,0},{2,3},{3,2},{4,5},{5,4},{6,7},{7,6},{8,9},{9,8},{10,11... | collective-permute-start | bytes 786440 | tf_op jit(solution)/shard_map/ppermute | solution.py:538
  67.1 12.4 %collective-permute-start.15 = (bf16[256,512]{1,0:T(8,128)(2,1)S(1)}, bf16[256,512]{1,0:T(8,128)(2,1)S(1)}, u32[]{:S(2)}, u32[]{:S(2)}) collective-permute-start(bf16[256,512]{1,0:T(8,128)(2,1)S(1)} %get-tuple-element.92), channel_id=1, source_target_pairs={{0,1},{1,0},{2,3},{3,2},{4,5},{5,4},{6,7},{7,6},{8,9},{9,8},{10,11... | collective-permute-start | bytes 786440 | tf_op jit(solution)/shard_map/ppermute | solution.py:538
  68.6 14.7 %collective-permute-start.11 = (bf16[256,512]{1,0:T(8,128)(2,1)S(1)}, bf16[256,512]{1,0:T(8,128)(2,1)S(1)}, u32[]{:S(2)}, u32[]{:S(2)}) collective-permute-start(bf16[256,512]{1,0:T(8,128)(2,1)S(1)} %get-tuple-element.87), channel_id=1, source_target_pairs={{0,1},{1,0},{2,3},{3,2},{4,5},{5,4},{6,7},{7,6},{8,9},{9,8},{10,11... | collective-permute-start | bytes 786440 | tf_op jit(solution)/shard_map/ppermute | solution.py:538
  72.1 11.2 %collective-permute-start.13 = (bf16[256,512]{1,0:T(8,128)(2,1)S(1)}, bf16[256,512]{1,0:T(8,128)(2,1)S(1)}, u32[]{:S(2)}, u32[]{:S(2)}) collective-permute-start(bf16[256,512]{1,0:T(8,128)(2,1)S(1)} %combine.8.refs_0_), channel_id=1, source_target_pairs={{0,2},{1,3},{2,4},{3,5},{4,6},{5,7},{6,0},{7,1},{8,10},{9,11},{10,... | collective-permute-start | bytes 786440 | tf_op jit(solution)/shard_map/ppermute | solution.py:538
  76.0 14.3 %collective-permute-start.10 = (bf16[256,512]{1,0:T(8,128)(2,1)S(1)}, bf16[256,512]{1,0:T(8,128)(2,1)S(1)}, u32[]{:S(2)}, u32[]{:S(2)}) collective-permute-start(bf16[256,512]{1,0:T(8,128)(2,1)S(1)} %get-tuple-element.85), channel_id=1, source_target_pairs={{0,1},{1,0},{2,3},{3,2},{4,5},{5,4},{6,7},{7,6},{8,9},{9,8},{10,11... | collective-permute-start | bytes 786440 | tf_op jit(solution)/shard_map/ppermute | solution.py:538
  79.6 10.7 %collective-permute-start.16 = (bf16[256,512]{1,0:T(8,128)(2,1)S(1)}, bf16[256,512]{1,0:T(8,128)(2,1)S(1)}, u32[]{:S(2)}, u32[]{:S(2)}) collective-permute-start(bf16[256,512]{1,0:T(8,128)(2,1)S(1)} %combine.10.refs_0_), channel_id=1, source_target_pairs={{0,6},{1,7},{2,0},{3,1},{4,2},{5,3},{6,4},{7,5},{8,14},{9,15},{10,... | collective-permute-start | bytes 786440 | tf_op jit(solution)/shard_map/ppermute | solution.py:538
  83.4 10.1 %collective-permute-start.14 = (bf16[256,512]{1,0:T(8,128)(2,1)S(1)}, bf16[256,512]{1,0:T(8,128)(2,1)S(1)}, u32[]{:S(2)}, u32[]{:S(2)}) collective-permute-start(bf16[256,512]{1,0:T(8,128)(2,1)S(1)} %combine.9), channel_id=1, source_target_pairs={{0,2},{1,3},{2,4},{3,5},{4,6},{5,7},{6,0},{7,1},{8,10},{9,11},{10,... | collective-permute-start | bytes 786440 | tf_op jit(solution)/shard_map/ppermute | solution.py:538
  94.5 14.9 %collective-permute-start.17 = (bf16[256,800]{1,0:T(8,128)(2,1)S(1)}, bf16[256,800]{1,0:T(8,128)(2,1)S(1)}, u32[]{:S(2)}, u32[]{:S(2)}) collective-permute-start(bf16[256,800]{1,0:T(8,128)(2,1)S(1)} %project_low.3), channel_id=1, source_target_pairs={{0,1},{1,0},{2,3},{3,2},{4,5},{5,4},{6,7},{7,6},{8,9},{9,8},{10,11... | collective-permute-start | bytes 1228808 | tf_op jit(solution)/shard_map/ppermute | solution.py:538
  96.0 10.4 %collective-permute-start.20 = (bf16[256,512]{1,0:T(8,128)(2,1)S(1)}, bf16[256,512]{1,0:T(8,128)(2,1)S(1)}, u32[]{:S(2)}, u32[]{:S(2)}) collective-permute-start(bf16[256,512]{1,0:T(8,128)(2,1)S(1)} %combine.11.rows_ref.refs_0_), channel_id=1, source_target_pairs={{0,2},{1,3},{2,4},{3,5},{4,6},{5,7},{6,0},{7,1},{8,10},{9,11},{10,... | collective-permute-start | bytes 786440 | tf_op jit(solution)/shard_map/ppermute | solution.py:538
  101.2 13.5 %collective-permute-start.23 = (bf16[256,512]{1,0:T(8,128)(2,1)S(1)}, bf16[256,512]{1,0:T(8,128)(2,1)S(1)}, u32[]{:S(2)}, u32[]{:S(2)}) collective-permute-start(bf16[256,512]{1,0:T(8,128)(2,1)S(1)} %combine.11.rows_ref.refs_0_), channel_id=1, source_target_pairs={{0,6},{1,7},{2,0},{3,1},{4,2},{5,3},{6,4},{7,5},{8,14},{9,15},{10,... | collective-permute-start | bytes 786440 | tf_op jit(solution)/shard_map/ppermute | solution.py:538
  106.4 12.7 %collective-permute-start.21 = (bf16[256,512]{1,0:T(8,128)(2,1)S(1)}, bf16[256,512]{1,0:T(8,128)(2,1)S(1)}, u32[]{:S(2)}, u32[]{:S(2)}) collective-permute-start(bf16[256,512]{1,0:T(8,128)(2,1)S(1)} %collective-permute-done.20.refs_0_), channel_id=1, source_target_pairs={{0,2},{1,3},{2,4},{3,5},{4,6},{5,7},{6,0},{7,1},{8,10},{9,11},{10,... | collective-permute-start | bytes 786440 | tf_op jit(solution)/shard_map/ppermute | solution.py:538
  109.3 12.6 %collective-permute-start.25 = (bf16[256,512]{1,0:T(8,128)(2,1)S(1)}, bf16[256,512]{1,0:T(8,128)(2,1)S(1)}, u32[]{:S(2)}, u32[]{:S(2)}) collective-permute-start(bf16[256,512]{1,0:T(8,128)(2,1)S(1)} %collective-permute-done.20.refs_0_), channel_id=1, source_target_pairs={{0,1},{1,0},{2,3},{3,2},{4,5},{5,4},{6,7},{7,6},{8,9},{9,8},{10,11... | collective-permute-start | bytes 786440 | tf_op jit(solution)/shard_map/ppermute | solution.py:538
  109.5 11.7 %collective-permute-start.18 = (bf16[256,288]{1,0:T(8,128)(2,1)S(1)}, bf16[256,288]{1,0:T(8,128)(2,1)S(1)}, u32[]{:S(2)}, u32[]{:S(2)}) collective-permute-start(bf16[256,288]{1,0:T(8,128)(2,1)S(1)} %add_convert_fusion.1), channel_id=1, source_target_pairs={{0,2},{1,3},{2,0},{3,1},{4,6},{5,7},{6,4},{7,5},{8,10},{9,11},{10,... | collective-permute-start | bytes 442376 | tf_op jit(solution)/shard_map/ppermute | solution.py:542
  114.7 9.3 %collective-permute-start.24 = (bf16[256,512]{1,0:T(8,128)(2,1)S(1)}, bf16[256,512]{1,0:T(8,128)(2,1)S(1)}, u32[]{:S(2)}, u32[]{:S(2)}) collective-permute-start(bf16[256,512]{1,0:T(8,128)(2,1)S(1)} %relay.5), channel_id=1, source_target_pairs={{0,1},{1,0},{2,3},{3,2},{4,5},{5,4},{6,7},{7,6},{8,9},{9,8},{10,11... | collective-permute-start | bytes 786440 | tf_op jit(solution)/shard_map/ppermute | solution.py:538
  121.2 11.0 %collective-permute-start.19 = (bf16[256,288]{1,0:T(8,128)(2,1)S(1)}, bf16[256,288]{1,0:T(8,128)(2,1)S(1)}, u32[]{:S(2)}, u32[]{:S(2)}) collective-permute-start(bf16[256,288]{1,0:T(8,128)(2,1)S(1)} %add_convert_fusion.refs_7_.own_ref), channel_id=1, source_target_pairs={{0,4},{1,5},{2,6},{3,7},{4,0},{5,1},{6,2},{7,3},{8,12},{9,13},{10,... | collective-permute-start | bytes 442376 | tf_op jit(solution)/shard_map/ppermute | solution.py:542
  154.0 9.2 %collective-permute-start.28 = (bf16[256,512]{1,0:T(8,128)(2,1)S(1)}, bf16[256,512]{1,0:T(8,128)(2,1)S(1)}, u32[]{:S(2)}, u32[]{:S(2)}) collective-permute-start(bf16[256,512]{1,0:T(8,128)(2,1)S(1)} %get-tuple-element.122), channel_id=1, source_target_pairs={{0,1},{1,0},{2,3},{3,2},{4,5},{5,4},{6,7},{7,6},{8,9},{9,8},{10,11... | collective-permute-start | bytes 786440 | tf_op jit(solution)/shard_map/ppermute | solution.py:538
  157.8 11.0 %collective-permute-start.31 = (bf16[256,512]{1,0:T(8,128)(2,1)S(1)}, bf16[256,512]{1,0:T(8,128)(2,1)S(1)}, u32[]{:S(2)}, u32[]{:S(2)}) collective-permute-start(bf16[256,512]{1,0:T(8,128)(2,1)S(1)} %get-tuple-element.124), channel_id=1, source_target_pairs={{0,1},{1,0},{2,3},{3,2},{4,5},{5,4},{6,7},{7,6},{8,9},{9,8},{10,11... | collective-permute-start | bytes 786440 | tf_op jit(solution)/shard_map/ppermute | solution.py:538
  159.7 14.7 %collective-permute-start.27 = (bf16[256,512]{1,0:T(8,128)(2,1)S(1)}, bf16[256,512]{1,0:T(8,128)(2,1)S(1)}, u32[]{:S(2)}, u32[]{:S(2)}) collective-permute-start(bf16[256,512]{1,0:T(8,128)(2,1)S(1)} %get-tuple-element.120), channel_id=1, source_target_pairs={{0,1},{1,0},{2,3},{3,2},{4,5},{5,4},{6,7},{7,6},{8,9},{9,8},{10,11... | collective-permute-start | bytes 786440 | tf_op jit(solution)/shard_map/ppermute | solution.py:538
  163.3 11.2 %collective-permute-start.29 = (bf16[256,512]{1,0:T(8,128)(2,1)S(1)}, bf16[256,512]{1,0:T(8,128)(2,1)S(1)}, u32[]{:S(2)}, u32[]{:S(2)}) collective-permute-start(bf16[256,512]{1,0:T(8,128)(2,1)S(1)} %combine.12), channel_id=1, source_target_pairs={{0,2},{1,3},{2,4},{3,5},{4,6},{5,7},{6,0},{7,1},{8,10},{9,11},{10,... | collective-permute-start | bytes 786440 | tf_op jit(solution)/shard_map/ppermute | solution.py:538
  166.4 13.0 %collective-permute-start.26 = (bf16[256,512]{1,0:T(8,128)(2,1)S(1)}, bf16[256,512]{1,0:T(8,128)(2,1)S(1)}, u32[]{:S(2)}, u32[]{:S(2)}) collective-permute-start(bf16[256,512]{1,0:T(8,128)(2,1)S(1)} %get-tuple-element.118), channel_id=1, source_target_pairs={{0,1},{1,0},{2,3},{3,2},{4,5},{5,4},{6,7},{7,6},{8,9},{9,8},{10,11... | collective-permute-start | bytes 786440 | tf_op jit(solution)/shard_map/ppermute | solution.py:538
  168.9 10.6 %collective-permute-start.32 = (bf16[256,512]{1,0:T(8,128)(2,1)S(1)}, bf16[256,512]{1,0:T(8,128)(2,1)S(1)}, u32[]{:S(2)}, u32[]{:S(2)}) collective-permute-start(bf16[256,512]{1,0:T(8,128)(2,1)S(1)} %combine.14), channel_id=1, source_target_pairs={{0,6},{1,7},{2,0},{3,1},{4,2},{5,3},{6,4},{7,5},{8,14},{9,15},{10,... | collective-permute-start | bytes 786440 | tf_op jit(solution)/shard_map/ppermute | solution.py:538
  174.5 9.1 %collective-permute-start.30 = (bf16[256,512]{1,0:T(8,128)(2,1)S(1)}, bf16[256,512]{1,0:T(8,128)(2,1)S(1)}, u32[]{:S(2)}, u32[]{:S(2)}) collective-permute-start(bf16[256,512]{1,0:T(8,128)(2,1)S(1)} %combine.13), channel_id=1, source_target_pairs={{0,2},{1,3},{2,4},{3,5},{4,6},{5,7},{6,0},{7,1},{8,10},{9,11},{10,... | collective-permute-start | bytes 786440 | tf_op jit(solution)/shard_map/ppermute | solution.py:538
  (10 other events, 72.0 us)

commit v4 on v0

--- a/solution.py
+++ b/solution.py
@@ -339,7 +339,7 @@
         return time, tuple(after)
 
     zero = jnp.zeros((fold, LANES), F32)
-    time, held = lax.fori_loop(0, rows, advance, (zero, (zero,) * states), unroll=8)
+    time, held = lax.fori_loop(0, rows, advance, (zero, (zero,) * states), unroll=16)
     for s in range(states):
         final_ref[s] = held[s].astype(BF16)
     final_ref[states] = time.astype(BF16)
@@ -415,7 +415,7 @@
             mixed_s[here, :] = (sums[0] + sums[1]) + (sums[2] + sums[3])
             return carried
 
-        lax.fori_loop(0, rows, correct, 0, unroll=8)
+        lax.fori_loop(0, rows, correct, 0, unroll=16)
 
         factor = row_factor(square_ref[...], width)
         for r in range(fold):

time: 183 us -> 183 us (level)
  no operation moved by 1% of the time
where the time goes in v4:
time: 183 us; the launch traced here: 182 us
  Pallas kernels  84.8 us (46%)
  waiting for transfers between devices  41.2 us (23%)
  starting transfers between devices  40.6 us (22%)
  blocking collectives  10.9 us (6%)
  local copies, waits for them, and re-layouts  4.23 us (2%)
    ppermute x29, waiting for transfers between devices, send(): return lax.ppermute(value, 'tp', pairs)  35.4 us
    ppermute x29, starting transfers between devices, send(): return lax.ppermute(value, 'tp', pairs)  33.4 us
    pallas_call x2, Pallas kernels, local_scan(): pl.pallas_call(functools.partial(scan_kernel, layer, states, width), out_...  17.1 us
    pallas_call x5, Pallas kernels, unpack(): pl.pallas_call(functools.partial(unpack_kernel, count, layer, table_at, w...  15.8 us
    pallas_call x2, Pallas kernels, close_layer(): pl.pallas_call(functools.partial(close_kernel, layer, states, table_at, f...  14.8 us
    pallas_call x4, Pallas kernels, expand(): pl.pallas_call(functools.partial(expand_kernel, layer, table_at, feat), o...  13.3 us
    pallas_call x3, Pallas kernels, project(): pl.pallas_call(functools.partial(proj_kernel, count, before is None, laye...  11.3 us
    all_gather x2, blocking collectives, per_device(): finals = lax.all_gather(final, 'seq')  10.9 us
  transfers between devices with their start and end apart: 33, of which 17 were waited for; matrix products, arithmetic and copies ran while one was open for 0% of the time, Pallas kernels for 28%

profile of v4, /device:TPU:0, one launch (start us, length us, event | category | flops | bytes accessed | tf_op | source)
XLA Modules:
  0.0 182.5 jit_solution(10441078802562977126)
XLA Ops:
  0.0 3.0 %collective-permute-start = (bf16[256,512]{1,0:T(8,128)(2,1)}, bf16[256,512]{1,0:T(8,128)(2,1)S(1)}, u32[]{:S(2)}, u32[]{:S(2)}) collective-permute-start(bf16[256,512]{1,0:T(8,128)(2,1)} %refs_0_.3), channel_id=1, source_target_pairs={{0,1},{1,0},{2,3},{3,2},{4,5},{5,4},{6,7},{7,6},{8,9},{9,8},{10,11... | collective-permute-start | bytes 786440 | tf_op jit(solution)/shard_map/ppermute | solution.py:538
  6.9 3.3 %unpack.5 = (bf16[2,1024,1024]{2,1,0:T(8,128)(2,1)S(1)}, f32[8,128]{1,0:T(8,128)}) custom-call(s32[16]{0:T(128)S(1)} %pad_add_fusion.table_ref, bf16[2,65536,128]{2,1,0:T(8,128)(2,1)} %bitcast.21), custom_call_target="tpu_custom_call" | custom-call | flops 1 | bytes 1 | tf_op jit(solution)/shard_map/unpack/pallas_call | solution.py:175
  21.2 3.4 %collective-permute-start.2 = (bf16[256,288]{1,0:T(8,128)(2,1)S(1)}, bf16[256,288]{1,0:T(8,128)(2,1)S(1)}, u32[]{:S(2)}, u32[]{:S(2)}) collective-permute-start(bf16[256,288]{1,0:T(8,128)(2,1)S(1)} %add_convert_fusion.3.refs_7_), channel_id=1, source_target_pairs={{0,2},{1,3},{2,0},{3,1},{4,6},{5,7},{6,4},{7,5},{8,10},{9,11},{10,... | collective-permute-start | bytes 442376 | tf_op jit(solution)/shard_map/ppermute | solution.py:542
  26.7 3.8 %project.3 = (f32[256,1024]{1,0:T(8,128)S(1)}, f32[256,1024]{1,0:T(8,128)S(1)}, f32[256,1]{1,0:T(8,128)S(1)}) custom-call(s32[16]{0:T(128)S(1)} %pad_add_fusion.table_ref, bf16[256,512]{1,0:T(8,128)(2,1)S(1)} %collective-permute-done.4.refs_0_, ...), custom_call_target="tpu_custom_call", output_to_operand_aliasing={{0}: (5, {}), {1}: (6, {}), {2}: (7, {})} | custom-call | flops 10000000000 | bytes 1 | tf_op jit(solution)/shard_map/project/pallas_call | solution.py:118
  32.7 3.8 %project.4 = (f32[256,1024]{1,0:T(8,128)S(1)}, f32[256,1024]{1,0:T(8,128)S(1)}, f32[256,1]{1,0:T(8,128)S(1)}) custom-call(s32[16]{0:T(128)S(1)} %pad_add_fusion.table_ref, bf16[256,512]{1,0:T(8,128)(2,1)S(1)} %collective-permute-done.7.refs_0_, ...), custom_call_target="tpu_custom_call", output_to_operand_aliasing={{0}: (5, {}), {1}: (6, {}), {2}: (7, {})} | custom-call | flops 10000000000 | bytes 1 | tf_op jit(solution)/shard_map/project/pallas_call | solution.py:118
  36.5 3.8 %project.5 = (f32[256,1024]{1,0:T(8,128)S(1)}, f32[256,1024]{1,0:T(8,128)S(1)}, f32[256,1]{1,0:T(8,128)S(1)}) custom-call(s32[16]{0:T(128)S(1)} %pad_add_fusion.table_ref, bf16[256,512]{1,0:T(8,128)(2,1)S(1)} %collective-permute-done.5.value_ref.refs_0_, ...), custom_call_target="tpu_custom_call", output_to_operand_aliasing={{0}: (5, {}), {1}: (6, {}), {2}: (7, {})} | custom-call | flops 10000000000 | bytes 1 | tf_op jit(solution)/shard_map/project/pallas_call | solution.py:118
  40.4 8.5 %local_scan.2 = (f32[6152,128]{1,0:T(8,128)S(1)}, f32[6152,128]{1,0:T(8,128)S(1)}, bf16[17,8,128]{2,1,0:T(8,128)(2,1)S(1)}) custom-call(f32[256,32]{1,0:T(8,128)S(1)} %get-tuple-element.76.sel_ref, f32[256,288]{1,0:T(8,128)S(1)} %get-tuple-element.77.low_ref, f32[256,1]{1,0:T(8,128)S(1)} %get-tuple-element.75.refs_0_.square_ref.refs_4_, ...), custom_call_target="tpu_custom_call" | custom-call | flops 1 | bytes 1 | tf_op jit(solution)/shard_map/local_scan/pallas_call | solution.py:352
  48.9 5.4 %all-gather = bf16[68,8,128]{2,1,0:T(8,128)(2,1)S(1)} all-gather(bf16[17,8,128]{2,1,0:T(8,128)(2,1)S(1)} %get-tuple-element.82), channel_id=2, replica_groups=mesh['seq'=4,'tp'=8] {'seq'}, dimensions={0}, use_global_device_ids=true | all-gather | bytes 174080 | tf_op jit(solution)/shard_map/all_gather | solution.py:666
  54.4 7.5 %close_layer.2 = (bf16[256,1024]{1,0:T(8,128)(2,1)S(1)}, bf16[256,512]{1,0:T(8,128)(2,1)S(1)}) custom-call(s32[16]{0:T(128)S(1)} %pad_add_fusion.table_ref, s32[1]{0:T(128)} %bitcast.place_ref, f32[256,32]{1,0:T(8,128)S(1)} %get-tuple-element.76.sel_ref, f32[6152,128]{1,0:T(8,128)S(1)} %get-tuple-element.79.refs_0_, ...), custom_call_target="tpu_custom_call" | custom-call | flops 1 | bytes 1 | tf_op jit(solution)/shard_map/close_layer/pallas_call | solution.py:442
  62.4 3.6 %expand.5 = (bf16[256,512]{1,0:T(8,128)(2,1)S(1)}, bf16[256,512]{1,0:T(8,128)(2,1)S(1)}, bf16[256,512]{1,0:T(8,128)(2,1)S(1)}, bf16[256,512]{1,0:T(8,128)(2,1)S(1)}) custom-call(s32[16]{0:T(128)S(1)} %pad_add_fusion.table_ref, bf16[256,1024]{1,0:T(8,128)(2,1)S(1)} %get-tuple-element.83.gated_ref, bf16[2,1024,4096]{2,1,0:T(8,128)(2,1)} %w_ref.7), custom_call_target="tpu_custom_call" | custom-call | flops 1 | bytes 1 | tf_op jit(solution)/shard_map/expand/pallas_call | solution.py:468
  68.1 3.0 %collective-permute-done.12.refs_1_ = bf16[256,512]{1,0:T(8,128)(2,1)S(1)} collective-permute-done((bf16[256,512]{1,0:T(8,128)(2,1)S(1)}, bf16[256,512]{1,0:T(8,128)(2,1)S(1)}, u32[]{:S(2)}, u32[]{:S(2)}) %collective-permute-start.12) | collective-permute-done | bytes 262176 | tf_op jit(solution)/shard_map/ppermute | solution.py:538
  71.6 3.1 %expand.4 = (bf16[256,512]{1,0:T(8,128)(2,1)S(1)}, bf16[256,512]{1,0:T(8,128)(2,1)S(1)}, bf16[256,512]{1,0:T(8,128)(2,1)S(1)}) custom-call(s32[16]{0:T(128)S(1)} %pad_add_fusion.table_ref, bf16[256,1024]{1,0:T(8,128)(2,1)S(1)} %get-tuple-element.83.gated_ref, bf16[2,1024,4096]{2,1,0:T(8,128)(2,1)} %w_ref.7), custom_call_target="tpu_custom_call" | custom-call | flops 1 | bytes 1 | tf_op jit(solution)/shard_map/expand/pallas_call | solution.py:468
  75.5 3.0 %unpack.6 = (bf16[2,1024,1024]{2,1,0:T(8,128)(2,1)S(1)}, f32[8,128]{1,0:T(8,128)S(1)}) custom-call(s32[16]{0:T(128)S(1)} %pad_add_fusion.table_ref, bf16[2,65536,128]{2,1,0:T(8,128)(2,1)} %bitcast.25, bf16[256,512]{1,0:T(8,128)(2,1)S(1)} %combine.8.refs_0_), custom_call_target="tpu_custom_call" | custom-call | flops 1 | bytes 1 | tf_op jit(solution)/shard_map/unpack/pallas_call | solution.py:175
  78.6 3.3 %collective-permute-start.16 = (bf16[256,512]{1,0:T(8,128)(2,1)S(1)}, bf16[256,512]{1,0:T(8,128)(2,1)S(1)}, u32[]{:S(2)}, u32[]{:S(2)}) collective-permute-start(bf16[256,512]{1,0:T(8,128)(2,1)S(1)} %combine.10.refs_0_), channel_id=1, source_target_pairs={{0,6},{1,7},{2,0},{3,1},{4,2},{5,3},{6,4},{7,5},{8,14},{9,15},{10,... | collective-permute-start | bytes 786440 | tf_op jit(solution)/shard_map/ppermute | solution.py:538
  82.8 3.0 %unpack.7 = (bf16[2,1024,1024]{2,1,0:T(8,128)(2,1)S(1)}, f32[8,128]{1,0:T(8,128)S(1)}) custom-call(s32[16]{0:T(128)S(1)} %pad_add_fusion.table_ref, bf16[2,65536,128]{2,1,0:T(8,128)(2,1)} %bitcast.26, bf16[256,512]{1,0:T(8,128)(2,1)S(1)} %combine.10.refs_0_), custom_call_target="tpu_custom_call" | custom-call | flops 1 | bytes 1 | tf_op jit(solution)/shard_map/unpack/pallas_call | solution.py:175
  85.9 3.1 %unpack.8 = (bf16[2,1024,1024]{2,1,0:T(8,128)(2,1)S(1)}, f32[8,128]{1,0:T(8,128)S(1)}) custom-call(s32[16]{0:T(128)S(1)} %pad_add_fusion.table_ref, bf16[2,65536,128]{2,1,0:T(8,128)(2,1)} %bitcast.27, bf16[256,512]{1,0:T(8,128)(2,1)S(1)} %combine.10.refs_0_), custom_call_target="tpu_custom_call" | custom-call | flops 1 | bytes 1 | tf_op jit(solution)/shard_map/unpack/pallas_call | solution.py:175
  89.0 3.4 %collective-permute-done.14.refs_3_ = bf16[256,512]{1,0:T(8,128)(2,1)S(1)} collective-permute-done((bf16[256,512]{1,0:T(8,128)(2,1)S(1)}, bf16[256,512]{1,0:T(8,128)(2,1)S(1)}, u32[]{:S(2)}, u32[]{:S(2)}) %collective-permute-start.14) | collective-permute-done | bytes 262176 | tf_op jit(solution)/shard_map/ppermute | solution.py:538
  98.9 3.3 %unpack.9 = (bf16[2,1024,1024]{2,1,0:T(8,128)(2,1)S(1)}, f32[8,128]{1,0:T(8,128)}) custom-call(s32[16]{0:T(128)S(1)} %pad_add_fusion.table_ref, bf16[2,65536,128]{2,1,0:T(8,128)(2,1)} %bitcast.28, bf16[256,512]{1,0:T(8,128)(2,1)S(1)} %collective-permute-done.10.refs_2_.refs_0_), custom_call_target="tpu_custom_call" | custom-call | flops 1 | bytes 1 | tf_op jit(solution)/shard_map/unpack/pallas_call | solution.py:175
  102.2 3.9 %collective-permute-done.20.refs_0_ = bf16[256,512]{1,0:T(8,128)(2,1)S(1)} collective-permute-done((bf16[256,512]{1,0:T(8,128)(2,1)S(1)}, bf16[256,512]{1,0:T(8,128)(2,1)S(1)}, u32[]{:S(2)}, u32[]{:S(2)}) %collective-permute-start.20) | collective-permute-done | bytes 262176 | tf_op jit(solution)/shard_map/ppermute | solution.py:538
  108.5 3.2 %collective-permute-done.23.refs_0_ = bf16[256,512]{1,0:T(8,128)(2,1)S(1)} collective-permute-done((bf16[256,512]{1,0:T(8,128)(2,1)S(1)}, bf16[256,512]{1,0:T(8,128)(2,1)S(1)}, u32[]{:S(2)}, u32[]{:S(2)}) %collective-permute-start.23) | collective-permute-done | bytes 262176 | tf_op jit(solution)/shard_map/ppermute | solution.py:538
  115.0 5.0 %collective-permute-done.18 = bf16[256,288]{1,0:T(8,128)(2,1)S(1)} collective-permute-done((bf16[256,288]{1,0:T(8,128)(2,1)S(1)}, bf16[256,288]{1,0:T(8,128)(2,1)S(1)}, u32[]{:S(2)}, u32[]{:S(2)}) %collective-permute-start.18) | collective-permute-done | bytes 147488 | tf_op jit(solution)/shard_map/ppermute | solution.py:542
  125.3 2.7 %collective-permute-done.22.refs_1_ = bf16[256,512]{1,0:T(8,128)(2,1)S(1)} collective-permute-done((bf16[256,512]{1,0:T(8,128)(2,1)S(1)}, bf16[256,512]{1,0:T(8,128)(2,1)S(1)}, u32[]{:S(2)}, u32[]{:S(2)}) %collective-permute-start.22) | collective-permute-done | bytes 262176 | tf_op jit(solution)/shard_map/ppermute | solution.py:538
  130.7 8.5 %local_scan.3 = (f32[6152,128]{1,0:T(8,128)S(1)}, f32[6152,128]{1,0:T(8,128)S(1)}, bf16[17,8,128]{2,1,0:T(8,128)(2,1)S(1)}) custom-call(f32[256,32]{1,0:T(8,128)S(1)} %get-tuple-element.109.sel_ref, f32[256,288]{1,0:T(8,128)S(1)} %get-tuple-element.110.low_ref, f32[256,1]{1,0:T(8,128)S(1)} %get-tuple-element.108.refs_0_.square_ref.refs_4_, ...), custom_call_target="tpu_custom_call" | custom-call | flops 1 | bytes 1 | tf_op jit(solution)/shard_map/local_scan/pallas_call | solution.py:352
  139.2 5.4 %all-gather.1 = bf16[68,8,128]{2,1,0:T(8,128)(2,1)S(1)} all-gather(bf16[17,8,128]{2,1,0:T(8,128)(2,1)S(1)} %get-tuple-element.115), channel_id=3, replica_groups=mesh['seq'=4,'tp'=8] {'seq'}, dimensions={0}, use_global_device_ids=true | all-gather | bytes 174080 | tf_op jit(solution)/shard_map/all_gather | solution.py:666
  144.7 7.3 %close_layer.3 = (bf16[256,1024]{1,0:T(8,128)(2,1)S(1)}, bf16[256,512]{1,0:T(8,128)(2,1)S(1)}) custom-call(s32[16]{0:T(128)S(1)} %pad_add_fusion.table_ref, s32[1]{0:T(128)} %bitcast.place_ref, f32[256,32]{1,0:T(8,128)S(1)} %get-tuple-element.109.sel_ref, f32[6152,128]{1,0:T(8,128)S(1)} %get-tuple-element.112.refs_0_, ...), custom_call_target="tpu_custom_call" | custom-call | flops 1 | bytes 1 | tf_op jit(solution)/shard_map/close_layer/pallas_call | solution.py:442
  153.3 3.6 %expand.7 = (bf16[256,512]{1,0:T(8,128)(2,1)S(1)}, bf16[256,512]{1,0:T(8,128)(2,1)S(1)}, bf16[256,512]{1,0:T(8,128)(2,1)S(1)}, bf16[256,512]{1,0:T(8,128)(2,1)S(1)}) custom-call(s32[16]{0:T(128)S(1)} %pad_add_fusion.table_ref, bf16[256,1024]{1,0:T(8,128)(2,1)S(1)} %get-tuple-element.116.gated_ref, bf16[2,1024,4096]{2,1,0:T(8,128)(2,1)} %w_ref.7), custom_call_target="tpu_custom_call" | custom-call | flops 1 | bytes 1 | tf_op jit(solution)/shard_map/expand/pallas_call | solution.py:468
  158.9 2.3 %collective-permute-done.28.refs_1_ = bf16[256,512]{1,0:T(8,128)(2,1)S(1)} collective-permute-done((bf16[256,512]{1,0:T(8,128)(2,1)S(1)}, bf16[256,512]{1,0:T(8,128)(2,1)S(1)}, u32[]{:S(2)}, u32[]{:S(2)}) %collective-permute-start.28) | collective-permute-done | bytes 262176 | tf_op jit(solution)/shard_map/ppermute | solution.py:538
  161.4 3.1 %expand.6 = (bf16[256,512]{1,0:T(8,128)(2,1)S(1)}, bf16[256,512]{1,0:T(8,128)(2,1)S(1)}, bf16[256,512]{1,0:T(8,128)(2,1)S(1)}) custom-call(s32[16]{0:T(128)S(1)} %pad_add_fusion.table_ref, bf16[256,1024]{1,0:T(8,128)(2,1)S(1)} %get-tuple-element.116.gated_ref, bf16[2,1024,4096]{2,1,0:T(8,128)(2,1)} %w_ref.7), custom_call_target="tpu_custom_call" | custom-call | flops 1 | bytes 1 | tf_op jit(solution)/shard_map/expand/pallas_call | solution.py:468
  166.9 2.7 %collective-permute-start.32 = (bf16[256,512]{1,0:T(8,128)(2,1)S(1)}, bf16[256,512]{1,0:T(8,128)(2,1)S(1)}, u32[]{:S(2)}, u32[]{:S(2)}) collective-permute-start(bf16[256,512]{1,0:T(8,128)(2,1)S(1)} %combine.14), channel_id=1, source_target_pairs={{0,6},{1,7},{2,0},{3,1},{4,2},{5,3},{6,4},{7,5},{8,14},{9,15},{10,... | collective-permute-start | bytes 786440 | tf_op jit(solution)/shard_map/ppermute | solution.py:538
  169.7 2.8 %collective-permute-done.27.refs_1_ = bf16[256,512]{1,0:T(8,128)(2,1)S(1)} collective-permute-done((bf16[256,512]{1,0:T(8,128)(2,1)S(1)}, bf16[256,512]{1,0:T(8,128)(2,1)S(1)}, u32[]{:S(2)}, u32[]{:S(2)}) %collective-permute-start.27) | collective-permute-done | bytes 262176 | tf_op jit(solution)/shard_map/ppermute | solution.py:538
  172.6 4.9 %collective-permute-done.26.refs_2_ = bf16[256,512]{1,0:T(8,128)(2,1)S(1)} collective-permute-done((bf16[256,512]{1,0:T(8,128)(2,1)S(1)}, bf16[256,512]{1,0:T(8,128)(2,1)S(1)}, u32[]{:S(2)}, u32[]{:S(2)}) %collective-permute-start.26) | collective-permute-done | bytes 262176 | tf_op jit(solution)/shard_map/ppermute | solution.py:538
  177.5 4.1 %collective-permute-done.30.refs_3_ = bf16[256,512]{1,0:T(8,128)(2,1)S(1)} collective-permute-done((bf16[256,512]{1,0:T(8,128)(2,1)S(1)}, bf16[256,512]{1,0:T(8,128)(2,1)S(1)}, u32[]{:S(2)}, u32[]{:S(2)}) %collective-permute-start.30) | collective-permute-done | bytes 262176 | tf_op jit(solution)/shard_map/ppermute | solution.py:538
  (99 shorter events, 51.1 us)
Async XLA Ops:
  0.0 12.3 %collective-permute-start = (bf16[256,512]{1,0:T(8,128)(2,1)}, bf16[256,512]{1,0:T(8,128)(2,1)S(1)}, u32[]{:S(2)}, u32[]{:S(2)}) collective-permute-start(bf16[256,512]{1,0:T(8,128)(2,1)} %refs_0_.3), channel_id=1, source_target_pairs={{0,1},{1,0},{2,3},{3,2},{4,5},{5,4},{6,7},{7,6},{8,9},{9,8},{10,11... | collective-permute-start | bytes 786440 | tf_op jit(solution)/shard_map/ppermute | solution.py:538
  3.0 11.3 %collective-permute-start.4 = (bf16[256,512]{1,0:T(8,128)(2,1)}, bf16[256,512]{1,0:T(8,128)(2,1)S(1)}, u32[]{:S(2)}, u32[]{:S(2)}) collective-permute-start(bf16[256,512]{1,0:T(8,128)(2,1)} %refs_0_.3), channel_id=1, source_target_pairs={{0,2},{1,3},{2,4},{3,5},{4,6},{5,7},{6,0},{7,1},{8,10},{9,11},{10,... | collective-permute-start | bytes 786440 | tf_op jit(solution)/shard_map/ppermute | solution.py:538
  4.5 14.8 %collective-permute-start.7 = (bf16[256,512]{1,0:T(8,128)(2,1)}, bf16[256,512]{1,0:T(8,128)(2,1)S(1)}, u32[]{:S(2)}, u32[]{:S(2)}) collective-permute-start(bf16[256,512]{1,0:T(8,128)(2,1)} %refs_0_.3), channel_id=1, source_target_pairs={{0,6},{1,7},{2,0},{3,1},{4,2},{5,3},{6,4},{7,5},{8,14},{9,15},{10,... | collective-permute-start | bytes 786440 | tf_op jit(solution)/shard_map/ppermute | solution.py:538
  13.2 7.9 %collective-permute-start.1 = (bf16[256,288]{1,0:T(8,128)(2,1)S(1)}, bf16[256,288]{1,0:T(8,128)(2,1)S(1)}, u32[]{:S(2)}, u32[]{:S(2)}) collective-permute-start(bf16[256,288]{1,0:T(8,128)(2,1)S(1)} %project_low.2), channel_id=1, source_target_pairs={{0,1},{1,0},{2,3},{3,2},{4,5},{5,4},{6,7},{7,6},{8,9},{9,8},{10,11... | collective-permute-start | bytes 442376 | tf_op jit(solution)/shard_map/ppermute | solution.py:538
  14.2 11.3 %collective-permute-start.5 = (bf16[256,512]{1,0:T(8,128)(2,1)S(1)}, bf16[256,512]{1,0:T(8,128)(2,1)S(1)}, u32[]{:S(2)}, u32[]{:S(2)}) collective-permute-start(bf16[256,512]{1,0:T(8,128)(2,1)S(1)} %collective-permute-done.4.refs_0_), channel_id=1, source_target_pairs={{0,2},{1,3},{2,4},{3,5},{4,6},{5,7},{6,0},{7,1},{8,10},{9,11},{10,... | collective-permute-start | bytes 786440 | tf_op jit(solution)/shard_map/ppermute | solution.py:538
  14.2 12.5 %collective-permute-start.9 = (bf16[256,512]{1,0:T(8,128)(2,1)S(1)}, bf16[256,512]{1,0:T(8,128)(2,1)S(1)}, u32[]{:S(2)}, u32[]{:S(2)}) collective-permute-start(bf16[256,512]{1,0:T(8,128)(2,1)S(1)} %collective-permute-done.4.refs_0_), channel_id=1, source_target_pairs={{0,1},{1,0},{2,3},{3,2},{4,5},{5,4},{6,7},{7,6},{8,9},{9,8},{10,11... | collective-permute-start | bytes 786440 | tf_op jit(solution)/shard_map/ppermute | solution.py:538
  19.3 13.3 %collective-permute-start.8 = (bf16[256,512]{1,0:T(8,128)(2,1)S(1)}, bf16[256,512]{1,0:T(8,128)(2,1)S(1)}, u32[]{:S(2)}, u32[]{:S(2)}) collective-permute-start(bf16[256,512]{1,0:T(8,128)(2,1)S(1)} %collective-permute-done.7.refs_0_), channel_id=1, source_target_pairs={{0,1},{1,0},{2,3},{3,2},{4,5},{5,4},{6,7},{7,6},{8,9},{9,8},{10,11... | collective-permute-start | bytes 786440 | tf_op jit(solution)/shard_map/ppermute | solution.py:538
  21.2 9.3 %collective-permute-start.2 = (bf16[256,288]{1,0:T(8,128)(2,1)S(1)}, bf16[256,288]{1,0:T(8,128)(2,1)S(1)}, u32[]{:S(2)}, u32[]{:S(2)}) collective-permute-start(bf16[256,288]{1,0:T(8,128)(2,1)S(1)} %add_convert_fusion.3.refs_7_), channel_id=1, source_target_pairs={{0,2},{1,3},{2,0},{3,1},{4,6},{5,7},{6,4},{7,5},{8,10},{9,11},{10,... | collective-permute-start | bytes 442376 | tf_op jit(solution)/shard_map/ppermute | solution.py:542
  25.6 10.9 %collective-permute-start.6 = (bf16[256,512]{1,0:T(8,128)(2,1)S(1)}, bf16[256,512]{1,0:T(8,128)(2,1)S(1)}, u32[]{:S(2)}, u32[]{:S(2)}) collective-permute-start(bf16[256,512]{1,0:T(8,128)(2,1)S(1)} %relay.2), channel_id=1, source_target_pairs={{0,1},{1,0},{2,3},{3,2},{4,5},{5,4},{6,7},{7,6},{8,9},{9,8},{10,11... | collective-permute-start | bytes 786440 | tf_op jit(solution)/shard_map/ppermute | solution.py:538
  30.6 9.7 %collective-permute-start.3 = (bf16[256,288]{1,0:T(8,128)(2,1)S(1)}, bf16[256,288]{1,0:T(8,128)(2,1)S(1)}, u32[]{:S(2)}, u32[]{:S(2)}) collective-permute-start(bf16[256,288]{1,0:T(8,128)(2,1)S(1)} %add_convert_fusion.2.refs_7_.own_ref), channel_id=1, source_target_pairs={{0,4},{1,5},{2,6},{3,7},{4,0},{5,1},{6,2},{7,3},{8,12},{9,13},{10,... | collective-permute-start | bytes 442376 | tf_op jit(solution)/shard_map/ppermute | solution.py:542
  61.9 9.2 %collective-permute-start.12 = (bf16[256,512]{1,0:T(8,128)(2,1)S(1)}, bf16[256,512]{1,0:T(8,128)(2,1)S(1)}, u32[]{:S(2)}, u32[]{:S(2)}) collective-permute-start(bf16[256,512]{1,0:T(8,128)(2,1)S(1)} %get-tuple-element.89), channel_id=1, source_target_pairs={{0,1},{1,0},{2,3},{3,2},{4,5},{5,4},{6,7},{7,6},{8,9},{9,8},{10,11... | collective-permute-start | bytes 786440 | tf_op jit(solution)/shard_map/ppermute | solution.py:538
  66.0 12.6 %collective-permute-start.15 = (bf16[256,512]{1,0:T(8,128)(2,1)S(1)}, bf16[256,512]{1,0:T(8,128)(2,1)S(1)}, u32[]{:S(2)}, u32[]{:S(2)}) collective-permute-start(bf16[256,512]{1,0:T(8,128)(2,1)S(1)} %get-tuple-element.92), channel_id=1, source_target_pairs={{0,1},{1,0},{2,3},{3,2},{4,5},{5,4},{6,7},{7,6},{8,9},{9,8},{10,11... | collective-permute-start | bytes 786440 | tf_op jit(solution)/shard_map/ppermute | solution.py:538
  67.6 14.7 %collective-permute-start.11 = (bf16[256,512]{1,0:T(8,128)(2,1)S(1)}, bf16[256,512]{1,0:T(8,128)(2,1)S(1)}, u32[]{:S(2)}, u32[]{:S(2)}) collective-permute-start(bf16[256,512]{1,0:T(8,128)(2,1)S(1)} %get-tuple-element.87), channel_id=1, source_target_pairs={{0,1},{1,0},{2,3},{3,2},{4,5},{5,4},{6,7},{7,6},{8,9},{9,8},{10,11... | collective-permute-start | bytes 786440 | tf_op jit(solution)/shard_map/ppermute | solution.py:538
  71.2 11.2 %collective-permute-start.13 = (bf16[256,512]{1,0:T(8,128)(2,1)S(1)}, bf16[256,512]{1,0:T(8,128)(2,1)S(1)}, u32[]{:S(2)}, u32[]{:S(2)}) collective-permute-start(bf16[256,512]{1,0:T(8,128)(2,1)S(1)} %combine.8.refs_0_), channel_id=1, source_target_pairs={{0,2},{1,3},{2,4},{3,5},{4,6},{5,7},{6,0},{7,1},{8,10},{9,11},{10,... | collective-permute-start | bytes 786440 | tf_op jit(solution)/shard_map/ppermute | solution.py:538
  74.7 14.3 %collective-permute-start.10 = (bf16[256,512]{1,0:T(8,128)(2,1)S(1)}, bf16[256,512]{1,0:T(8,128)(2,1)S(1)}, u32[]{:S(2)}, u32[]{:S(2)}) collective-permute-start(bf16[256,512]{1,0:T(8,128)(2,1)S(1)} %get-tuple-element.85), channel_id=1, source_target_pairs={{0,1},{1,0},{2,3},{3,2},{4,5},{5,4},{6,7},{7,6},{8,9},{9,8},{10,11... | collective-permute-start | bytes 786440 | tf_op jit(solution)/shard_map/ppermute | solution.py:538
  78.6 10.4 %collective-permute-start.16 = (bf16[256,512]{1,0:T(8,128)(2,1)S(1)}, bf16[256,512]{1,0:T(8,128)(2,1)S(1)}, u32[]{:S(2)}, u32[]{:S(2)}) collective-permute-start(bf16[256,512]{1,0:T(8,128)(2,1)S(1)} %combine.10.refs_0_), channel_id=1, source_target_pairs={{0,6},{1,7},{2,0},{3,1},{4,2},{5,3},{6,4},{7,5},{8,14},{9,15},{10,... | collective-permute-start | bytes 786440 | tf_op jit(solution)/shard_map/ppermute | solution.py:538
  82.4 9.9 %collective-permute-start.14 = (bf16[256,512]{1,0:T(8,128)(2,1)S(1)}, bf16[256,512]{1,0:T(8,128)(2,1)S(1)}, u32[]{:S(2)}, u32[]{:S(2)}) collective-permute-start(bf16[256,512]{1,0:T(8,128)(2,1)S(1)} %combine.9), channel_id=1, source_target_pairs={{0,2},{1,3},{2,4},{3,5},{4,6},{5,7},{6,0},{7,1},{8,10},{9,11},{10,... | collective-permute-start | bytes 786440 | tf_op jit(solution)/shard_map/ppermute | solution.py:538
  93.4 18.3 %collective-permute-start.17 = (bf16[256,800]{1,0:T(8,128)(2,1)S(1)}, bf16[256,800]{1,0:T(8,128)(2,1)S(1)}, u32[]{:S(2)}, u32[]{:S(2)}) collective-permute-start(bf16[256,800]{1,0:T(8,128)(2,1)S(1)} %project_low.3), channel_id=1, source_target_pairs={{0,1},{1,0},{2,3},{3,2},{4,5},{5,4},{6,7},{7,6},{8,9},{9,8},{10,11... | collective-permute-start | bytes 1228808 | tf_op jit(solution)/shard_map/ppermute | solution.py:538
  95.1 11.1 %collective-permute-start.20 = (bf16[256,512]{1,0:T(8,128)(2,1)S(1)}, bf16[256,512]{1,0:T(8,128)(2,1)S(1)}, u32[]{:S(2)}, u32[]{:S(2)}) collective-permute-start(bf16[256,512]{1,0:T(8,128)(2,1)S(1)} %combine.11.rows_ref.refs_0_), channel_id=1, source_target_pairs={{0,2},{1,3},{2,4},{3,5},{4,6},{5,7},{6,0},{7,1},{8,10},{9,11},{10,... | collective-permute-start | bytes 786440 | tf_op jit(solution)/shard_map/ppermute | solution.py:538
  96.8 14.8 %collective-permute-start.23 = (bf16[256,512]{1,0:T(8,128)(2,1)S(1)}, bf16[256,512]{1,0:T(8,128)(2,1)S(1)}, u32[]{:S(2)}, u32[]{:S(2)}) collective-permute-start(bf16[256,512]{1,0:T(8,128)(2,1)S(1)} %combine.11.rows_ref.refs_0_), channel_id=1, source_target_pairs={{0,6},{1,7},{2,0},{3,1},{4,2},{5,3},{6,4},{7,5},{8,14},{9,15},{10,... | collective-permute-start | bytes 786440 | tf_op jit(solution)/shard_map/ppermute | solution.py:538
  106.1 14.1 %collective-permute-start.21 = (bf16[256,512]{1,0:T(8,128)(2,1)S(1)}, bf16[256,512]{1,0:T(8,128)(2,1)S(1)}, u32[]{:S(2)}, u32[]{:S(2)}) collective-permute-start(bf16[256,512]{1,0:T(8,128)(2,1)S(1)} %collective-permute-done.20.refs_0_), channel_id=1, source_target_pairs={{0,2},{1,3},{2,4},{3,5},{4,6},{5,7},{6,0},{7,1},{8,10},{9,11},{10,... | collective-permute-start | bytes 786440 | tf_op jit(solution)/shard_map/ppermute | solution.py:538
  108.1 13.6 %collective-permute-start.25 = (bf16[256,512]{1,0:T(8,128)(2,1)S(1)}, bf16[256,512]{1,0:T(8,128)(2,1)S(1)}, u32[]{:S(2)}, u32[]{:S(2)}) collective-permute-start(bf16[256,512]{1,0:T(8,128)(2,1)S(1)} %collective-permute-done.20.refs_0_), channel_id=1, source_target_pairs={{0,1},{1,0},{2,3},{3,2},{4,5},{5,4},{6,7},{7,6},{8,9},{9,8},{10,11... | collective-permute-start | bytes 786440 | tf_op jit(solution)/shard_map/ppermute | solution.py:538
  111.7 11.8 %collective-permute-start.24 = (bf16[256,512]{1,0:T(8,128)(2,1)S(1)}, bf16[256,512]{1,0:T(8,128)(2,1)S(1)}, u32[]{:S(2)}, u32[]{:S(2)}) collective-permute-start(bf16[256,512]{1,0:T(8,128)(2,1)S(1)} %collective-permute-done.23.refs_0_), channel_id=1, source_target_pairs={{0,1},{1,0},{2,3},{3,2},{4,5},{5,4},{6,7},{7,6},{8,9},{9,8},{10,11... | collective-permute-start | bytes 786440 | tf_op jit(solution)/shard_map/ppermute | solution.py:538
  111.7 8.3 %collective-permute-start.18 = (bf16[256,288]{1,0:T(8,128)(2,1)S(1)}, bf16[256,288]{1,0:T(8,128)(2,1)S(1)}, u32[]{:S(2)}, u32[]{:S(2)}) collective-permute-start(bf16[256,288]{1,0:T(8,128)(2,1)S(1)} %add_convert_fusion.1.refs_7_), channel_id=1, source_target_pairs={{0,2},{1,3},{2,0},{3,1},{4,6},{5,7},{6,4},{7,5},{8,10},{9,11},{10,... | collective-permute-start | bytes 442376 | tf_op jit(solution)/shard_map/ppermute | solution.py:542
  120.1 10.5 %collective-permute-start.19 = (bf16[256,288]{1,0:T(8,128)(2,1)S(1)}, bf16[256,288]{1,0:T(8,128)(2,1)S(1)}, u32[]{:S(2)}, u32[]{:S(2)}) collective-permute-start(bf16[256,288]{1,0:T(8,128)(2,1)S(1)} %add_convert_fusion.refs_1_.refs_7_.own_ref), channel_id=1, source_target_pairs={{0,4},{1,5},{2,6},{3,7},{4,0},{5,1},{6,2},{7,3},{8,12},{9,13},{10,... | collective-permute-start | bytes 442376 | tf_op jit(solution)/shard_map/ppermute | solution.py:542
  152.0 9.2 %collective-permute-start.28 = (bf16[256,512]{1,0:T(8,128)(2,1)S(1)}, bf16[256,512]{1,0:T(8,128)(2,1)S(1)}, u32[]{:S(2)}, u32[]{:S(2)}) collective-permute-start(bf16[256,512]{1,0:T(8,128)(2,1)S(1)} %get-tuple-element.122), channel_id=1, source_target_pairs={{0,1},{1,0},{2,3},{3,2},{4,5},{5,4},{6,7},{7,6},{8,9},{9,8},{10,11... | collective-permute-start | bytes 786440 | tf_op jit(solution)/shard_map/ppermute | solution.py:538
  156.9 10.0 %collective-permute-start.31 = (bf16[256,512]{1,0:T(8,128)(2,1)S(1)}, bf16[256,512]{1,0:T(8,128)(2,1)S(1)}, u32[]{:S(2)}, u32[]{:S(2)}) collective-permute-start(bf16[256,512]{1,0:T(8,128)(2,1)S(1)} %get-tuple-element.124), channel_id=1, source_target_pairs={{0,1},{1,0},{2,3},{3,2},{4,5},{5,4},{6,7},{7,6},{8,9},{9,8},{10,11... | collective-permute-start | bytes 786440 | tf_op jit(solution)/shard_map/ppermute | solution.py:538
  157.8 14.7 %collective-permute-start.27 = (bf16[256,512]{1,0:T(8,128)(2,1)S(1)}, bf16[256,512]{1,0:T(8,128)(2,1)S(1)}, u32[]{:S(2)}, u32[]{:S(2)}) collective-permute-start(bf16[256,512]{1,0:T(8,128)(2,1)S(1)} %get-tuple-element.120), channel_id=1, source_target_pairs={{0,1},{1,0},{2,3},{3,2},{4,5},{5,4},{6,7},{7,6},{8,9},{9,8},{10,11... | collective-permute-start | bytes 786440 | tf_op jit(solution)/shard_map/ppermute | solution.py:538
  161.3 11.2 %collective-permute-start.29 = (bf16[256,512]{1,0:T(8,128)(2,1)S(1)}, bf16[256,512]{1,0:T(8,128)(2,1)S(1)}, u32[]{:S(2)}, u32[]{:S(2)}) collective-permute-start(bf16[256,512]{1,0:T(8,128)(2,1)S(1)} %combine.12), channel_id=1, source_target_pairs={{0,2},{1,3},{2,4},{3,5},{4,6},{5,7},{6,0},{7,1},{8,10},{9,11},{10,... | collective-permute-start | bytes 786440 | tf_op jit(solution)/shard_map/ppermute | solution.py:538
  164.5 13.0 %collective-permute-start.26 = (bf16[256,512]{1,0:T(8,128)(2,1)S(1)}, bf16[256,512]{1,0:T(8,128)(2,1)S(1)}, u32[]{:S(2)}, u32[]{:S(2)}) collective-permute-start(bf16[256,512]{1,0:T(8,128)(2,1)S(1)} %get-tuple-element.118), channel_id=1, source_target_pairs={{0,1},{1,0},{2,3},{3,2},{4,5},{5,4},{6,7},{7,6},{8,9},{9,8},{10,11... | collective-permute-start | bytes 786440 | tf_op jit(solution)/shard_map/ppermute | solution.py:538
  166.9 10.6 %collective-permute-start.32 = (bf16[256,512]{1,0:T(8,128)(2,1)S(1)}, bf16[256,512]{1,0:T(8,128)(2,1)S(1)}, u32[]{:S(2)}, u32[]{:S(2)}) collective-permute-start(bf16[256,512]{1,0:T(8,128)(2,1)S(1)} %combine.14), channel_id=1, source_target_pairs={{0,6},{1,7},{2,0},{3,1},{4,2},{5,3},{6,4},{7,5},{8,14},{9,15},{10,... | collective-permute-start | bytes 786440 | tf_op jit(solution)/shard_map/ppermute | solution.py:538
  172.6 9.0 %collective-permute-start.30 = (bf16[256,512]{1,0:T(8,128)(2,1)S(1)}, bf16[256,512]{1,0:T(8,128)(2,1)S(1)}, u32[]{:S(2)}, u32[]{:S(2)}) collective-permute-start(bf16[256,512]{1,0:T(8,128)(2,1)S(1)} %combine.13), channel_id=1, source_target_pairs={{0,2},{1,3},{2,4},{3,5},{4,6},{5,7},{6,0},{7,1},{8,10},{9,11},{10,... | collective-permute-start | bytes 786440 | tf_op jit(solution)/shard_map/ppermute | solution.py:538
  (11 other events, 77.2 us)
